TPU v7x, 32 devices: a whole 2x2x4 slice. The times are simulated.
32 devices in a mesh: bond: 8 (over y, x, core), leg: 4 (over z).
Axes of the slice: x: 2, y: 2, z: 4, core: 2. Of those that a mesh axis runs over, the one named last changes fastest.
Arguments:
- amplitudes: float32 [2, 1024, 262144], P(None, 'bond', 'leg'), may hold values from -6 to 6
- vectors: float32 [64, 262144], P(None, ('leg', 'bond')), may hold values from -0.01171875 to 0.01171875
- row_map: float32 [64, 4096], P('leg'), may hold values from -0.09375 to 0.09375
- col_map: float32 [64, 4096], P('bond'), may hold values from -0.09375 to 0.09375
Outputs:
- coarse: float32 [2, 8, 64, 64], P(None, None, 'leg', 'bond')
All inputs are finite; a program needn't handle non-finite values.
Results may differ from a plain program's by a relative error of at most 0.00014.
Values sent between devices are 32-bit elements; how exact they have to be, the bound alone decides.
No kernel may reach another device: no remote copies, remote signals or barrier semaphores. Data moves between devices by JAX's collectives and lax.ppermute only.
A program may use at most 128 MiB of HBM per device.

v0:
```python
import jax
import jax.numpy as jnp
from jax import lax
from jax.sharding import PartitionSpec as P


def coarsen(slab, row_maps, col_maps):
    highest = lax.Precision.HIGHEST
    even = slab[:, 0::2]
    odd = slab[:, 1::2]
    inner = jnp.einsum("ztjc,qcd->ztqjd", even, col_maps, precision=highest)
    real_part = jnp.einsum("tqjd,tkd->tqjk", inner[0], odd[0], precision=highest) - jnp.einsum(
        "tqjd,tkd->tqjk", inner[1], odd[1], precision=highest
    )
    imag_part = jnp.einsum("tqjd,tkd->tqjk", inner[0], odd[1], precision=highest) + jnp.einsum(
        "tqjd,tkd->tqjk", inner[1], odd[0], precision=highest
    )
    paired = jnp.stack([real_part, imag_part])
    return jnp.einsum("pjk,ztqjk->ztpq", row_maps, paired, precision=highest)


def local(amplitudes, vectors, row_map, col_map):
    highest = lax.Precision.HIGHEST
    bond_dim = vectors.shape[0]
    partial_proj = jnp.einsum(
        "jk,zrk->zjr",
        lax.all_gather(vectors, "bond", axis=1, tiled=True),
        amplitudes,
        precision=highest,
    )
    summed = lax.psum(partial_proj, "leg")
    projected = lax.all_gather(summed, "bond", axis=2, tiled=True)
    slab_count = projected.shape[2] // bond_dim
    slab = projected.reshape(2, bond_dim, slab_count, bond_dim).transpose(0, 2, 1, 3)
    row_maps = row_map.reshape(row_map.shape[0], bond_dim, bond_dim)
    col_maps = col_map.reshape(col_map.shape[0], bond_dim, bond_dim)
    return coarsen(slab, row_maps, col_maps)


def solution(mesh):
    return jax.shard_map(
        local,
        mesh=mesh,
        in_specs=(
            P(None, "bond", "leg"),
            P(None, ("leg", "bond")),
            P("leg", None),
            P("bond", None),
        ),
        out_specs=P(None, None, "leg", "bond"),
        check_vma=False,
    )
```

profile of v0, /device:TPU:0, one launch (start us, length us, event | category | flops | bytes accessed | tf_op | source)
XLA Modules:
  0.0 241.1 jit_solution(13143545119933517569)
XLA Ops:
  6.5 0.0 all-gather.2.cloned.1.call-start
  6.5 0.7 all-gather.2.cloned.1.call-update
  7.3 0.0 copy-start.1
  7.3 0.0 copy-start
  7.3 0.0 all-reduce.2.cloned.1.call-start
  7.3 94.5 %all-gather.2.cloned.1.call-done = f32[64,65536]{1,0:T(8,128)} async-done(((f32[64,8192]{1,0:T(8,128)}), f32[64,65536]{1,0:T(8,128)}) %all-gather.2.cloned.1.call-update) | async-done | bytes 16777232 | tf_op jit(solution)/shard_map/all_gather | solution.py:27
  101.9 67.1 %fusion.11 = f32[2,64,128]{2,1,0:T(8,128)} fusion(f32[2,128,65536]{2,1,0:T(8,128)} %param.4, f32[64,65536]{1,0:T(8,128)} %all-gather.2.cloned.1.call-done), kind=kOutput, calls=%fused_computation.15 | convolution fusion | flops 12884901888 | bytes 83951616 | tf_op jit(solution)/shard_map/jk,zrk->zjr/dot_general | solution.py:25
  168.9 0.0 all-reduce.2.cloned.1.call-update
  169.0 0.0 copy-done.1
  169.0 0.1 reshape.14
  169.1 0.0 copy-done
  169.1 0.2 reshape.11
  169.3 33.8 %all-reduce.2.cloned.1.call-done = f32[2,64,128]{2,1,0:T(8,128)} async-done(((f32[2,64,128]{2,1,0:T(8,128)}), f32[2,64,128]{2,1,0:T(8,128)}) %all-reduce.2.cloned.1.call-update) | async-done | bytes 65552 | tf_op jit(solution)/shard_map/psum | solution.py:31
  203.1 11.3 %all_gather.7 = f32[2,64,1024]{2,1,0:T(8,128)S(1)} all-gather(f32[2,64,128]{2,1,0:T(8,128)} %all-reduce.2.cloned.1.call-done), channel_id=1, replica_groups=mesh['bond'=8,'leg'=4] {'bond'}, dimensions={2}, use_global_device_ids=true | all-gather | bytes 589824 | tf_op jit(solution)/shard_map/all_gather | solution.py:32
  214.4 0.3 reshape.9
  214.7 0.3 copy.23
  215.1 3.5 %convolution_bitcast_fusion = f32[2,8,8,64,64]{4,3,2,1,0:T(8,128)S(1)} fusion(f32[2,16,64,64]{3,2,1,0:T(8,128)S(1)} %bitcast.58, f32[8,64,64,1,1]{2,1,0,3,4:T(8,128)S(1)} %reshape.14), kind=kOutput, calls=%fused_computation.5 | convolution fusion | flops 402653184 | bytes 2883584 | tf_op jit(solution)/shard_map/ztjc,qcd->ztqjd/dot_general | solution.py:11
  218.6 2.0 fusion.4
  220.5 2.0 fusion.5
  222.5 2.0 add_bitcast_fusion
  224.6 2.3 subtract_bitcast_fusion
  226.9 0.8 pad_maximum_fusion
  227.7 6.5 %fusion.8 = f32[2,8,16,8]{2,3,1,0:T(8,128)} fusion(f32[2,8,8,64,64]{4,3,2,1,0:T(8,128)S(1)} %pad_maximum_fusion, f32[16,64,64,1,1]{2,1,0,4,3:T(8,128)S(1)} %bitcast.59), kind=kOutput, calls=%fused_computation.14 | convolution fusion | flops 100663296 | bytes 2367488 | tf_op jit(solution)/shard_map/pjk,ztqjk->ztpq/dot_general | solution.py:19
  (1 shorter events, 0.0 us)
Async XLA Ops:
  6.5 95.3 %all-gather.2.cloned.1.call-start = ((), (), s32[]{:S(2)}) async-start(), calls=%async_computation | async-start | bytes 18874368 | tf_op jit(solution)/shard_map/all_gather | solution.py:27
  7.3 161.7 %copy-start.1 = (f32[8,4096]{1,0:T(8,128)S(1)}, f32[8,4096]{1,0:T(8,128)}, u32[]{:S(2)}) copy-start(f32[8,4096]{1,0:T(8,128)} %param.7) | copy-start | bytes 393220
  7.3 161.8 %copy-start = (f32[16,4096]{1,0:T(8,128)S(1)}, f32[16,4096]{1,0:T(8,128)}, u32[]{:S(2)}) copy-start(f32[16,4096]{1,0:T(8,128)} %param.6) | copy-start | bytes 786436
  7.3 195.8 %all-reduce.2.cloned.1.call-start = ((), (), s32[]{:S(2)}) async-start(), calls=%async_computation.1 | async-start | bytes 131072 | tf_op jit(solution)/shard_map/psum | solution.py:31
Sparse Core Ops, SparseCore 0:
  9.3 92.5 all-gather.1
  169.1 33.9 all-reduce.1
where the time goes:
time: 241 us
  waiting for transfers between devices  129 us (54%)
  matrix products  85.4 us (35%)
  between operations  13.5 us (6%)
  blocking collectives  11.3 us (5%)
    all_gather x1, waiting for transfers between devices, local(): lax.all_gather(vectors, 'bond', axis=1, tiled=True)  94.5 us
    dot_general x1, matrix products, local(): jnp.einsum('jk,zrk->zjr', lax.all_gather(vectors, 'bond', axis=1, tiled=T...  67.1 us
    psum x1, waiting for transfers between devices, local(): summed = lax.psum(partial_proj, 'leg')  33.8 us
    all_gather x1, blocking collectives, local(): projected = lax.all_gather(summed, 'bond', axis=2, tiled=True)  11.3 us
    dot_general x1, matrix products, coarsen(): return jnp.einsum('pjk,ztqjk->ztpq', row_maps, paired, precision=highest)  6.53 us
  transfers between devices with their start and end apart: 2, of which 2 were waited for; matrix products, arithmetic and copies ran while one was open for 0% of the time, Pallas kernels for 0%

commit v1 on v0

--- a/solution.py
+++ b/solution.py
@@ -1,7 +1,81 @@
+import functools
+
 import jax
 import jax.numpy as jnp
+import numpy as np
 from jax import lax
+from jax.experimental import pallas as pl
+from jax.experimental.pallas import tpu as pltpu
 from jax.sharding import PartitionSpec as P
+
+LANES = 128
+
+
+def split_bf16(x):
+    hi = x.astype(jnp.bfloat16)
+    return hi, (x - hi.astype(jnp.float32)).astype(jnp.bfloat16)
+
+
+def project_kernel(spans, table, amp, *refs):
+    count = len(spans)
+    blocks, start, out, both = refs[:count], refs[count], refs[count + 1], refs[count + 2]
+    step = pl.program_id(0)
+    bond_dim = both.shape[0] // 2
+    for index, (first, last) in enumerate(spans):
+
+        @pl.when((step >= first) & (step < last))
+        def _():
+            hi, lo = split_bf16(blocks[index][...])
+            both[:bond_dim, :] = hi
+            both[bond_dim:, :] = lo
+
+    @pl.when(step == 0)
+    def _():
+        out[...] = start[...]
+
+    hi, lo = split_bf16(amp[...].reshape(-1, amp.shape[-1]))
+    dims = (((1,), (1,)), ((), ()))
+    out[...] += lax.dot_general(
+        hi, both[...], dims, preferred_element_type=jnp.float32
+    ) + lax.dot_general(lo, both[...], dims, preferred_element_type=jnp.float32)
+
+
+def project(row, table, amplitudes, blocks, unit, start):
+    parts, rows, _ = amplitudes.shape
+    bond_dim = blocks[0].shape[0]
+    spans = []
+    for block in blocks:
+        first = spans[-1][1] if spans else 0
+        spans.append((first, first + block.shape[1] // unit))
+    steps = spans[-1][1]
+    whole = lambda i, t: (0, 0)
+
+    def columns(first, last):
+        return lambda i, t: (0, jnp.clip(i - first, 0, last - first - 1))
+
+    grid_spec = pltpu.PrefetchScalarGridSpec(
+        num_scalar_prefetch=1,
+        grid=(steps,),
+        in_specs=[pl.BlockSpec((parts, rows, unit), lambda i, t: (0, 0, t[row, i]))]
+        + [pl.BlockSpec((bond_dim, unit), columns(*span)) for span in spans]
+        + [pl.BlockSpec(start.shape, whole)],
+        out_specs=pl.BlockSpec(start.shape, whole),
+        scratch_shapes=[pltpu.VMEM((2 * bond_dim, unit), jnp.bfloat16)],
+    )
+    return pl.pallas_call(
+        functools.partial(project_kernel, spans),
+        grid_spec=grid_spec,
+        out_shape=jax.ShapeDtypeStruct(start.shape, jnp.float32),
+        input_output_aliases={len(blocks) + 2: 0},
+        compiler_params=pltpu.CompilerParams(
+            dimension_semantics=("arbitrary",), vmem_limit_bytes=20 * 2**20
+        ),
+        cost_estimate=pl.CostEstimate(
+            flops=8 * steps * bond_dim * parts * rows * unit,
+            bytes_accessed=4 * steps * unit * (parts * rows + bond_dim),
+            transcendentals=0,
+        ),
+    )(table, amplitudes, *blocks, start)
 
 
 def coarsen(slab, row_maps, col_maps):
@@ -19,17 +93,81 @@
     return jnp.einsum("pjk,ztqjk->ztpq", row_maps, paired, precision=highest)
 
 
-def local(amplitudes, vectors, row_map, col_map):
-    highest = lax.Precision.HIGHEST
+def swap(x, axis, size, mask):
+    return lax.ppermute(x, axis, [(i, i ^ mask) for i in range(size)])
+
+
+def after(x, *others):
+    return lax.optimization_barrier((x, *others))[0]
+
+
+def make_rounds(dims, parts, halves):
+    fresh = [[(0, p * halves + h) for h in range(halves)] for p in range(parts)]
+    older = [[] for _ in range(parts)]
+    rounds = []
+    for step in range(dims):
+        masks = [2 << ((p + step) % dims) for p in range(parts)]
+        older = [fresh[p] + older[p] for p in range(parts)]
+        fresh = [[(o ^ masks[p], i) for o, i in older[p]] for p in range(parts)]
+        for turn in range(len(older[0])):
+            rounds.append([(masks[p], older[p][turn], fresh[p][turn]) for p in range(parts)])
+    return rounds
+
+
+def gather_and_project(amplitudes, vectors, size):
+    bond_dim, width = vectors.shape
+    dims = (size // 2).bit_length() - 1
+    parts = dims if dims and width % (dims * LANES) == 0 else 1
+    halves = 2 if width % (2 * parts * LANES) == 0 else 1
+    unit = width // (parts * halves)
+    per_device = parts * halves
+    rounds = make_rounds(dims, parts, halves)
+
+    groups = [[(mask, i) for i in range(per_device)] for mask in (0, 1)]
+    for turn in rounds:
+        got = [block for _, _, block in turn]
+        groups.append(got + [(origin ^ 1, i) for origin, i in got])
+    longest = max(len(g) for g in groups)
+    groups = [g + [(0, 0)] * (longest - len(g)) for g in groups]
+    where = np.array(groups, np.int32)
+    table = (lax.axis_index("bond") ^ where[:, :, 0]) * per_device + where[:, :, 1]
+
+    held = {(0, i): vectors[:, i * unit : (i + 1) * unit] for i in range(per_device)}
+    total = jnp.zeros((amplitudes.shape[0] * amplitudes.shape[1], 2 * bond_dim), jnp.float32)
+    other = swap(vectors, "bond", size, 1)
+    add = lambda row, blocks, total: project(row, table, amplitudes, blocks, unit, total)
+    arrived = []
+    pending = [lambda total: add(0, [vectors], total), lambda total: add(1, [other], total)]
+    for number, turn in enumerate(rounds):
+        got = []
+        for mask, sent, block in turn:
+            array = held[sent]
+            if number >= 2:
+                array = after(array, total, *arrived[number - 2])
+            held[block] = swap(array, "bond", size, mask)
+            got.append(held[block])
+        arrived.append(got)
+        if number >= 1:
+            if number >= 2:
+                total = after(total, *arrived[number - 2])
+            total = pending[number - 1](total)
+        twin = [swap(array, "bond", size, 1) for array in got]
+        pending.append(functools.partial(add, number + 2, got + twin))
+    for step in pending[max(len(rounds) - 1, 0) :]:
+        total = step(total)
+    return total
+
+
+def local(bond, leg, amplitudes, vectors, row_map, col_map):
     bond_dim = vectors.shape[0]
-    partial_proj = jnp.einsum(
-        "jk,zrk->zjr",
-        lax.all_gather(vectors, "bond", axis=1, tiled=True),
-        amplitudes,
-        precision=highest,
-    )
-    summed = lax.psum(partial_proj, "leg")
-    projected = lax.all_gather(summed, "bond", axis=2, tiled=True)
+    total = gather_and_project(amplitudes, vectors, bond)
+    total = total[:, :bond_dim] + total[:, bond_dim:]
+    mask = 1
+    while mask < leg:
+        total = total + swap(total, "leg", leg, mask)
+        mask *= 2
+    part = total.reshape(amplitudes.shape[0], amplitudes.shape[1], bond_dim).transpose(0, 2, 1)
+    projected = lax.all_gather(part, "bond", axis=2, tiled=True)
     slab_count = projected.shape[2] // bond_dim
     slab = projected.reshape(2, bond_dim, slab_count, bond_dim).transpose(0, 2, 1, 3)
     row_maps = row_map.reshape(row_map.shape[0], bond_dim, bond_dim)
@@ -39,7 +177,7 @@
 
 def solution(mesh):
     return jax.shard_map(
-        local,
+        functools.partial(local, mesh.shape["bond"], mesh.shape["leg"]),
         mesh=mesh,
         in_specs=(
             P(None, "bond", "leg"),

time: 241 us -> 152 us (0.63)
  waiting for transfers between devices: 129 us -> 41.6 us
  matrix products: 85.4 us -> 18.3 us
  Pallas kernels: 0 us -> 52.9 us
  starting transfers between devices: 0.04 us -> 23.2 us
  between operations: 13.5 us -> 0.34 us
  local copies, waits for them, and re-layouts: 0.95 us -> 3.87 us
    all_gather x1 -> x0, waiting for transfers between devices: 94.5 us -> none  [local(): lax.all_gather(vectors, 'bond', axis=1, tiled=True)]
    dot_general x1 -> x0, matrix products: 67.1 us -> none  [local(): jnp.einsum('jk,zrk->zjr', lax.all_gather(vectors, 'bond', axis=1, tiled=T...]
    pallas_call x0 -> x8, Pallas kernels: none -> 52.9 us  [project(): pl.pallas_call(functools.partial(project_kernel, spans), grid_spec=grid_s...]
    ppermute x0 -> x27, waiting for transfers between devices: none -> 41.6 us  [swap(): return lax.ppermute(x, axis, [(i, i ^ mask) for i in range(size)])]
    psum x1 -> x0, waiting for transfers between devices: 33.8 us -> none  [local(): summed = lax.psum(partial_proj, 'leg')]
    ppermute x0 -> x27, starting transfers between devices: none -> 23.2 us  [swap(): return lax.ppermute(x, axis, [(i, i ^ mask) for i in range(size)])]
    slice x0 -> x1, local copies, waits for them, and re-layouts: none -> 2.81 us  [gather_and_project(): vectors[:, i * unit:(i + 1) * unit]]
  transfers between devices with their start and end apart: 2 -> 27, of which waited for: 2 -> 8; matrix products, arithmetic and copies ran while one was open for 0% -> 2% of each run, Pallas kernels for 0% -> 31%
where the time goes in v1:
time: 152 us; the launch traced here: 151 us
  Pallas kernels  52.9 us (35%)
  waiting for transfers between devices  41.6 us (27%)
  starting transfers between devices  23.2 us (15%)
  matrix products  18.3 us (12%)
  blocking collectives  10.1 us (7%)
  local copies, waits for them, and re-layouts  3.87 us (3%)
    pallas_call x8, Pallas kernels, project(): pl.pallas_call(functools.partial(project_kernel, spans), grid_spec=grid_s...  52.9 us
    ppermute x27, waiting for transfers between devices, swap(): return lax.ppermute(x, axis, [(i, i ^ mask) for i in range(size)])  41.6 us
    ppermute x27, starting transfers between devices, swap(): return lax.ppermute(x, axis, [(i, i ^ mask) for i in range(size)])  23.2 us
    all_gather x1, blocking collectives, local(): projected = lax.all_gather(part, 'bond', axis=2, tiled=True)  10.1 us
    dot_general x1, matrix products, coarsen(): return jnp.einsum('pjk,ztqjk->ztpq', row_maps, paired, precision=highest)  6.53 us
    dot_general x1, matrix products, coarsen(): inner = jnp.einsum('ztjc,qcd->ztqjd', even, col_maps, precision=highest)  3.49 us
  transfers between devices with their start and end apart: 27, of which 8 were waited for; matrix products, arithmetic and copies ran while one was open for 2% of the time, Pallas kernels for 31%

profile of v1, /device:TPU:0, one launch (start us, length us, event | category | flops | bytes accessed | tf_op | source)
XLA Modules:
  0.0 151.3 jit_solution(16197733180632717892)
XLA Ops:
  0.0 0.5 collective-permute-start.8
  0.5 2.8 %fusion.13 = (f32[64,2048]{1,0:T(8,128)}, f32[64,2048]{1,0:T(8,128)S(1)}, f32[64,2048]{1,0:T(8,128)}, f32[64,2048]{1,0:T(8,128)}) fusion(f32[64,8192]{1,0:T(8,128)} %refs_0_.1), kind=kLoop, calls=%fused_computation.22 | loop fusion | bytes 4194304 | tf_op jit(solution)/shard_map/slice | solution.py:135
  3.3 2.5 %collective-permute-start.4 = (f32[64,2048]{1,0:T(8,128)S(1)}, f32[64,2048]{1,0:T(8,128)}, u32[]{:S(2)}, u32[]{:S(2)}) collective-permute-start(f32[64,2048]{1,0:T(8,128)S(1)} %get-tuple-element.26), channel_id=1, source_target_pairs={{0,8},{4,12},{8,0},{12,4},{16,24},{20,28},{24,16},{28,20},{1,9},{5... | collective-permute-start | bytes 1572872 | tf_op jit(solution)/shard_map/ppermute | solution.py:97
  5.9 1.5 %collective-permute-start.5 = (f32[64,2048]{1,0:T(8,128)}, f32[64,2048]{1,0:T(8,128)}, u32[]{:S(2)}, u32[]{:S(2)}) collective-permute-start(f32[64,2048]{1,0:T(8,128)} %get-tuple-element.27), channel_id=1, source_target_pairs={{0,16},{4,20},{8,24},{12,28},{16,0},{20,4},{24,8},{28,12},{1,17},{... | collective-permute-start | bytes 1572872 | tf_op jit(solution)/shard_map/ppermute | solution.py:97
  7.4 0.5 collective-permute-start
  7.9 0.0 collective-permute-start.1
  7.9 10.8 %collective-permute-done.4.refs_0_ = f32[64,2048]{1,0:T(8,128)} collective-permute-done((f32[64,2048]{1,0:T(8,128)S(1)}, f32[64,2048]{1,0:T(8,128)}, u32[]{:S(2)}, u32[]{:S(2)}) %collective-permute-start.4) | collective-permute-done | bytes 524320 | tf_op jit(solution)/shard_map/ppermute | solution.py:97
  18.8 6.5 %shard_map.64.refs_1_ = f32[256,128]{1,0:T(8,128)S(1)} custom-call(s32[8,4]{1,0:T(8,128)S(1)} %multiply_add_fusion.table, f32[2,128,65536]{2,1,0:T(8,128)} %amp.15, f32[64,8192]{1,0:T(8,128)S(1)} %copy-done, f32[256,128]{1,0:T(8,128)S(1)} %broadcast_in_dim.3.refs_1_), custom_call_target="tpu_custom_call", output_to_operand_aliasing={{}: (3, {})} | custom-call | flops 1073741824 | bytes 10485760 | tf_op jit(solution)/shard_map/pallas_call | solution.py:65
  25.3 0.6 collective-permute-start.7
  25.9 3.6 %collective-permute-done.refs_0_ = f32[64,2048]{1,0:T(8,128)S(1)} collective-permute-done((f32[64,2048]{1,0:T(8,128)}, f32[64,2048]{1,0:T(8,128)S(1)}, u32[]{:S(2)}, u32[]{:S(2)}) %collective-permute-start) | collective-permute-done | bytes 524320 | tf_op jit(solution)/shard_map/ppermute | solution.py:97
  29.5 1.8 %collective-permute-start.9 = (f32[64,2048]{1,0:T(8,128)}, f32[64,2048]{1,0:T(8,128)S(1)}, u32[]{:S(2)}, u32[]{:S(2)}) collective-permute-start(f32[64,2048]{1,0:T(8,128)} %collective-permute-done.4.refs_0_), channel_id=1, source_target_pairs={{0,16},{4,20},{8,24},{12,28},{16,0},{20,4},{24,8},{28,12},{1,17},{... | collective-permute-start | bytes 1572872 | tf_op jit(solution)/shard_map/ppermute | solution.py:97
  31.3 0.0 collective-permute-done.1.refs_1_
  31.3 1.5 collective-permute-start.10
  32.8 0.0 collective-permute-done.6.refs_2_
  32.8 0.0 collective-permute-start.2
  32.8 0.0 collective-permute-done.8.refs_0_
  32.8 0.5 collective-permute-start.3
  33.3 6.7 %shard_map.65.refs_4_ = f32[256,128]{1,0:T(8,128)S(1)} custom-call(s32[8,4]{1,0:T(8,128)S(1)} %multiply_add_fusion.table, f32[2,128,65536]{2,1,0:T(8,128)} %amp.15, f32[64,8192]{1,0:T(8,128)} %collective-permute-done.8.refs_0_, f32[256,128]{1,0:T(8,128)S(1)} %shard_map.64.refs_1_), custom_call_target="tpu_custom_call", output_to_operand_aliasing={{}: (3, {})} | custom-call | flops 1073741824 | bytes 10485760 | tf_op jit(solution)/shard_map/pallas_call | solution.py:65
  40.1 0.6 collective-permute-start.11
  40.6 3.3 %collective-permute-done.9.refs_0_ = f32[64,2048]{1,0:T(8,128)S(1)} collective-permute-done((f32[64,2048]{1,0:T(8,128)}, f32[64,2048]{1,0:T(8,128)S(1)}, u32[]{:S(2)}, u32[]{:S(2)}) %collective-permute-start.9) | collective-permute-done | bytes 524320 | tf_op jit(solution)/shard_map/ppermute | solution.py:97
  44.0 2.3 %collective-permute-start.12 = (f32[64,2048]{1,0:T(8,128)S(1)}, f32[64,2048]{1,0:T(8,128)S(1)}, u32[]{:S(2)}, u32[]{:S(2)}) collective-permute-start(f32[64,2048]{1,0:T(8,128)S(1)} %collective-permute-done.1.refs_1_), channel_id=1, source_target_pairs={{0,8},{4,12},{8,0},{12,4},{16,24},{20,28},{24,16},{28,20},{1,9},{5... | collective-permute-start | bytes 1572872 | tf_op jit(solution)/shard_map/ppermute | solution.py:97
  46.3 0.0 collective-permute-done.10.refs_1_
  46.3 0.0 collective-permute-start.23
  46.3 0.5 collective-permute-start.24
  46.8 7.0 %shard_map.66.refs_4_ = f32[256,128]{1,0:T(8,128)S(1)} custom-call(s32[8,4]{1,0:T(8,128)S(1)} %multiply_add_fusion.table, f32[2,128,65536]{2,1,0:T(8,128)} %amp.15, f32[64,2048]{1,0:T(8,128)} %collective-permute-done.4.refs_0_, f32[64,2048]{1,0:T(8,128)} %collective-permute-done.5.refs_1_, ...), custom_call_target="tpu_custom_call", output_to_operand_aliasing={{}: (6, {})} | custom-call | flops 1073741824 | bytes 10485760 | tf_op jit(solution)/shard_map/pallas_call | solution.py:65
  53.9 1.6 %collective-permute-start.17 = (f32[64,2048]{1,0:T(8,128)S(1)}, f32[64,2048]{1,0:T(8,128)S(1)}, u32[]{:S(2)}, u32[]{:S(2)}) collective-permute-start(f32[64,2048]{1,0:T(8,128)S(1)} %copy-done.2), channel_id=1, source_target_pairs={{0,16},{4,20},{8,24},{12,28},{16,0},{20,4},{24,8},{28,12},{1,17},{... | collective-permute-start | bytes 1572872 | tf_op jit(solution)/shard_map/ppermute | solution.py:97
  55.5 0.0 collective-permute-done.11.refs_0_
  55.5 0.6 collective-permute-start.18
  56.1 0.0 collective-permute-done.12.refs_1_
  56.1 0.0 collective-permute-start.21
  56.1 6.5 %shard_map.67.refs_4_ = f32[256,128]{1,0:T(8,128)S(1)} custom-call(s32[8,4]{1,0:T(8,128)S(1)} %multiply_add_fusion.table, f32[2,128,65536]{2,1,0:T(8,128)} %amp.15, f32[64,2048]{1,0:T(8,128)S(1)} %collective-permute-done.refs_0_, f32[64,2048]{1,0:T(8,128)S(1)} %collective-permute-done.1.refs_1_, ...), custom_call_target="tpu_custom_call", output_to_operand_aliasing={{}: (6, {})} | custom-call | flops 1073741824 | bytes 10485760 | tf_op jit(solution)/shard_map/pallas_call | solution.py:65
  62.6 0.0 collective-permute-done.23.refs_2_
  62.6 1.5 collective-permute-start.14
  64.1 1.3 collective-permute-start.13
  65.5 3.0 %collective-permute-done.17.refs_0_ = f32[64,2048]{1,0:T(8,128)S(1)} collective-permute-done((f32[64,2048]{1,0:T(8,128)S(1)}, f32[64,2048]{1,0:T(8,128)S(1)}, u32[]{:S(2)}, u32[]{:S(2)}) %collective-permute-start.17) | collective-permute-done | bytes 524320 | tf_op jit(solution)/shard_map/ppermute | solution.py:97
  68.5 2.0 %collective-permute-done.18.refs_1_ = f32[64,2048]{1,0:T(8,128)S(1)} collective-permute-done((f32[64,2048]{1,0:T(8,128)}, f32[64,2048]{1,0:T(8,128)S(1)}, u32[]{:S(2)}, u32[]{:S(2)}) %collective-permute-start.18) | collective-permute-done | bytes 524320 | tf_op jit(solution)/shard_map/ppermute | solution.py:97
  70.5 0.5 collective-permute-start.20
  71.0 9.5 %collective-permute-done.14.refs_1_ = f32[64,2048]{1,0:T(8,128)S(1)} collective-permute-done((f32[64,2048]{1,0:T(8,128)}, f32[64,2048]{1,0:T(8,128)S(1)}, u32[]{:S(2)}, u32[]{:S(2)}) %collective-permute-start.14) | collective-permute-done | bytes 524320 | tf_op jit(solution)/shard_map/ppermute | solution.py:97
  80.6 0.5 collective-permute-start.15
  81.1 6.5 %shard_map.68.refs_4_ = f32[256,128]{1,0:T(8,128)S(1)} custom-call(s32[8,4]{1,0:T(8,128)S(1)} %multiply_add_fusion.table, f32[2,128,65536]{2,1,0:T(8,128)} %amp.15, f32[64,2048]{1,0:T(8,128)S(1)} %collective-permute-done.9.refs_0_, f32[64,2048]{1,0:T(8,128)S(1)} %collective-permute-done.10.refs_1_, ...), custom_call_target="tpu_custom_call", output_to_operand_aliasing={{}: (6, {})} | custom-call | flops 1073741824 | bytes 10485760 | tf_op jit(solution)/shard_map/pallas_call | solution.py:65
  87.6 6.5 %shard_map.69.refs_4_ = f32[256,128]{1,0:T(8,128)S(1)} custom-call(s32[8,4]{1,0:T(8,128)S(1)} %multiply_add_fusion.table, f32[2,128,65536]{2,1,0:T(8,128)} %amp.15, f32[64,2048]{1,0:T(8,128)S(1)} %collective-permute-done.11.refs_0_, f32[64,2048]{1,0:T(8,128)S(1)} %collective-permute-done.12.refs_1_, ...), custom_call_target="tpu_custom_call", output_to_operand_aliasing={{}: (6, {})} | custom-call | flops 1073741824 | bytes 10485760 | tf_op jit(solution)/shard_map/pallas_call | solution.py:65
  94.2 6.5 %shard_map.70.refs_4_ = f32[256,128]{1,0:T(8,128)S(1)} custom-call(s32[8,4]{1,0:T(8,128)S(1)} %multiply_add_fusion.table, f32[2,128,65536]{2,1,0:T(8,128)} %amp.15, f32[64,2048]{1,0:T(8,128)S(1)} %collective-permute-done.17.refs_0_, f32[64,2048]{1,0:T(8,128)S(1)} %collective-permute-done.18.refs_1_, ...), custom_call_target="tpu_custom_call", output_to_operand_aliasing={{}: (6, {})} | custom-call | flops 1073741824 | bytes 10485760 | tf_op jit(solution)/shard_map/pallas_call | solution.py:65
  100.7 0.0 copy-start.4
  100.7 0.0 copy-start.3
  100.8 6.5 %shard_map.71 = f32[256,128]{1,0:T(8,128)S(1)} custom-call(s32[8,4]{1,0:T(8,128)S(1)} %multiply_add_fusion.table, f32[2,128,65536]{2,1,0:T(8,128)} %amp.15, f32[64,2048]{1,0:T(8,128)S(1)} %collective-permute-done.13.refs_0_, f32[64,2048]{1,0:T(8,128)S(1)} %collective-permute-done.14.refs_1_, ...), custom_call_target="tpu_custom_call", output_to_operand_aliasing={{}: (6, {})} | custom-call | flops 1073741824 | bytes 10485760 | tf_op jit(solution)/shard_map/pallas_call | solution.py:65
  107.3 0.1 slice_add_fusion
  107.4 1.7 %collective-permute-start.25 = (f32[256,64]{1,0:T(8,128)S(1)}, f32[256,64]{1,0:T(8,128)S(1)}, u32[]{:S(2)}, u32[]{:S(2)}) collective-permute-start(f32[256,64]{1,0:T(8,128)S(1)} %slice_add_fusion), channel_id=1, source_target_pairs={{0,1},{1,0},{2,3},{3,2},{4,5},{5,4},{6,7},{7,6},{8,9},{9,8},{10,11... | collective-permute-start | bytes 196616 | tf_op jit(solution)/shard_map/ppermute | solution.py:97
  109.0 3.8 %collective-permute-done.25 = f32[256,64]{1,0:T(8,128)S(1)} collective-permute-done((f32[256,64]{1,0:T(8,128)S(1)}, f32[256,64]{1,0:T(8,128)S(1)}, u32[]{:S(2)}, u32[]{:S(2)}) %collective-permute-start.25) | collective-permute-done | bytes 65568 | tf_op jit(solution)/shard_map/ppermute | solution.py:97
  112.9 0.1 fusion.14
  113.0 2.6 %collective-permute-start.26 = (f32[256,64]{1,0:T(8,128)S(1)}, f32[256,64]{1,0:T(8,128)S(1)}, u32[]{:S(2)}, u32[]{:S(2)}) collective-permute-start(f32[256,64]{1,0:T(8,128)S(1)} %fusion.14), channel_id=1, source_target_pairs={{0,2},{1,3},{2,0},{3,1},{4,6},{5,7},{6,4},{7,5},{8,10},{9,11},{10,... | collective-permute-start | bytes 196616 | tf_op jit(solution)/shard_map/ppermute | solution.py:97
  115.6 0.1 reshape.17
  115.7 0.2 reshape.15
  116.0 5.4 %collective-permute-done.26 = f32[256,64]{1,0:T(8,128)S(1)} collective-permute-done((f32[256,64]{1,0:T(8,128)S(1)}, f32[256,64]{1,0:T(8,128)S(1)}, u32[]{:S(2)}, u32[]{:S(2)}) %collective-permute-start.26) | collective-permute-done | bytes 65568 | tf_op jit(solution)/shard_map/ppermute | solution.py:97
  121.4 0.1 copy.17
  121.5 10.1 %all_gather.3 = f32[2,64,1024]{2,1,0:T(8,128)S(1)} all-gather(f32[2,64,128]{2,1,0:T(8,128)S(1)} %bitcast.55), channel_id=1, replica_groups=mesh['bond'=8,'leg'=4] {'bond'}, dimensions={2}, use_global_device_ids=true | all-gather | bytes 589824 | tf_op jit(solution)/shard_map/all_gather | solution.py:170
  131.5 0.3 reshape.13
  131.8 0.3 copy.36
  132.2 3.5 %convolution_bitcast_fusion = f32[2,8,8,64,64]{4,3,2,1,0:T(8,128)S(1)} fusion(f32[2,16,64,64]{3,2,1,0:T(8,128)S(1)} %bitcast.52, f32[8,64,64,1,1]{2,1,0,3,4:T(8,128)S(1)} %reshape.17), kind=kOutput, calls=%fused_computation.3 | convolution fusion | flops 402653184 | bytes 2883584 | tf_op jit(solution)/shard_map/ztjc,qcd->ztqjd/dot_general | solution.py:85
  135.7 2.0 %fusion.3 = f32[8,8,64,64]{3,2,1,0:T(8,128)S(1)} fusion(f32[2,8,8,64,64]{4,3,2,1,0:T(8,128)S(1)} %convolution_bitcast_fusion, f32[2,8,64,64]{3,2,1,0:T(8,128)S(1)} %slice.48), kind=kOutput, calls=%fused_computation.9 | convolution fusion | flops 201326592 | bytes 3407872 | tf_op jit(solution)/shard_map/tqjd,tkd->tqjk/dot_general | solution.py:86
  137.6 2.0 %fusion.2 = f32[8,8,64,64]{3,2,1,0:T(8,128)S(1)} fusion(f32[2,8,8,64,64]{4,3,2,1,0:T(8,128)S(1)} %convolution_bitcast_fusion, f32[2,8,64,64]{3,2,1,0:T(8,128)S(1)} %slice.48), kind=kOutput, calls=%fused_computation.8 | convolution fusion | flops 201326592 | bytes 3407872 | tf_op jit(solution)/shard_map/tqjd,tkd->tqjk/dot_general | solution.py:89
  139.6 2.0 %subtract_bitcast_fusion = f32[1,8,8,64,64]{4,3,2,1,0:T(8,128)S(1)} fusion(f32[8,8,64,64]{3,2,1,0:T(8,128)S(1)} %fusion.3, f32[2,8,8,64,64]{4,3,2,1,0:T(8,128)S(1)} %convolution_bitcast_fusion, f32[2,8,64,64]{3,2,1,0:T(8,128)S(1)} %slice.48), kind=kOutput, calls=%fused_computation.7 | convolution fusion | flops 201588736 | bytes 5505024 | tf_op jit(solution)/shard_map/tqjd,tkd->tqjk/dot_general | solution.py:86
  141.7 2.3 %add_bitcast_fusion = f32[1,8,8,64,64]{4,3,2,1,0:T(8,128)S(1)} fusion(f32[8,8,64,64]{3,2,1,0:T(8,128)S(1)} %fusion.2, f32[2,8,8,64,64]{4,3,2,1,0:T(8,128)S(1)} %convolution_bitcast_fusion, f32[2,8,64,64]{3,2,1,0:T(8,128)S(1)} %slice.48), kind=kOutput, calls=%fused_computation.6 | convolution fusion | flops 201588736 | bytes 5505024 | tf_op jit(solution)/shard_map/tqjd,tkd->tqjk/dot_general | solution.py:89
  144.0 0.8 pad_maximum_fusion
  144.8 6.5 %fusion.6 = f32[2,8,16,8]{2,3,1,0:T(8,128)} fusion(f32[2,8,8,64,64]{4,3,2,1,0:T(8,128)S(1)} %pad_maximum_fusion, f32[16,64,64,1,1]{2,1,0,4,3:T(8,128)S(1)} %bitcast.53), kind=kOutput, calls=%fused_computation.12 | convolution fusion | flops 100663296 | bytes 2367488 | tf_op jit(solution)/shard_map/pjk,ztqjk->ztpq/dot_general | solution.py:93
  (32 shorter events, 0.1 us)
Async XLA Ops:
  0.0 18.7 %copy-start.5 = (s32[8,4]{1,0:T(8,128)S(1)}, s32[8,4]{1,0:T(8,128)}, u32[]{:S(2)}) copy-start(s32[8,4]{1,0:T(8,128)} %constant.14.clone) | copy-start | bytes 388
  0.0 18.7 %copy-start.6 = (s32[8,4]{1,0:T(8,128)S(1)}, s32[8,4]{1,0:T(8,128)}, u32[]{:S(2)}) copy-start(s32[8,4]{1,0:T(8,128)} %constant.15.clone) | copy-start | bytes 388
  0.0 18.8 %copy-start = (f32[64,8192]{1,0:T(8,128)S(1)}, f32[64,8192]{1,0:T(8,128)}, u32[]{:S(2)}) copy-start(f32[64,8192]{1,0:T(8,128)} %refs_0_.1) | copy-start | bytes 6291460
  0.0 32.8 %collective-permute-start.8 = (f32[64,8192]{1,0:T(8,128)}, f32[64,8192]{1,0:T(8,128)}, u32[]{:S(2)}, u32[]{:S(2)}) collective-permute-start(f32[64,8192]{1,0:T(8,128)} %refs_0_.1), channel_id=1, source_target_pairs={{0,4},{4,0},{8,12},{12,8},{16,20},{20,16},{24,28},{28,24},{1,5},{5... | collective-permute-start | bytes 6291464 | tf_op jit(solution)/shard_map/ppermute | solution.py:97
  3.3 4.6 %copy-start.1 = (f32[64,2048]{1,0:T(8,128)}, f32[64,2048]{1,0:T(8,128)S(1)}, u32[]{:S(2)}) copy-start(f32[64,2048]{1,0:T(8,128)S(1)} %get-tuple-element.26) | copy-start | bytes 1572868
  3.3 15.4 %collective-permute-start.4 = (f32[64,2048]{1,0:T(8,128)S(1)}, f32[64,2048]{1,0:T(8,128)}, u32[]{:S(2)}, u32[]{:S(2)}) collective-permute-start(f32[64,2048]{1,0:T(8,128)S(1)} %get-tuple-element.26), channel_id=1, source_target_pairs={{0,8},{4,12},{8,0},{12,4},{16,24},{20,28},{24,16},{28,20},{1,9},{5... | collective-permute-start | bytes 1572872 | tf_op jit(solution)/shard_map/ppermute | solution.py:97
  5.9 19.5 %collective-permute-start.5 = (f32[64,2048]{1,0:T(8,128)}, f32[64,2048]{1,0:T(8,128)}, u32[]{:S(2)}, u32[]{:S(2)}) collective-permute-start(f32[64,2048]{1,0:T(8,128)} %get-tuple-element.27), channel_id=1, source_target_pairs={{0,16},{4,20},{8,24},{12,28},{16,0},{20,4},{24,8},{28,12},{1,17},{... | collective-permute-start | bytes 1572872 | tf_op jit(solution)/shard_map/ppermute | solution.py:97
  7.4 22.2 %collective-permute-start = (f32[64,2048]{1,0:T(8,128)}, f32[64,2048]{1,0:T(8,128)S(1)}, u32[]{:S(2)}, u32[]{:S(2)}) collective-permute-start(f32[64,2048]{1,0:T(8,128)} %get-tuple-element.24), channel_id=1, source_target_pairs={{0,8},{4,12},{8,0},{12,4},{16,24},{20,28},{24,16},{28,20},{1,9},{5... | collective-permute-start | bytes 1572872 | tf_op jit(solution)/shard_map/ppermute | solution.py:97
  7.9 23.4 %collective-permute-start.1 = (f32[64,2048]{1,0:T(8,128)}, f32[64,2048]{1,0:T(8,128)S(1)}, u32[]{:S(2)}, u32[]{:S(2)}) collective-permute-start(f32[64,2048]{1,0:T(8,128)} %get-tuple-element.25), channel_id=1, source_target_pairs={{0,16},{4,20},{8,24},{12,28},{16,0},{20,4},{24,8},{28,12},{1,17},{... | collective-permute-start | bytes 1572872 | tf_op jit(solution)/shard_map/ppermute | solution.py:97
  18.7 14.1 %collective-permute-start.6 = (f32[64,2048]{1,0:T(8,128)}, f32[64,2048]{1,0:T(8,128)}, u32[]{:S(2)}, u32[]{:S(2)}) collective-permute-start(f32[64,2048]{1,0:T(8,128)} %collective-permute-done.4.refs_0_), channel_id=1, source_target_pairs={{0,4},{4,0},{8,12},{12,8},{16,20},{20,16},{24,28},{28,24},{1,5},{5... | collective-permute-start | bytes 1572872 | tf_op jit(solution)/shard_map/ppermute | solution.py:97
  25.3 14.7 %collective-permute-start.7 = (f32[64,2048]{1,0:T(8,128)}, f32[64,2048]{1,0:T(8,128)S(1)}, u32[]{:S(2)}, u32[]{:S(2)}) collective-permute-start(f32[64,2048]{1,0:T(8,128)} %collective-permute-done.5.refs_1_), channel_id=1, source_target_pairs={{0,4},{4,0},{8,12},{12,8},{16,20},{20,16},{24,28},{28,24},{1,5},{5... | collective-permute-start | bytes 1572872 | tf_op jit(solution)/shard_map/ppermute | solution.py:97
  29.5 14.5 %collective-permute-start.9 = (f32[64,2048]{1,0:T(8,128)}, f32[64,2048]{1,0:T(8,128)S(1)}, u32[]{:S(2)}, u32[]{:S(2)}) collective-permute-start(f32[64,2048]{1,0:T(8,128)} %collective-permute-done.4.refs_0_), channel_id=1, source_target_pairs={{0,16},{4,20},{8,24},{12,28},{16,0},{20,4},{24,8},{28,12},{1,17},{... | collective-permute-start | bytes 1572872 | tf_op jit(solution)/shard_map/ppermute | solution.py:97
  31.3 15.0 %collective-permute-start.10 = (f32[64,2048]{1,0:T(8,128)}, f32[64,2048]{1,0:T(8,128)S(1)}, u32[]{:S(2)}, u32[]{:S(2)}) collective-permute-start(f32[64,2048]{1,0:T(8,128)} %collective-permute-done.5.refs_1_), channel_id=1, source_target_pairs={{0,8},{4,12},{8,0},{12,4},{16,24},{20,28},{24,16},{28,20},{1,9},{5... | collective-permute-start | bytes 1572872 | tf_op jit(solution)/shard_map/ppermute | solution.py:97
  32.8 13.5 %collective-permute-start.2 = (f32[64,2048]{1,0:T(8,128)S(1)}, f32[64,2048]{1,0:T(8,128)S(1)}, u32[]{:S(2)}, u32[]{:S(2)}) collective-permute-start(f32[64,2048]{1,0:T(8,128)S(1)} %collective-permute-done.refs_0_), channel_id=1, source_target_pairs={{0,4},{4,0},{8,12},{12,8},{16,20},{20,16},{24,28},{28,24},{1,5},{5... | collective-permute-start | bytes 1572872 | tf_op jit(solution)/shard_map/ppermute | solution.py:97
  32.8 21.1 %collective-permute-start.3 = (f32[64,2048]{1,0:T(8,128)S(1)}, f32[64,2048]{1,0:T(8,128)S(1)}, u32[]{:S(2)}, u32[]{:S(2)}) collective-permute-start(f32[64,2048]{1,0:T(8,128)S(1)} %collective-permute-done.1.refs_1_), channel_id=1, source_target_pairs={{0,4},{4,0},{8,12},{12,8},{16,20},{20,16},{24,28},{28,24},{1,5},{5... | collective-permute-start | bytes 1572872 | tf_op jit(solution)/shard_map/ppermute | solution.py:97
  40.0 13.9 %copy-start.2 = (f32[64,2048]{1,0:T(8,128)S(1)}, f32[64,2048]{1,0:T(8,128)}, u32[]{:S(2)}) copy-start(f32[64,2048]{1,0:T(8,128)} %copy-done.1) | copy-start | bytes 1572868
  40.1 15.4 %collective-permute-start.11 = (f32[64,2048]{1,0:T(8,128)S(1)}, f32[64,2048]{1,0:T(8,128)S(1)}, u32[]{:S(2)}, u32[]{:S(2)}) collective-permute-start(f32[64,2048]{1,0:T(8,128)S(1)} %collective-permute-done.refs_0_), channel_id=1, source_target_pairs={{0,16},{4,20},{8,24},{12,28},{16,0},{20,4},{24,8},{28,12},{1,17},{... | collective-permute-start | bytes 1572872 | tf_op jit(solution)/shard_map/ppermute | solution.py:97
  44.0 12.1 %collective-permute-start.12 = (f32[64,2048]{1,0:T(8,128)S(1)}, f32[64,2048]{1,0:T(8,128)S(1)}, u32[]{:S(2)}, u32[]{:S(2)}) collective-permute-start(f32[64,2048]{1,0:T(8,128)S(1)} %collective-permute-done.1.refs_1_), channel_id=1, source_target_pairs={{0,8},{4,12},{8,0},{12,4},{16,24},{20,28},{24,16},{28,20},{1,9},{5... | collective-permute-start | bytes 1572872 | tf_op jit(solution)/shard_map/ppermute | solution.py:97
  46.3 16.3 %collective-permute-start.23 = (f32[64,2048]{1,0:T(8,128)S(1)}, f32[64,2048]{1,0:T(8,128)S(1)}, u32[]{:S(2)}, u32[]{:S(2)}) collective-permute-start(f32[64,2048]{1,0:T(8,128)S(1)} %collective-permute-done.9.refs_0_), channel_id=1, source_target_pairs={{0,4},{4,0},{8,12},{12,8},{16,20},{20,16},{24,28},{28,24},{1,5},{5... | collective-permute-start | bytes 1572872 | tf_op jit(solution)/shard_map/ppermute | solution.py:97
  46.3 17.8 %collective-permute-start.24 = (f32[64,2048]{1,0:T(8,128)S(1)}, f32[64,2048]{1,0:T(8,128)S(1)}, u32[]{:S(2)}, u32[]{:S(2)}) collective-permute-start(f32[64,2048]{1,0:T(8,128)S(1)} %collective-permute-done.10.refs_1_), channel_id=1, source_target_pairs={{0,4},{4,0},{8,12},{12,8},{16,20},{20,16},{24,28},{28,24},{1,5},{5... | collective-permute-start | bytes 1572872 | tf_op jit(solution)/shard_map/ppermute | solution.py:97
  53.9 14.6 %collective-permute-start.17 = (f32[64,2048]{1,0:T(8,128)S(1)}, f32[64,2048]{1,0:T(8,128)S(1)}, u32[]{:S(2)}, u32[]{:S(2)}) collective-permute-start(f32[64,2048]{1,0:T(8,128)S(1)} %copy-done.2), channel_id=1, source_target_pairs={{0,16},{4,20},{8,24},{12,28},{16,0},{20,4},{24,8},{28,12},{1,17},{... | collective-permute-start | bytes 1572872 | tf_op jit(solution)/shard_map/ppermute | solution.py:97
  55.5 15.0 %collective-permute-start.18 = (f32[64,2048]{1,0:T(8,128)}, f32[64,2048]{1,0:T(8,128)S(1)}, u32[]{:S(2)}, u32[]{:S(2)}) collective-permute-start(f32[64,2048]{1,0:T(8,128)} %get-tuple-element.27), channel_id=1, source_target_pairs={{0,8},{4,12},{8,0},{12,4},{16,24},{20,28},{24,16},{28,20},{1,9},{5... | collective-permute-start | bytes 1572872 | tf_op jit(solution)/shard_map/ppermute | solution.py:97
  56.1 14.4 %collective-permute-start.21 = (f32[64,2048]{1,0:T(8,128)S(1)}, f32[64,2048]{1,0:T(8,128)S(1)}, u32[]{:S(2)}, u32[]{:S(2)}) collective-permute-start(f32[64,2048]{1,0:T(8,128)S(1)} %collective-permute-done.11.refs_0_), channel_id=1, source_target_pairs={{0,4},{4,0},{8,12},{12,8},{16,20},{20,16},{24,28},{28,24},{1,5},{5... | collective-permute-start | bytes 1572872 | tf_op jit(solution)/shard_map/ppermute | solution.py:97
  62.6 17.9 %collective-permute-start.14 = (f32[64,2048]{1,0:T(8,128)}, f32[64,2048]{1,0:T(8,128)S(1)}, u32[]{:S(2)}, u32[]{:S(2)}) collective-permute-start(f32[64,2048]{1,0:T(8,128)} %get-tuple-element.25), channel_id=1, source_target_pairs={{0,8},{4,12},{8,0},{12,4},{16,24},{20,28},{24,16},{28,20},{1,9},{5... | collective-permute-start | bytes 1572872 | tf_op jit(solution)/shard_map/ppermute | solution.py:97
  64.1 16.4 %collective-permute-start.13 = (f32[64,2048]{1,0:T(8,128)}, f32[64,2048]{1,0:T(8,128)S(1)}, u32[]{:S(2)}, u32[]{:S(2)}) collective-permute-start(f32[64,2048]{1,0:T(8,128)} %get-tuple-element.24), channel_id=1, source_target_pairs={{0,16},{4,20},{8,24},{12,28},{16,0},{20,4},{24,8},{28,12},{1,17},{... | collective-permute-start | bytes 1572872 | tf_op jit(solution)/shard_map/ppermute | solution.py:97
  68.5 19.1 %collective-permute-start.22 = (f32[64,2048]{1,0:T(8,128)S(1)}, f32[64,2048]{1,0:T(8,128)S(1)}, u32[]{:S(2)}, u32[]{:S(2)}) collective-permute-start(f32[64,2048]{1,0:T(8,128)S(1)} %collective-permute-done.12.refs_1_), channel_id=1, source_target_pairs={{0,4},{4,0},{8,12},{12,8},{16,20},{20,16},{24,28},{28,24},{1,5},{5... | collective-permute-start | bytes 1572872 | tf_op jit(solution)/shard_map/ppermute | solution.py:97
  70.5 23.6 %collective-permute-start.19 = (f32[64,2048]{1,0:T(8,128)S(1)}, f32[64,2048]{1,0:T(8,128)S(1)}, u32[]{:S(2)}, u32[]{:S(2)}) collective-permute-start(f32[64,2048]{1,0:T(8,128)S(1)} %collective-permute-done.17.refs_0_), channel_id=1, source_target_pairs={{0,4},{4,0},{8,12},{12,8},{16,20},{20,16},{24,28},{28,24},{1,5},{5... | collective-permute-start | bytes 1572872 | tf_op jit(solution)/shard_map/ppermute | solution.py:97
  70.5 23.6 %collective-permute-start.20 = (f32[64,2048]{1,0:T(8,128)S(1)}, f32[64,2048]{1,0:T(8,128)S(1)}, u32[]{:S(2)}, u32[]{:S(2)}) collective-permute-start(f32[64,2048]{1,0:T(8,128)S(1)} %collective-permute-done.18.refs_1_), channel_id=1, source_target_pairs={{0,4},{4,0},{8,12},{12,8},{16,20},{20,16},{24,28},{28,24},{1,5},{5... | collective-permute-start | bytes 1572872 | tf_op jit(solution)/shard_map/ppermute | solution.py:97
  80.6 20.2 %collective-permute-start.16 = (f32[64,2048]{1,0:T(8,128)S(1)}, f32[64,2048]{1,0:T(8,128)S(1)}, u32[]{:S(2)}, u32[]{:S(2)}) collective-permute-start(f32[64,2048]{1,0:T(8,128)S(1)} %collective-permute-done.14.refs_1_), channel_id=1, source_target_pairs={{0,4},{4,0},{8,12},{12,8},{16,20},{20,16},{24,28},{28,24},{1,5},{5... | collective-permute-start | bytes 1572872 | tf_op jit(solution)/shard_map/ppermute | solution.py:97
  80.6 20.2 %collective-permute-start.15 = (f32[64,2048]{1,0:T(8,128)S(1)}, f32[64,2048]{1,0:T(8,128)S(1)}, u32[]{:S(2)}, u32[]{:S(2)}) collective-permute-start(f32[64,2048]{1,0:T(8,128)S(1)} %collective-permute-done.13.refs_0_), channel_id=1, source_target_pairs={{0,4},{4,0},{8,12},{12,8},{16,20},{20,16},{24,28},{28,24},{1,5},{5... | collective-permute-start | bytes 1572872 | tf_op jit(solution)/shard_map/ppermute | solution.py:97
  100.7 14.9 %copy-start.4 = (f32[8,4096]{1,0:T(8,128)S(1)}, f32[8,4096]{1,0:T(8,128)}, u32[]{:S(2)}) copy-start(f32[8,4096]{1,0:T(8,128)} %param.9) | copy-start | bytes 393220
  100.7 15.0 %copy-start.3 = (f32[16,4096]{1,0:T(8,128)S(1)}, f32[16,4096]{1,0:T(8,128)}, u32[]{:S(2)}) copy-start(f32[16,4096]{1,0:T(8,128)} %param.8) | copy-start | bytes 786436
  107.4 5.5 %collective-permute-start.25 = (f32[256,64]{1,0:T(8,128)S(1)}, f32[256,64]{1,0:T(8,128)S(1)}, u32[]{:S(2)}, u32[]{:S(2)}) collective-permute-start(f32[256,64]{1,0:T(8,128)S(1)} %slice_add_fusion), channel_id=1, source_target_pairs={{0,1},{1,0},{2,3},{3,2},{4,5},{5,4},{6,7},{7,6},{8,9},{9,8},{10,11... | collective-permute-start | bytes 196616 | tf_op jit(solution)/shard_map/ppermute | solution.py:97
  113.0 8.4 %collective-permute-start.26 = (f32[256,64]{1,0:T(8,128)S(1)}, f32[256,64]{1,0:T(8,128)S(1)}, u32[]{:S(2)}, u32[]{:S(2)}) collective-permute-start(f32[256,64]{1,0:T(8,128)S(1)} %fusion.14), channel_id=1, source_target_pairs={{0,2},{1,3},{2,0},{3,1},{4,6},{5,7},{6,4},{7,5},{8,10},{9,11},{10,... | collective-permute-start | bytes 196616 | tf_op jit(solution)/shard_map/ppermute | solution.py:97

commit v2 on v0

v2 whole, which is shorter than its diff:
```python
import functools
import math

import jax
import jax.numpy as jnp
import numpy as np
from jax import lax
from jax.experimental import pallas as pl
from jax.experimental.pallas import tpu as pltpu
from jax.sharding import PartitionSpec as P

LANES = 128
STEP = 2048
TWIN_CUTS = 2
TRANSPOSED = (((1,), (1,)), ((), ()))
PLAIN = (((1,), (0,)), ((), ()))


def split_bf16(x):
    hi = x.astype(jnp.bfloat16)
    return hi, (x - hi.astype(jnp.float32)).astype(jnp.bfloat16)


def dot(a, b, dims):
    return lax.dot_general(a, b, dims, preferred_element_type=jnp.float32)


def project_kernel(places, block_width, row, last, table, amp, *refs):
    count = 1 + max(place[0] for place in places)
    blocks, start, out = refs[:count], refs[count], refs[count + 1]
    amp_slots, block_slots, both, total, amp_sems, block_sems = refs[count + 2 :]
    steps, bond_dim, unit = block_slots.shape
    for step, (which, position, column, offset) in enumerate(places):
        here = pl.ds(pl.multiple_of(table[row, column] * block_width + offset, LANES), unit)
        pltpu.make_async_copy(amp.at[:, :, here], amp_slots.at[step], amp_sems.at[step]).start()
        there = pl.ds(position, unit)
        pltpu.make_async_copy(blocks[which].at[:, there], block_slots.at[step], block_sems.at[step]).start()
    total[...] = start[...]

    def body(step, carry):
        pltpu.make_async_copy(
            blocks[0].at[:, pl.ds(0, unit)], block_slots.at[step], block_sems.at[step]
        ).wait()
        hi, lo = split_bf16(block_slots[step])
        both[:bond_dim, :] = hi
        both[bond_dim:, :] = lo
        pltpu.make_async_copy(
            amp.at[:, :, pl.ds(0, unit)], amp_slots.at[step], amp_sems.at[step]
        ).wait()
        hi, lo = split_bf16(amp_slots[step].reshape(-1, unit))
        weights = both[...]
        total[...] += dot(hi, weights, TRANSPOSED) + dot(lo, weights, TRANSPOSED)
        return carry

    lax.fori_loop(0, steps, body, 0)
    if last:
        out[...] = (total[:, :bond_dim] + total[:, bond_dim:]).T
    else:
        out[...] = total[...]


def project(table, row, column, amplitudes, blocks, unit, start, last=False):
    step = functools.reduce(math.gcd, [block.shape[1] for block in blocks], unit)
    step = STEP if step % STEP == 0 else step
    parts, rows, _ = amplitudes.shape
    bond_dim = blocks[0].shape[0]
    places = []
    offset = column * unit
    for which, block in enumerate(blocks):
        for position in range(0, block.shape[1], step):
            places.append((which, position, offset // unit, offset % unit))
            offset += step
    steps = len(places)
    shape = (bond_dim, parts * rows) if last else start.shape
    vmem = pl.BlockSpec(memory_space=pltpu.VMEM)
    anywhere = pl.BlockSpec(memory_space=pl.ANY)
    scratch = 4 * steps * step * (parts * rows + bond_dim)
    return pl.pallas_call(
        functools.partial(project_kernel, places, unit, row, last),
        in_specs=[pl.BlockSpec(memory_space=pltpu.SMEM), anywhere] + [anywhere] * len(blocks) + [vmem],
        out_specs=vmem,
        out_shape=jax.ShapeDtypeStruct(shape, jnp.float32),
        scratch_shapes=[
            pltpu.VMEM((steps, parts, rows, step), jnp.float32),
            pltpu.VMEM((steps, bond_dim, step), jnp.float32),
            pltpu.VMEM((2 * bond_dim, step), jnp.bfloat16),
            pltpu.VMEM(start.shape, jnp.float32),
            pltpu.SemaphoreType.DMA((steps,)),
            pltpu.SemaphoreType.DMA((steps,)),
        ],
        compiler_params=pltpu.CompilerParams(vmem_limit_bytes=scratch + 10 * 2**20),
        cost_estimate=pl.CostEstimate(
            flops=8 * steps * bond_dim * parts * rows * step,
            bytes_accessed=4 * steps * step * (parts * rows + bond_dim),
            transcendentals=0,
        ),
    )(table, amplitudes, *blocks, start)


def coarsen_kernel(rows_q, slab, first_hi, first_lo, third, out, paired):
    pairs, bond_dim, lanes = slab.shape
    wide = 2 * bond_dim
    hi, lo = split_bf16(slab[...].reshape(pairs * bond_dim, lanes))
    inner = dot(hi, first_hi[...], PLAIN) + dot(lo, first_hi[...], PLAIN) + dot(hi, first_lo[...], PLAIN)
    for t in range(pairs):
        here = inner[t * bond_dim : (t + 1) * bond_dim]
        left = jnp.concatenate([here[:, q * wide : (q + 1) * wide] for q in range(rows_q)], 0)
        real = slab[t, :, bond_dim : 2 * bond_dim]
        imag = slab[t, :, 3 * bond_dim : 4 * bond_dim]
        right = jnp.concatenate(
            [jnp.concatenate([real, -imag], 1), jnp.concatenate([imag, real], 1)], 0
        )
        left_hi, left_lo = split_bf16(left)
        right_hi, right_lo = split_bf16(right)
        size = rows_q * bond_dim
        paired[t * size : (t + 1) * size, :] = (
            dot(left_hi, right_hi, TRANSPOSED)
            + dot(left_lo, right_hi, TRANSPOSED)
            + dot(left_hi, right_lo, TRANSPOSED)
        )
    count = pairs * rows_q
    total = jnp.zeros((2 * count, third.shape[0]), jnp.float32)
    for j in range(0, bond_dim, 2):
        columns = [paired[pl.ds(j + i, count, stride=bond_dim), :] for i in range(2)]
        hi, lo = split_bf16(jnp.concatenate(columns, 1))
        both = jnp.concatenate([hi, lo], 0)
        total += dot(both, third[:, j * wide : (j + 2) * wide], TRANSPOSED)
    half = third.shape[0] // 2
    result = total[:count, :half] + total[count:, :half] + total[:count, half:]
    rows_p = half // 2
    out[0] = result[:, :rows_p]
    out[1] = result[:, rows_p:]


def coarsen(slab, weights):
    first_hi, first_lo, third = weights
    pairs, bond_dim, _ = slab.shape
    rows_q = first_hi.shape[1] // (2 * bond_dim)
    rows_p = third.shape[0] // 4
    out = pl.pallas_call(
        functools.partial(coarsen_kernel, rows_q),
        in_specs=[pl.BlockSpec(memory_space=pltpu.VMEM)] * 4,
        out_specs=pl.BlockSpec(memory_space=pltpu.VMEM),
        out_shape=jax.ShapeDtypeStruct((2, pairs * rows_q, rows_p), jnp.float32),
        scratch_shapes=[pltpu.VMEM((pairs * rows_q * bond_dim, 2 * bond_dim), jnp.float32)],
        compiler_params=pltpu.CompilerParams(vmem_limit_bytes=40 * 2**20),
    )(slab, first_hi, first_lo, third)
    return out.reshape(2, pairs, rows_q, rows_p).transpose(0, 1, 3, 2)


def rounded_split(x):
    hi = lax.reduce_precision(x, exponent_bits=8, mantissa_bits=7)
    return hi.astype(jnp.bfloat16), (x - hi).astype(jnp.bfloat16)


def coarsen_weights(row_map, col_map, bond_dim):
    rows_q, rows_p = col_map.shape[0], row_map.shape[0]
    cols = col_map.reshape(rows_q, bond_dim, bond_dim).transpose(1, 0, 2)
    zero = jnp.zeros_like(cols)
    real = jnp.stack([cols, zero], 2).reshape(bond_dim, -1)
    imag = jnp.stack([zero, cols], 2).reshape(bond_dim, -1)
    gap = jnp.zeros_like(real)
    first_hi, first_lo = rounded_split(jnp.concatenate([real, gap, imag, gap], 0))
    rows = row_map.reshape(rows_p, bond_dim, bond_dim)
    zero = jnp.zeros_like(rows)
    third = jnp.concatenate([jnp.concatenate([rows, zero], 2), jnp.concatenate([zero, rows], 2)], 0)
    third = third.reshape(2 * rows_p, -1)
    return first_hi, first_lo, jnp.concatenate(rounded_split(third), 0)


def swap(x, axis, size, partner):
    return lax.ppermute(x, axis, [(i, partner(i)) for i in range(size)])


def twin(device):
    return device ^ 1


def after(x, *others):
    return lax.optimization_barrier((x, *others))[0]


def gather_and_project(amplitudes, vectors, size, weights):
    bond_dim, width = vectors.shape
    dims = (size // 2).bit_length() - 1
    halves = 2 if width % (2 * LANES) == 0 else 1
    unit = width // halves

    held = [(0, 0, h) for h in range(halves)]
    rounds = []
    for step in range(dims):
        masks = [2 << ((core + step) % dims) for core in range(2)]
        got = [(first ^ masks[0], second ^ masks[1], h) for first, second, h in held]
        rounds += [(masks, sent, block) for sent, block in zip(held, got)]
        held = held + got

    def both(blocks):
        return blocks + [(second ^ 1, first ^ 1, h) for first, second, h in blocks]

    groups = [both(held[:halves])] + [both([block]) for _, _, block in rounds]
    longest = max(len(g) for g in groups)
    where = np.array([g + [(0, 0, 0)] * (longest - len(g)) for g in groups], np.int32)
    me = lax.axis_index("bond")
    origin = me ^ jnp.where(me % 2 == 0, where[:, :, 0], where[:, :, 1])
    table = origin * halves + where[:, :, 2]

    arrays = {block: vectors[:, block[2] * unit : (block[2] + 1) * unit] for block in held[:halves]}
    total = jnp.zeros((amplitudes.shape[0] * amplitudes.shape[1], 2 * bond_dim), jnp.float32)
    add = functools.partial(project, table)
    arrived = []
    totals = [total]
    products = [lambda total: add(0, 0, amplitudes, [vectors], unit, total)]

    def products_done(count):
        while len(totals) <= count:
            totals.append(products[len(totals) - 1](totals[-1]))
        return totals[count]

    for number, (masks, sent, block) in enumerate(rounds):
        array = arrays[sent]
        if number >= 2:
            array = after(array, arrived[number - 2])
        if number == 3:
            array = after(array, *weights)
        if number >= 1:
            array = after(array, products_done(number))
        arrays[block] = swap(array, "bond", size, lambda i: i ^ masks[i % 2])
        arrived.append(arrays[block])
        if number == 0:
            other = swap(vectors, "bond", size, twin)
            products.append(lambda total: add(0, halves, amplitudes, [other], unit, total))
        mine = arrays[block]
        if number >= len(rounds) - 2:
            mine = after(mine, products_done(number + 2))
        cuts = TWIN_CUTS if unit % (TWIN_CUTS * LANES) == 0 else 1
        pair = [arrays[block]]
        for cut in range(cuts):
            some = mine[:, cut * unit // cuts : (cut + 1) * unit // cuts] if cuts > 1 else mine
            pair.append(swap(some, "bond", size, twin))
        products.append(
            lambda total, number=number, pair=pair: add(number + 1, 0, amplitudes, pair, unit, total)
        )
    total = products_done(len(rounds) + 1)
    if rounds:
        total = add(len(rounds), 0, amplitudes, pair[:1], unit, total)
        total = add(len(rounds), 1, amplitudes, pair[1:], unit, total, last=True)
    return total


def local(bond, leg, amplitudes, vectors, row_map, col_map):
    bond_dim = vectors.shape[0]
    parts, rows, _ = amplitudes.shape
    weights = coarsen_weights(row_map, col_map, bond_dim)
    total = gather_and_project(amplitudes, vectors, bond, weights)
    mask = 1
    while mask < leg:
        total = total + swap(total, "leg", leg, lambda i: i ^ mask)
        mask *= 2
    slab = lax.all_gather(total, "bond", axis=0)
    if rows != 2 * bond_dim:
        slab = slab.reshape(bond, bond_dim, parts, rows).transpose(1, 2, 0, 3)
        slab = slab.reshape(bond_dim, parts, -1, 2 * bond_dim).transpose(2, 0, 1, 3)
        slab = slab.reshape(-1, bond_dim, parts * 2 * bond_dim)
    return coarsen(slab, weights)


def solution(mesh):
    return jax.shard_map(
        functools.partial(local, mesh.shape["bond"], mesh.shape["leg"]),
        mesh=mesh,
        in_specs=(
            P(None, "bond", "leg"),
            P(None, ("leg", "bond")),
            P("leg", None),
            P("bond", None),
        ),
        out_specs=P(None, None, "leg", "bond"),
        check_vma=False,
    )
```

time: 241 us -> 109 us (0.45)
  waiting for transfers between devices: 129 us -> 16.9 us
  matrix products: 85.4 us -> 0 us
  Pallas kernels: 0 us -> 50.7 us
  starting transfers between devices: 0.04 us -> 19.1 us
  between operations: 13.5 us -> 0.31 us
  local copies, waits for them, and re-layouts: 0.95 us -> 7.25 us
  other arithmetic: 0.81 us -> 4.27 us
    all_gather x1 -> x0, waiting for transfers between devices: 94.5 us -> none  [local(): lax.all_gather(vectors, 'bond', axis=1, tiled=True)]
    dot_general x7 -> x0, matrix products: 85.4 us -> none  [the longest x1 67.1 us: local(): jnp.einsum('jk,zrk->zjr', lax.all_gather(vectors, 'bond', axis=1, tiled=T...]
    pallas_call x0 -> x10, Pallas kernels: none -> 50.7 us  [the longest x9 46.3 us: project(): pl.pallas_call(functools.partial(project_kernel, places, unit, row, last)...]
    psum x1 -> x0, waiting for transfers between devices: 33.8 us -> none  [local(): summed = lax.psum(partial_proj, 'leg')]
    ppermute x0 -> x21, starting transfers between devices: none -> 19.1 us  [swap(): return lax.ppermute(x, axis, [(i, partner(i)) for i in range(size)])]
    ppermute x0 -> x21, waiting for transfers between devices: none -> 16.9 us  [swap(): return lax.ppermute(x, axis, [(i, partner(i)) for i in range(size)])]
    slice x1 -> x7, local copies, waits for them, and re-layouts: 0.04 us -> 3.76 us  [the longest x1 3.22 us: gather_and_project(): vectors[:, block[2] * unit:(block[2] + 1) * unit]]
    concatenate x0 -> x2, other arithmetic: none -> 2.53 us  [the longest x1 1.44 us: coarsen_weights(): jnp.concatenate([jnp.concatenate([rows, zero], 2), jnp.concatenate([zero,...]
  transfers between devices with their start and end apart: 2 -> 21, of which waited for: 2 -> 7; matrix products, arithmetic and copies ran while one was open for 0% -> 10% of each run, Pallas kernels for 0% -> 39%
where the time goes in v2:
time: 109 us
  Pallas kernels  50.7 us (47%)
  starting transfers between devices  19.1 us (18%)
  waiting for transfers between devices  16.9 us (16%)
  blocking collectives  10.2 us (9%)
  local copies, waits for them, and re-layouts  7.25 us (7%)
  other arithmetic  4.27 us (4%)
    pallas_call x9, Pallas kernels, project(): pl.pallas_call(functools.partial(project_kernel, places, unit, row, last)...  46.3 us
    ppermute x21, starting transfers between devices, swap(): return lax.ppermute(x, axis, [(i, partner(i)) for i in range(size)])  19.1 us
    ppermute x21, waiting for transfers between devices, swap(): return lax.ppermute(x, axis, [(i, partner(i)) for i in range(size)])  16.9 us
    all_gather x1, blocking collectives, local(): slab = lax.all_gather(total, 'bond', axis=0)  10.2 us
    pallas_call x1, Pallas kernels, coarsen(): pl.pallas_call(functools.partial(coarsen_kernel, rows_q), in_specs=[pl.Bl...  4.46 us
    slice x1, local copies, waits for them, and re-layouts, gather_and_project(): vectors[:, block[2] * unit:(block[2] + 1) * unit]  3.22 us
  transfers between devices with their start and end apart: 21, of which 7 were waited for; matrix products, arithmetic and copies ran while one was open for 10% of the time, Pallas kernels for 39%

profile of v2, /device:TPU:0, one launch (start us, length us, event | category | flops | bytes accessed | tf_op | source)
XLA Modules:
  0.0 108.8 jit_solution(8094462193539344400)
XLA Ops:
  0.0 0.5 collective-permute-start.4
  0.5 3.2 %fusion.2 = (f32[64,4096]{1,0:T(8,128)}, f32[64,4096]{1,0:T(8,128)}) fusion(f32[64,8192]{1,0:T(8,128)} %refs_0_.1), kind=kLoop, calls=%fused_computation.12 | loop fusion | bytes 4194304 | tf_op jit(solution)/shard_map/slice | solution.py:207
  3.8 2.5 %collective-permute-start.1 = (f32[64,4096]{1,0:T(8,128)}, f32[64,4096]{1,0:T(8,128)S(1)}, u32[]{:S(2)}, u32[]{:S(2)}) collective-permute-start(f32[64,4096]{1,0:T(8,128)} %get-tuple-element.23), channel_id=1, source_target_pairs={{0,8},{4,20},{8,0},{12,28},{16,24},{20,4},{24,16},{28,12},{1,9},{5... | collective-permute-start | bytes 3145736 | tf_op jit(solution)/shard_map/ppermute | solution.py:172
  6.3 0.0 copy-start.2
  6.3 5.5 %shard_map.73.refs_1_ = f32[256,128]{1,0:T(8,128)S(1)} custom-call(s32[7,4]{1,0:T(8,128)S(1)} %multiply_add_fusion.table, f32[2,128,65536]{2,1,0:T(8,128)} %amp.17, f32[64,8192]{1,0:T(8,128)S(1)} %copy-done, f32[256,128]{1,0:T(8,128)S(1)} %broadcast_in_dim.7.refs_1_), custom_call_target="tpu_custom_call" | custom-call | flops 1073741824 | bytes 10485760 | tf_op jit(solution)/shard_map/pallas_call | solution.py:78
  11.8 0.1 collective-permute-start
  11.9 1.0 reshape.21
  12.9 1.4 %select_maximum_fusion = f32[32,64,128]{2,1,0:T(8,128)S(1)} fusion(f32[16,64,64]{2,1,0:T(8,128)} %reshape.21), kind=kLoop, calls=%fused_computation.6 | loop fusion | flops 1310720 | bytes 1310720 | tf_op jit(solution)/shard_map/concatenate | solution.py:166
  14.3 0.0 copy-start.3
  14.3 0.6 reduce-precision_convert_fusion
  15.0 1.1 %pad_maximum_fusion.1.third = bf16[64,8192]{1,0:T(8,128)(2,1)} fusion(bf16[32,8192]{1,0:T(8,128)(2,1)S(1)} %get-tuple-element.44, bf16[32,8192]{1,0:T(8,128)(2,1)S(1)} %get-tuple-element.43), kind=kLoop, calls=%fused_computation.10 | loop fusion | flops 2097152 | bytes 2097152 | tf_op jit(solution)/shard_map/concatenate | solution.py:168
  16.1 0.1 reshape.18
  16.2 0.2 copy.8
  16.3 0.5 fusion.9
  16.8 0.5 reshape.19
  17.3 1.2 %reshape.20 = f32[64,1024]{1,0:T(8,128)} reshape(f32[64,8,2,64]{3,2,1,0:T(2,128)S(1)} %get-tuple-element.48) | data formatting | bytes 524288 | tf_op jit(solution)/shard_map/reshape | solution.py:161
  18.5 1.1 %fusion = (bf16[256,1024]{1,0:T(8,128)(2,1)S(1)}, bf16[256,1024]{1,0:T(8,128)(2,1)S(1)}) fusion(f32[64,1024]{1,0:T(8,128)S(1)} %broadcast_in_dim.8, f32[64,1024]{1,0:T(8,128)} %reshape.20, f32[64,1024]{1,0:T(8,128)S(1)} %reshape.19), kind=kLoop, calls=%fused_computation.4 | loop fusion | flops 1835008 | bytes 1835008 | tf_op jit(solution)/shard_map/convert_element_type | solution.py:153
  19.6 0.0 collective-permute-done.1.refs_0_
  19.6 0.1 fusion.8
  19.7 0.2 collective-permute-start.2
  19.9 0.4 collective-permute-start.3
  20.3 0.0 collective-permute-done.4.refs_0_
  20.3 5.6 %shard_map.74.refs_3_ = f32[256,128]{1,0:T(8,128)S(1)} custom-call(s32[7,4]{1,0:T(8,128)S(1)} %multiply_add_fusion.table, f32[2,128,65536]{2,1,0:T(8,128)} %amp.17, f32[64,8192]{1,0:T(8,128)} %collective-permute-done.4.refs_0_, f32[256,128]{1,0:T(8,128)S(1)} %shard_map.73.refs_1_), custom_call_target="tpu_custom_call" | custom-call | flops 1073741824 | bytes 10485760 | tf_op jit(solution)/shard_map/pallas_call | solution.py:78
  25.9 2.1 %collective-permute-start.6 = (f32[64,4096]{1,0:T(8,128)}, f32[64,4096]{1,0:T(8,128)S(1)}, u32[]{:S(2)}, u32[]{:S(2)}) collective-permute-start(f32[64,4096]{1,0:T(8,128)} %get-tuple-element.23), channel_id=1, source_target_pairs={{0,16},{4,12},{8,24},{12,4},{16,0},{20,28},{24,8},{28,20},{1,17},{... | collective-permute-start | bytes 3145736 | tf_op jit(solution)/shard_map/ppermute | solution.py:172
  28.0 3.7 %collective-permute-done.refs_0_ = f32[64,4096]{1,0:T(8,128)S(1)} collective-permute-done((f32[64,4096]{1,0:T(8,128)}, f32[64,4096]{1,0:T(8,128)S(1)}, u32[]{:S(2)}, u32[]{:S(2)}) %collective-permute-start) | collective-permute-done | bytes 1048608 | tf_op jit(solution)/shard_map/ppermute | solution.py:172
  31.8 0.1 fusion.6
  31.9 0.1 collective-permute-start.10
  31.9 0.5 collective-permute-start.9
  32.4 0.0 collective-permute-done.2.refs_1_
  32.4 0.0 collective-permute-done.3.refs_2_
  32.4 5.5 %shard_map.75.refs_3_ = f32[256,128]{1,0:T(8,128)S(1)} custom-call(s32[7,4]{1,0:T(8,128)S(1)} %multiply_add_fusion.table, f32[2,128,65536]{2,1,0:T(8,128)} %amp.17, f32[64,4096]{1,0:T(8,128)S(1)} %collective-permute-done.1.refs_0_, f32[64,2048]{1,0:T(8,128)S(1)} %collective-permute-done.2.refs_1_, f32[64,2048]{1,0:T(8,128)S(1)} %collective-permute-done.3.refs_2_, ...), custom_call_target="tpu_custom_call" | custom-call | flops 1073741824 | bytes 10485760 | tf_op jit(solution)/shard_map/pallas_call | solution.py:78
  37.9 2.4 %collective-permute-start.5 = (f32[64,4096]{1,0:T(8,128)}, f32[64,4096]{1,0:T(8,128)S(1)}, u32[]{:S(2)}, u32[]{:S(2)}) collective-permute-start(f32[64,4096]{1,0:T(8,128)} %get-tuple-element.20), channel_id=1, source_target_pairs={{0,16},{4,12},{8,24},{12,4},{16,0},{20,28},{24,8},{28,20},{1,17},{... | collective-permute-start | bytes 3145736 | tf_op jit(solution)/shard_map/ppermute | solution.py:172
  40.3 0.0 collective-permute-done.10.refs_2_
  40.3 0.0 collective-permute-done.9.refs_1_
  40.3 5.5 %shard_map.76.refs_3_ = f32[256,128]{1,0:T(8,128)S(1)} custom-call(s32[7,4]{1,0:T(8,128)S(1)} %multiply_add_fusion.table, f32[2,128,65536]{2,1,0:T(8,128)} %amp.17, f32[64,4096]{1,0:T(8,128)S(1)} %collective-permute-done.refs_0_, f32[64,2048]{1,0:T(8,128)S(1)} %collective-permute-done.9.refs_1_, f32[64,2048]{1,0:T(8,128)S(1)} %collective-permute-done.10.refs_2_, ...), custom_call_target="tpu_custom_call" | custom-call | flops 1073741824 | bytes 10485760 | tf_op jit(solution)/shard_map/pallas_call | solution.py:78
  45.8 0.1 fusion.7
  45.9 0.1 collective-permute-start.7
  46.0 0.5 collective-permute-start.8
  46.5 0.8 collective-permute-start.12
  47.3 6.0 %collective-permute-done.5.refs_0_ = f32[64,4096]{1,0:T(8,128)S(1)} collective-permute-done((f32[64,4096]{1,0:T(8,128)}, f32[64,4096]{1,0:T(8,128)S(1)}, u32[]{:S(2)}, u32[]{:S(2)}) %collective-permute-start.5) | collective-permute-done | bytes 1048608 | tf_op jit(solution)/shard_map/ppermute | solution.py:172
  53.3 0.1 fusion.5
  53.4 0.1 collective-permute-start.13
  53.5 0.5 collective-permute-start.14
  54.0 5.5 %shard_map.77.refs_3_ = f32[256,128]{1,0:T(8,128)S(1)} custom-call(s32[7,4]{1,0:T(8,128)S(1)} %multiply_add_fusion.table, f32[2,128,65536]{2,1,0:T(8,128)} %amp.17, f32[64,4096]{1,0:T(8,128)S(1)} %collective-permute-done.6.refs_0_, f32[64,2048]{1,0:T(8,128)S(1)} %collective-permute-done.7.refs_1_, f32[64,2048]{1,0:T(8,128)S(1)} %collective-permute-done.8.refs_2_, ...), custom_call_target="tpu_custom_call" | custom-call | flops 1073741824 | bytes 10485760 | tf_op jit(solution)/shard_map/pallas_call | solution.py:78
  59.4 2.1 %collective-permute-start.11 = (f32[64,4096]{1,0:T(8,128)S(1)}, f32[64,4096]{1,0:T(8,128)S(1)}, u32[]{:S(2)}, u32[]{:S(2)}) collective-permute-start(f32[64,4096]{1,0:T(8,128)S(1)} %collective-permute-done.refs_0_), channel_id=1, source_target_pairs={{0,16},{4,12},{8,24},{12,4},{16,0},{20,28},{24,8},{28,20},{1,17},{... | collective-permute-start | bytes 3145736 | tf_op jit(solution)/shard_map/ppermute | solution.py:172
  61.5 5.5 %shard_map.78.refs_3_ = f32[256,128]{1,0:T(8,128)S(1)} custom-call(s32[7,4]{1,0:T(8,128)S(1)} %multiply_add_fusion.table, f32[2,128,65536]{2,1,0:T(8,128)} %amp.17, f32[64,4096]{1,0:T(8,128)S(1)} %collective-permute-done.5.refs_0_, f32[64,2048]{1,0:T(8,128)S(1)} %collective-permute-done.13.refs_1_, f32[64,2048]{1,0:T(8,128)S(1)} %collective-permute-done.14.refs_2_, ...), custom_call_target="tpu_custom_call" | custom-call | flops 1073741824 | bytes 10485760 | tf_op jit(solution)/shard_map/pallas_call | solution.py:78
  67.0 0.1 fusion.4
  67.1 0.1 collective-permute-start.15
  67.2 0.5 collective-permute-start.16
  67.7 1.4 %collective-permute-done.15.refs_1_ = f32[64,2048]{1,0:T(8,128)S(1)} collective-permute-done((f32[64,2048]{1,0:T(8,128)S(1)}, f32[64,2048]{1,0:T(8,128)S(1)}, u32[]{:S(2)}, u32[]{:S(2)}) %collective-permute-start.15) | collective-permute-done | bytes 524320 | tf_op jit(solution)/shard_map/ppermute | solution.py:172
  69.1 0.7 collective-permute-done.16.refs_2_
  69.8 5.5 %shard_map.79.refs_1_ = f32[256,128]{1,0:T(8,128)S(1)} custom-call(s32[7,4]{1,0:T(8,128)S(1)} %multiply_add_fusion.table, f32[2,128,65536]{2,1,0:T(8,128)} %amp.17, f32[64,4096]{1,0:T(8,128)S(1)} %collective-permute-done.12.refs_0_, f32[64,2048]{1,0:T(8,128)S(1)} %collective-permute-done.15.refs_1_, f32[64,2048]{1,0:T(8,128)S(1)} %collective-permute-done.16.refs_2_, ...), custom_call_target="tpu_custom_call" | custom-call | flops 1073741824 | bytes 10485760 | tf_op jit(solution)/shard_map/pallas_call | solution.py:78
  75.3 0.5 collective-permute-done.11.refs_0_
  75.8 0.1 fusion.3
  75.9 0.1 collective-permute-start.17
  75.9 0.5 collective-permute-start.18
  76.4 3.8 %shard_map.80.refs_2_ = f32[256,128]{1,0:T(8,128)S(1)} custom-call(s32[7,4]{1,0:T(8,128)S(1)} %multiply_add_fusion.table, f32[2,128,65536]{2,1,0:T(8,128)} %amp.17, f32[64,4096]{1,0:T(8,128)S(1)} %collective-permute-done.11.refs_0_, f32[256,128]{1,0:T(8,128)S(1)} %shard_map.79.refs_1_), custom_call_target="tpu_custom_call" | custom-call | flops 536870912 | bytes 5242880 | tf_op jit(solution)/shard_map/pallas_call | solution.py:78
  80.3 4.1 %shard_map.81 = f32[64,256]{1,0:T(8,128)S(1)} custom-call(s32[7,4]{1,0:T(8,128)S(1)} %multiply_add_fusion.table, f32[2,128,65536]{2,1,0:T(8,128)} %amp.17, f32[64,2048]{1,0:T(8,128)S(1)} %collective-permute-done.17.refs_0_, f32[64,2048]{1,0:T(8,128)S(1)} %collective-permute-done.18.refs_1_, f32[256,128]{1,0:T(8,128)S(1)} %shard_map.80.refs_2_), custom_call_target="tpu_custom_call" | custom-call | flops 536870912 | bytes 5242880 | tf_op jit(solution)/shard_map/pallas_call | solution.py:78
  84.4 2.1 %collective-permute-start.19 = (f32[64,256]{1,0:T(8,128)S(1)}, f32[64,256]{1,0:T(8,128)S(1)}, u32[]{:S(2)}, u32[]{:S(2)}) collective-permute-start(f32[64,256]{1,0:T(8,128)S(1)} %shard_map.81), channel_id=1, source_target_pairs={{0,1},{1,0},{2,3},{3,2},{4,5},{5,4},{6,7},{7,6},{8,9},{9,8},{10,11... | collective-permute-start | bytes 196616 | tf_op jit(solution)/shard_map/ppermute | solution.py:172
  86.5 2.3 %collective-permute-done.19 = f32[64,256]{1,0:T(8,128)S(1)} collective-permute-done((f32[64,256]{1,0:T(8,128)S(1)}, f32[64,256]{1,0:T(8,128)S(1)}, u32[]{:S(2)}, u32[]{:S(2)}) %collective-permute-start.19) | collective-permute-done | bytes 65568 | tf_op jit(solution)/shard_map/ppermute | solution.py:172
  88.9 3.0 %collective-permute-start.20 = (f32[64,256]{1,0:T(8,128)S(1)}, f32[64,256]{1,0:T(8,128)S(1)}, u32[]{:S(2)}, u32[]{:S(2)}) collective-permute-start(f32[64,256]{1,0:T(8,128)S(1)} %add.23), channel_id=1, source_target_pairs={{0,2},{1,3},{2,0},{3,1},{4,6},{5,7},{6,4},{7,5},{8,10},{9,11},{10,... | collective-permute-start | bytes 196616 | tf_op jit(solution)/shard_map/ppermute | solution.py:172
  91.9 2.2 %collective-permute-done.20 = f32[64,256]{1,0:T(8,128)S(1)} collective-permute-done((f32[64,256]{1,0:T(8,128)S(1)}, f32[64,256]{1,0:T(8,128)S(1)}, u32[]{:S(2)}, u32[]{:S(2)}) %collective-permute-start.20) | collective-permute-done | bytes 65568 | tf_op jit(solution)/shard_map/ppermute | solution.py:172
  94.1 10.2 %all-gather = f32[512,256]{1,0:T(8,128)S(1)} all-gather(f32[64,256]{1,0:T(8,128)S(1)} %add.24), channel_id=2, replica_groups=mesh['bond'=8,'leg'=4] {'bond'}, dimensions={0}, use_global_device_ids=true | all-gather | bytes 589824 | tf_op jit(solution)/shard_map/all_gather | solution.py:259
  104.3 4.5 %shard_map.82 = f32[2,64,16]{2,1,0:T(8,128)} custom-call(f32[8,64,256]{2,1,0:T(8,128)S(1)} %bitcast.11, bf16[256,1024]{1,0:T(8,128)(2,1)S(1)} %get-tuple-element.46.first_hi, bf16[256,1024]{1,0:T(8,128)(2,1)S(1)} %get-tuple-element.45.first_lo, bf16[64,8192]{1,0:T(8,128)(2,1)S(1)} %copy-done.1), custom_call_target="tpu_custom_call" | custom-call | tf_op jit(solution)/shard_map/pallas_call | solution.py:140
  (25 shorter events, 0.1 us)
Async XLA Ops:
  0.0 6.3 %copy-start.4 = (s32[7,4]{1,0:T(8,128)S(1)}, s32[7,4]{1,0:T(8,128)}, u32[]{:S(2)}) copy-start(s32[7,4]{1,0:T(8,128)} %constant.32.clone) | copy-start | bytes 340
  0.0 6.3 %copy-start.5 = (s32[7,4]{1,0:T(8,128)S(1)}, s32[7,4]{1,0:T(8,128)}, u32[]{:S(2)}) copy-start(s32[7,4]{1,0:T(8,128)} %constant.33.clone) | copy-start | bytes 340
  0.0 6.3 %copy-start.6 = (s32[7,4]{1,0:T(8,128)S(1)}, s32[7,4]{1,0:T(8,128)}, u32[]{:S(2)}) copy-start(s32[7,4]{1,0:T(8,128)} %constant.34.clone) | copy-start | bytes 340
  0.0 6.3 %copy-start = (f32[64,8192]{1,0:T(8,128)S(1)}, f32[64,8192]{1,0:T(8,128)}, u32[]{:S(2)}) copy-start(f32[64,8192]{1,0:T(8,128)} %refs_0_.1) | copy-start | bytes 6291460
  0.0 20.3 %collective-permute-start.4 = (f32[64,8192]{1,0:T(8,128)}, f32[64,8192]{1,0:T(8,128)}, u32[]{:S(2)}, u32[]{:S(2)}) collective-permute-start(f32[64,8192]{1,0:T(8,128)} %refs_0_.1), channel_id=1, source_target_pairs={{0,4},{4,0},{8,12},{12,8},{16,20},{20,16},{24,28},{28,24},{1,5},{5... | collective-permute-start | bytes 6291464 | tf_op jit(solution)/shard_map/ppermute | solution.py:172
  3.8 15.9 %collective-permute-start.1 = (f32[64,4096]{1,0:T(8,128)}, f32[64,4096]{1,0:T(8,128)S(1)}, u32[]{:S(2)}, u32[]{:S(2)}) collective-permute-start(f32[64,4096]{1,0:T(8,128)} %get-tuple-element.23), channel_id=1, source_target_pairs={{0,8},{4,20},{8,0},{12,28},{16,24},{20,4},{24,16},{28,12},{1,9},{5... | collective-permute-start | bytes 3145736 | tf_op jit(solution)/shard_map/ppermute | solution.py:172
  6.3 5.6 %copy-start.2 = (f32[16,4096]{1,0:T(8,128)S(1)}, f32[16,4096]{1,0:T(8,128)}, u32[]{:S(2)}) copy-start(f32[16,4096]{1,0:T(8,128)} %param.9) | copy-start | bytes 786436
  11.8 20.0 %collective-permute-start = (f32[64,4096]{1,0:T(8,128)}, f32[64,4096]{1,0:T(8,128)S(1)}, u32[]{:S(2)}, u32[]{:S(2)}) collective-permute-start(f32[64,4096]{1,0:T(8,128)} %get-tuple-element.20), channel_id=1, source_target_pairs={{0,8},{4,20},{8,0},{12,28},{16,24},{20,4},{24,16},{28,12},{1,9},{5... | collective-permute-start | bytes 3145736 | tf_op jit(solution)/shard_map/ppermute | solution.py:172
  14.3 1.7 %copy-start.3 = (f32[8,4096]{1,0:T(8,128)S(1)}, f32[8,4096]{1,0:T(8,128)}, u32[]{:S(2)}) copy-start(f32[8,4096]{1,0:T(8,128)} %param.10) | copy-start | bytes 393220
  19.7 12.7 %collective-permute-start.2 = (f32[64,2048]{1,0:T(8,128)S(1)}, f32[64,2048]{1,0:T(8,128)S(1)}, u32[]{:S(2)}, u32[]{:S(2)}) collective-permute-start(f32[64,2048]{1,0:T(8,128)S(1)} %get-tuple-element.42), channel_id=1, source_target_pairs={{0,4},{4,0},{8,12},{12,8},{16,20},{20,16},{24,28},{28,24},{1,5},{5... | collective-permute-start | bytes 1572872 | tf_op jit(solution)/shard_map/ppermute | solution.py:172
  19.9 12.5 %collective-permute-start.3 = (f32[64,2048]{1,0:T(8,128)S(1)}, f32[64,2048]{1,0:T(8,128)S(1)}, u32[]{:S(2)}, u32[]{:S(2)}) collective-permute-start(f32[64,2048]{1,0:T(8,128)S(1)} %get-tuple-element.41), channel_id=1, source_target_pairs={{0,4},{4,0},{8,12},{12,8},{16,20},{20,16},{24,28},{28,24},{1,5},{5... | collective-permute-start | bytes 1572872 | tf_op jit(solution)/shard_map/ppermute | solution.py:172
  25.9 19.9 %collective-permute-start.6 = (f32[64,4096]{1,0:T(8,128)}, f32[64,4096]{1,0:T(8,128)S(1)}, u32[]{:S(2)}, u32[]{:S(2)}) collective-permute-start(f32[64,4096]{1,0:T(8,128)} %get-tuple-element.23), channel_id=1, source_target_pairs={{0,16},{4,12},{8,24},{12,4},{16,0},{20,28},{24,8},{28,20},{1,17},{... | collective-permute-start | bytes 3145736 | tf_op jit(solution)/shard_map/ppermute | solution.py:172
  31.9 8.4 %collective-permute-start.10 = (f32[64,2048]{1,0:T(8,128)S(1)}, f32[64,2048]{1,0:T(8,128)S(1)}, u32[]{:S(2)}, u32[]{:S(2)}) collective-permute-start(f32[64,2048]{1,0:T(8,128)S(1)} %get-tuple-element.37), channel_id=1, source_target_pairs={{0,4},{4,0},{8,12},{12,8},{16,20},{20,16},{24,28},{28,24},{1,5},{5... | collective-permute-start | bytes 1572872 | tf_op jit(solution)/shard_map/ppermute | solution.py:172
  31.9 8.4 %collective-permute-start.9 = (f32[64,2048]{1,0:T(8,128)S(1)}, f32[64,2048]{1,0:T(8,128)S(1)}, u32[]{:S(2)}, u32[]{:S(2)}) collective-permute-start(f32[64,2048]{1,0:T(8,128)S(1)} %get-tuple-element.38), channel_id=1, source_target_pairs={{0,4},{4,0},{8,12},{12,8},{16,20},{20,16},{24,28},{28,24},{1,5},{5... | collective-permute-start | bytes 1572872 | tf_op jit(solution)/shard_map/ppermute | solution.py:172
  37.9 15.4 %collective-permute-start.5 = (f32[64,4096]{1,0:T(8,128)}, f32[64,4096]{1,0:T(8,128)S(1)}, u32[]{:S(2)}, u32[]{:S(2)}) collective-permute-start(f32[64,4096]{1,0:T(8,128)} %get-tuple-element.20), channel_id=1, source_target_pairs={{0,16},{4,12},{8,24},{12,4},{16,0},{20,28},{24,8},{28,20},{1,17},{... | collective-permute-start | bytes 3145736 | tf_op jit(solution)/shard_map/ppermute | solution.py:172
  45.9 8.1 %collective-permute-start.7 = (f32[64,2048]{1,0:T(8,128)S(1)}, f32[64,2048]{1,0:T(8,128)S(1)}, u32[]{:S(2)}, u32[]{:S(2)}) collective-permute-start(f32[64,2048]{1,0:T(8,128)S(1)} %get-tuple-element.40), channel_id=1, source_target_pairs={{0,4},{4,0},{8,12},{12,8},{16,20},{20,16},{24,28},{28,24},{1,5},{5... | collective-permute-start | bytes 1572872 | tf_op jit(solution)/shard_map/ppermute | solution.py:172
  46.0 8.0 %collective-permute-start.8 = (f32[64,2048]{1,0:T(8,128)S(1)}, f32[64,2048]{1,0:T(8,128)S(1)}, u32[]{:S(2)}, u32[]{:S(2)}) collective-permute-start(f32[64,2048]{1,0:T(8,128)S(1)} %get-tuple-element.39), channel_id=1, source_target_pairs={{0,4},{4,0},{8,12},{12,8},{16,20},{20,16},{24,28},{28,24},{1,5},{5... | collective-permute-start | bytes 1572872 | tf_op jit(solution)/shard_map/ppermute | solution.py:172
  46.5 20.5 %collective-permute-start.12 = (f32[64,4096]{1,0:T(8,128)S(1)}, f32[64,4096]{1,0:T(8,128)S(1)}, u32[]{:S(2)}, u32[]{:S(2)}) collective-permute-start(f32[64,4096]{1,0:T(8,128)S(1)} %collective-permute-done.1.refs_0_), channel_id=1, source_target_pairs={{0,16},{4,12},{8,24},{12,4},{16,0},{20,28},{24,8},{28,20},{1,17},{... | collective-permute-start | bytes 3145736 | tf_op jit(solution)/shard_map/ppermute | solution.py:172
  53.4 8.2 %collective-permute-start.13 = (f32[64,2048]{1,0:T(8,128)S(1)}, f32[64,2048]{1,0:T(8,128)S(1)}, u32[]{:S(2)}, u32[]{:S(2)}) collective-permute-start(f32[64,2048]{1,0:T(8,128)S(1)} %get-tuple-element.36), channel_id=1, source_target_pairs={{0,4},{4,0},{8,12},{12,8},{16,20},{20,16},{24,28},{28,24},{1,5},{5... | collective-permute-start | bytes 1572872 | tf_op jit(solution)/shard_map/ppermute | solution.py:172
  53.5 8.1 %collective-permute-start.14 = (f32[64,2048]{1,0:T(8,128)S(1)}, f32[64,2048]{1,0:T(8,128)S(1)}, u32[]{:S(2)}, u32[]{:S(2)}) collective-permute-start(f32[64,2048]{1,0:T(8,128)S(1)} %get-tuple-element.35), channel_id=1, source_target_pairs={{0,4},{4,0},{8,12},{12,8},{16,20},{20,16},{24,28},{28,24},{1,5},{5... | collective-permute-start | bytes 1572872 | tf_op jit(solution)/shard_map/ppermute | solution.py:172
  59.4 16.3 %collective-permute-start.11 = (f32[64,4096]{1,0:T(8,128)S(1)}, f32[64,4096]{1,0:T(8,128)S(1)}, u32[]{:S(2)}, u32[]{:S(2)}) collective-permute-start(f32[64,4096]{1,0:T(8,128)S(1)} %collective-permute-done.refs_0_), channel_id=1, source_target_pairs={{0,16},{4,12},{8,24},{12,4},{16,0},{20,28},{24,8},{28,20},{1,17},{... | collective-permute-start | bytes 3145736 | tf_op jit(solution)/shard_map/ppermute | solution.py:172
  67.1 2.0 %collective-permute-start.15 = (f32[64,2048]{1,0:T(8,128)S(1)}, f32[64,2048]{1,0:T(8,128)S(1)}, u32[]{:S(2)}, u32[]{:S(2)}) collective-permute-start(f32[64,2048]{1,0:T(8,128)S(1)} %get-tuple-element.34), channel_id=1, source_target_pairs={{0,4},{4,0},{8,12},{12,8},{16,20},{20,16},{24,28},{28,24},{1,5},{5... | collective-permute-start | bytes 1572872 | tf_op jit(solution)/shard_map/ppermute | solution.py:172
  67.2 2.6 %collective-permute-start.16 = (f32[64,2048]{1,0:T(8,128)S(1)}, f32[64,2048]{1,0:T(8,128)S(1)}, u32[]{:S(2)}, u32[]{:S(2)}) collective-permute-start(f32[64,2048]{1,0:T(8,128)S(1)} %get-tuple-element.33), channel_id=1, source_target_pairs={{0,4},{4,0},{8,12},{12,8},{16,20},{20,16},{24,28},{28,24},{1,5},{5... | collective-permute-start | bytes 1572872 | tf_op jit(solution)/shard_map/ppermute | solution.py:172
  75.9 4.4 %collective-permute-start.17 = (f32[64,2048]{1,0:T(8,128)S(1)}, f32[64,2048]{1,0:T(8,128)S(1)}, u32[]{:S(2)}, u32[]{:S(2)}) collective-permute-start(f32[64,2048]{1,0:T(8,128)S(1)} %get-tuple-element.32), channel_id=1, source_target_pairs={{0,4},{4,0},{8,12},{12,8},{16,20},{20,16},{24,28},{28,24},{1,5},{5... | collective-permute-start | bytes 1572872 | tf_op jit(solution)/shard_map/ppermute | solution.py:172
  75.9 4.3 %collective-permute-start.18 = (f32[64,2048]{1,0:T(8,128)S(1)}, f32[64,2048]{1,0:T(8,128)S(1)}, u32[]{:S(2)}, u32[]{:S(2)}) collective-permute-start(f32[64,2048]{1,0:T(8,128)S(1)} %get-tuple-element.31), channel_id=1, source_target_pairs={{0,4},{4,0},{8,12},{12,8},{16,20},{20,16},{24,28},{28,24},{1,5},{5... | collective-permute-start | bytes 1572872 | tf_op jit(solution)/shard_map/ppermute | solution.py:172
  80.2 24.1 %copy-start.1 = (bf16[64,8192]{1,0:T(8,128)(2,1)S(1)}, bf16[64,8192]{1,0:T(8,128)(2,1)}, u32[]{:S(2)}) copy-start(bf16[64,8192]{1,0:T(8,128)(2,1)} %pad_maximum_fusion.1.third) | copy-start | bytes 3145732
  84.4 4.5 %collective-permute-start.19 = (f32[64,256]{1,0:T(8,128)S(1)}, f32[64,256]{1,0:T(8,128)S(1)}, u32[]{:S(2)}, u32[]{:S(2)}) collective-permute-start(f32[64,256]{1,0:T(8,128)S(1)} %shard_map.81), channel_id=1, source_target_pairs={{0,1},{1,0},{2,3},{3,2},{4,5},{5,4},{6,7},{7,6},{8,9},{9,8},{10,11... | collective-permute-start | bytes 196616 | tf_op jit(solution)/shard_map/ppermute | solution.py:172
  88.9 5.3 %collective-permute-start.20 = (f32[64,256]{1,0:T(8,128)S(1)}, f32[64,256]{1,0:T(8,128)S(1)}, u32[]{:S(2)}, u32[]{:S(2)}) collective-permute-start(f32[64,256]{1,0:T(8,128)S(1)} %add.23), channel_id=1, source_target_pairs={{0,2},{1,3},{2,0},{3,1},{4,6},{5,7},{6,4},{7,5},{8,10},{9,11},{10,... | collective-permute-start | bytes 196616 | tf_op jit(solution)/shard_map/ppermute | solution.py:172

commit v3 on v2

--- a/solution.py
+++ b/solution.py
@@ -10,6 +10,8 @@
 from jax.sharding import PartitionSpec as P
 
 LANES = 128
+FETCH_LAG = 1
+LIMIT = 24
 STEP = 2048
 TWIN_CUTS = 2
 TRANSPOSED = (((1,), (1,)), ((), ()))
@@ -25,16 +27,25 @@
     return lax.dot_general(a, b, dims, preferred_element_type=jnp.float32)
 
 
-def project_kernel(places, block_width, row, last, table, amp, *refs):
+def project_kernel(places, block_width, row, fetch, table, amp, *refs):
     count = 1 + max(place[0] for place in places)
     blocks, start, out = refs[:count], refs[count], refs[count + 1]
-    amp_slots, block_slots, both, total, amp_sems, block_sems = refs[count + 2 :]
+    refs = refs[count + 2 :]
+    if fetch is not None:
+        fetched, refs = refs[0], refs[1:]
+    amp_slots, block_slots, both, total, amp_sems, block_sems, fetch_sem = refs
     steps, bond_dim, unit = block_slots.shape
     for step, (which, position, column, offset) in enumerate(places):
         here = pl.ds(pl.multiple_of(table[row, column] * block_width + offset, LANES), unit)
         pltpu.make_async_copy(amp.at[:, :, here], amp_slots.at[step], amp_sems.at[step]).start()
         there = pl.ds(position, unit)
         pltpu.make_async_copy(blocks[which].at[:, there], block_slots.at[step], block_sems.at[step]).start()
+    if fetch is not None:
+        fetches = []
+        for index in range(fetched.shape[0]):
+            here = pl.ds(pl.multiple_of(table[fetch, index] * block_width, LANES), block_width)
+            fetches.append(pltpu.make_async_copy(amp.at[:, :, here], fetched.at[index], fetch_sem.at[index]))
+            fetches[-1].start()
     total[...] = start[...]
 
     def body(step, carry):
@@ -53,13 +64,13 @@
         return carry
 
     lax.fori_loop(0, steps, body, 0)
-    if last:
-        out[...] = (total[:, :bond_dim] + total[:, bond_dim:]).T
-    else:
-        out[...] = total[...]
-
-
-def project(table, row, column, amplitudes, blocks, unit, start, last=False):
+    out[...] = total[...]
+    if fetch is not None:
+        for copy in fetches:
+            copy.wait()
+
+
+def project(table, row, column, amplitudes, blocks, unit, start, fetch=None):
     step = functools.reduce(math.gcd, [block.shape[1] for block in blocks], unit)
     step = STEP if step % STEP == 0 else step
     parts, rows, _ = amplitudes.shape
@@ -71,15 +82,17 @@
             places.append((which, position, offset // unit, offset % unit))
             offset += step
     steps = len(places)
-    shape = (bond_dim, parts * rows) if last else start.shape
+    shapes = [jax.ShapeDtypeStruct(start.shape, jnp.float32)]
+    if fetch is not None:
+        shapes.append(pltpu.VMEM((2, parts, rows, unit), jnp.float32))
     vmem = pl.BlockSpec(memory_space=pltpu.VMEM)
     anywhere = pl.BlockSpec(memory_space=pl.ANY)
     scratch = 4 * steps * step * (parts * rows + bond_dim)
-    return pl.pallas_call(
-        functools.partial(project_kernel, places, unit, row, last),
+    result = pl.pallas_call(
+        functools.partial(project_kernel, places, unit, row, fetch),
         in_specs=[pl.BlockSpec(memory_space=pltpu.SMEM), anywhere] + [anywhere] * len(blocks) + [vmem],
-        out_specs=vmem,
-        out_shape=jax.ShapeDtypeStruct(shape, jnp.float32),
+        out_specs=[vmem] * len(shapes),
+        out_shape=shapes,
         scratch_shapes=[
             pltpu.VMEM((steps, parts, rows, step), jnp.float32),
             pltpu.VMEM((steps, bond_dim, step), jnp.float32),
@@ -87,6 +100,7 @@
             pltpu.VMEM(start.shape, jnp.float32),
             pltpu.SemaphoreType.DMA((steps,)),
             pltpu.SemaphoreType.DMA((steps,)),
+            pltpu.SemaphoreType.DMA((2,)),
         ],
         compiler_params=pltpu.CompilerParams(vmem_limit_bytes=scratch + 10 * 2**20),
         cost_estimate=pl.CostEstimate(
@@ -95,6 +109,70 @@
             transcendentals=0,
         ),
     )(table, amplitudes, *blocks, start)
+    return result[0] if fetch is None else result
+
+
+def fetch_kernel(row, table, amp, token, fetched, sems):
+    unit = fetched.shape[-1]
+    copies = []
+    for index in range(fetched.shape[0]):
+        here = pl.ds(pl.multiple_of(table[row, index] * unit, LANES), unit)
+        copies.append(pltpu.make_async_copy(amp.at[:, :, here], fetched.at[index], sems.at[index]))
+        copies[-1].start()
+    for copy in copies:
+        copy.wait()
+
+
+def fetch_columns(table, row, amplitudes, unit, token):
+    parts, rows, _ = amplitudes.shape
+    return pl.pallas_call(
+        functools.partial(fetch_kernel, row),
+        in_specs=[pl.BlockSpec(memory_space=pltpu.SMEM)] + [pl.BlockSpec(memory_space=pl.ANY)] * 2,
+        out_specs=pl.BlockSpec(memory_space=pltpu.VMEM),
+        out_shape=pltpu.VMEM((2, parts, rows, unit), jnp.float32),
+        scratch_shapes=[pltpu.SemaphoreType.DMA((2,))],
+        compiler_params=pltpu.CompilerParams(vmem_limit_bytes=16 * 2**20),
+    )(table, amplitudes, token)
+
+
+def project_fetched_kernel(which, step, last, fetched, *refs):
+    blocks, start, out = refs[:-2], refs[-2], refs[-1]
+    bond_dim = blocks[0].shape[0]
+    total = start[...]
+    offset = 0
+    for block in blocks:
+        for position in range(0, block.shape[1], step):
+            hi, lo = split_bf16(block[:, position : position + step])
+            weights = jnp.concatenate([hi, lo], 0)
+            amp = fetched[which, :, :, offset : offset + step]
+            hi, lo = split_bf16(amp.reshape(-1, step))
+            total += dot(hi, weights, TRANSPOSED) + dot(lo, weights, TRANSPOSED)
+            offset += step
+    if last:
+        out[...] = (total[:, :bond_dim] + total[:, bond_dim:]).T
+    else:
+        out[...] = total
+
+
+def project_fetched(fetched, which, blocks, start, last=False):
+    _, parts, rows, unit = fetched.shape
+    bond_dim = blocks[0].shape[0]
+    step = functools.reduce(math.gcd, [block.shape[1] for block in blocks], unit)
+    step = STEP if step % STEP == 0 else step
+    vmem = pl.BlockSpec(memory_space=pltpu.VMEM)
+    shape = (bond_dim, parts * rows) if last else start.shape
+    return pl.pallas_call(
+        functools.partial(project_fetched_kernel, which, step, last),
+        in_specs=[vmem] * (len(blocks) + 2),
+        out_specs=vmem,
+        out_shape=jax.ShapeDtypeStruct(shape, jnp.float32),
+        compiler_params=pltpu.CompilerParams(vmem_limit_bytes=LIMIT * 2**20),
+        cost_estimate=pl.CostEstimate(
+            flops=8 * unit * bond_dim * parts * rows,
+            bytes_accessed=4 * unit * (parts * rows + bond_dim),
+            transcendentals=0,
+        ),
+    )(fetched, *blocks, start)
 
 
 def coarsen_kernel(rows_q, slab, first_hi, first_lo, third, out, paired):
@@ -207,8 +285,8 @@
     arrays = {block: vectors[:, block[2] * unit : (block[2] + 1) * unit] for block in held[:halves]}
     total = jnp.zeros((amplitudes.shape[0] * amplitudes.shape[1], 2 * bond_dim), jnp.float32)
     add = functools.partial(project, table)
-    arrived = []
-    totals = [total]
+    arrived, fetched = [], []
+    totals = [after(total, *arrays.values())]
     products = [lambda total: add(0, 0, amplitudes, [vectors], unit, total)]
 
     def products_done(count):
@@ -218,7 +296,7 @@
 
     for number, (masks, sent, block) in enumerate(rounds):
         array = arrays[sent]
-        if number >= 2:
+        if number >= 2 and number != 3:
             array = after(array, arrived[number - 2])
         if number == 3:
             array = after(array, *weights)
@@ -237,14 +315,17 @@
         for cut in range(cuts):
             some = mine[:, cut * unit // cuts : (cut + 1) * unit // cuts] if cuts > 1 else mine
             pair.append(swap(some, "bond", size, twin))
-        products.append(
-            lambda total, number=number, pair=pair: add(number + 1, 0, amplitudes, pair, unit, total)
-        )
+
+        def product(total, number=number, pair=pair):
+            if number == len(rounds) - 2:
+                fetched.append(fetch_columns(table, len(rounds), amplitudes, unit, totals[len(rounds) - 1]))
+                total = after(total, fetched[0])
+            return add(number + 1, 0, amplitudes, pair, unit, total)
+
+        products.append(product)
     total = products_done(len(rounds) + 1)
-    if rounds:
-        total = add(len(rounds), 0, amplitudes, pair[:1], unit, total)
-        total = add(len(rounds), 1, amplitudes, pair[1:], unit, total, last=True)
-    return total
+    total = project_fetched(fetched[0], 0, pair[:1], total)
+    return project_fetched(fetched[0], 1, pair[1:], total, last=True)
 
 
 def local(bond, leg, amplitudes, vectors, row_map, col_map):

time: 109 us -> 106 us (0.972)
  waiting for transfers between devices: 16.9 us -> 15.8 us
    ppermute x21, waiting for transfers between devices: 16.9 us -> 15.8 us  [swap(): return lax.ppermute(x, axis, [(i, partner(i)) for i in range(size)])]
    pallas_call x9 -> x10, Pallas kernels: 46.3 us -> 45.4 us  [the longest x7 38.7 us: project(): pl.pallas_call(functools.partial(project_kernel, places, unit, row, fetch...]
  transfers between devices with their start and end apart: 21 -> 21, of which waited for: 7 -> 6; matrix products, arithmetic and copies ran while one was open for 10% -> 11% of each run, Pallas kernels for 39% -> 42%
where the time goes in v3:
time: 106 us
  Pallas kernels  49.9 us (47%)
  starting transfers between devices  18.3 us (17%)
  waiting for transfers between devices  15.8 us (15%)
  blocking collectives  9.85 us (9%)
  local copies, waits for them, and re-layouts  7.25 us (7%)
  other arithmetic  4.27 us (4%)
    pallas_call x7, Pallas kernels, project(): pl.pallas_call(functools.partial(project_kernel, places, unit, row, fetch...  38.7 us
    ppermute x21, starting transfers between devices, swap(): return lax.ppermute(x, axis, [(i, partner(i)) for i in range(size)])  18.3 us
    ppermute x21, waiting for transfers between devices, swap(): return lax.ppermute(x, axis, [(i, partner(i)) for i in range(size)])  15.8 us
    all_gather x1, blocking collectives, local(): slab = lax.all_gather(total, 'bond', axis=0)  9.85 us
    pallas_call x1, Pallas kernels, coarsen(): pl.pallas_call(functools.partial(coarsen_kernel, rows_q), in_specs=[pl.Bl...  4.45 us
    pallas_call x1, Pallas kernels, fetch_columns(): pl.pallas_call(functools.partial(fetch_kernel, row), in_specs=[pl.BlockSp...  4.08 us
    slice x1, local copies, waits for them, and re-layouts, gather_and_project(): vectors[:, block[2] * unit:(block[2] + 1) * unit]  3.22 us
    pallas_call x2, Pallas kernels, project_fetched(): pl.pallas_call(functools.partial(project_fetched_kernel, which, step, las...  2.69 us
  transfers between devices with their start and end apart: 21, of which 6 were waited for; matrix products, arithmetic and copies ran while one was open for 11% of the time, Pallas kernels for 42%

profile of v3, /device:TPU:0, one launch (start us, length us, event | category | flops | bytes accessed | tf_op | source)
XLA Modules:
  0.0 105.6 jit_solution(16188942086744060891)
XLA Ops:
  0.0 0.5 collective-permute-start.1
  0.5 3.2 %fusion.2 = (f32[64,4096]{1,0:T(8,128)}, f32[64,4096]{1,0:T(8,128)}) fusion(f32[64,8192]{1,0:T(8,128)} %refs_0_.1), kind=kLoop, calls=%fused_computation.12 | loop fusion | bytes 4194304 | tf_op jit(solution)/shard_map/slice | solution.py:285
  3.8 2.5 %collective-permute-start = (f32[64,4096]{1,0:T(8,128)}, f32[64,4096]{1,0:T(8,128)S(1)}, u32[]{:S(2)}, u32[]{:S(2)}) collective-permute-start(f32[64,4096]{1,0:T(8,128)} %get-tuple-element.20), channel_id=1, source_target_pairs={{0,8},{4,20},{8,0},{12,28},{16,24},{20,4},{24,16},{28,12},{1,9},{5... | collective-permute-start | bytes 3145736 | tf_op jit(solution)/shard_map/ppermute | solution.py:250
  6.3 0.0 copy-start.2
  6.3 5.5 %shard_map.73.refs_1_ = f32[256,128]{1,0:T(8,128)S(1)} custom-call(s32[7,4]{1,0:T(8,128)S(1)} %multiply_add_fusion.table, f32[2,128,65536]{2,1,0:T(8,128)} %amp.15, f32[64,8192]{1,0:T(8,128)S(1)} %copy-done, f32[256,128]{1,0:T(8,128)S(1)} %broadcast_in_dim.7.refs_1_), custom_call_target="tpu_custom_call" | custom-call | flops 1073741824 | bytes 10485760 | tf_op jit(solution)/shard_map/pallas_call | solution.py:91
  11.8 0.1 collective-permute-start.5
  11.9 1.0 reshape.21
  12.9 1.4 %select_maximum_fusion = f32[32,64,128]{2,1,0:T(8,128)S(1)} fusion(f32[16,64,64]{2,1,0:T(8,128)} %reshape.21), kind=kLoop, calls=%fused_computation.6 | loop fusion | flops 1310720 | bytes 1310720 | tf_op jit(solution)/shard_map/concatenate | solution.py:244
  14.4 0.0 copy-start.3
  14.4 0.6 reduce-precision_convert_fusion
  15.0 1.1 %pad_maximum_fusion.1.third = bf16[64,8192]{1,0:T(8,128)(2,1)} fusion(bf16[32,8192]{1,0:T(8,128)(2,1)S(1)} %get-tuple-element.40, bf16[32,8192]{1,0:T(8,128)(2,1)S(1)} %get-tuple-element.39), kind=kLoop, calls=%fused_computation.10 | loop fusion | flops 2097152 | bytes 2097152 | tf_op jit(solution)/shard_map/concatenate | solution.py:246
  16.1 0.1 reshape.18
  16.2 0.2 copy.8
  16.4 0.5 fusion.9
  16.9 0.5 reshape.19
  17.3 1.2 %reshape.20 = f32[64,1024]{1,0:T(8,128)} reshape(f32[64,8,2,64]{3,2,1,0:T(2,128)S(1)} %get-tuple-element.50) | data formatting | bytes 524288 | tf_op jit(solution)/shard_map/reshape | solution.py:239
  18.5 1.1 %fusion = (bf16[256,1024]{1,0:T(8,128)(2,1)S(1)}, bf16[256,1024]{1,0:T(8,128)(2,1)S(1)}) fusion(f32[64,1024]{1,0:T(8,128)S(1)} %broadcast_in_dim.8, f32[64,1024]{1,0:T(8,128)} %reshape.20, f32[64,1024]{1,0:T(8,128)S(1)} %reshape.19), kind=kLoop, calls=%fused_computation.4 | loop fusion | flops 1835008 | bytes 1835008 | tf_op jit(solution)/shard_map/convert_element_type | solution.py:231
  19.6 0.0 collective-permute-done.refs_0_
  19.7 0.1 fusion.6
  19.7 0.2 collective-permute-start.9
  19.9 0.4 collective-permute-start.8
  20.3 5.6 %shard_map.74.refs_3_ = f32[256,128]{1,0:T(8,128)S(1)} custom-call(s32[7,4]{1,0:T(8,128)S(1)} %multiply_add_fusion.table, f32[2,128,65536]{2,1,0:T(8,128)} %amp.15, f32[64,8192]{1,0:T(8,128)} %collective-permute-done.1.refs_0_, f32[256,128]{1,0:T(8,128)S(1)} %shard_map.73.refs_1_), custom_call_target="tpu_custom_call" | custom-call | flops 1073741824 | bytes 10485760 | tf_op jit(solution)/shard_map/pallas_call | solution.py:91
  26.0 2.1 %collective-permute-start.2 = (f32[64,4096]{1,0:T(8,128)}, f32[64,4096]{1,0:T(8,128)S(1)}, u32[]{:S(2)}, u32[]{:S(2)}) collective-permute-start(f32[64,4096]{1,0:T(8,128)} %get-tuple-element.20), channel_id=1, source_target_pairs={{0,16},{4,12},{8,24},{12,4},{16,0},{20,28},{24,8},{28,20},{1,17},{... | collective-permute-start | bytes 3145736 | tf_op jit(solution)/shard_map/ppermute | solution.py:250
  28.1 3.7 %collective-permute-done.5.refs_0_ = f32[64,4096]{1,0:T(8,128)S(1)} collective-permute-done((f32[64,4096]{1,0:T(8,128)}, f32[64,4096]{1,0:T(8,128)S(1)}, u32[]{:S(2)}, u32[]{:S(2)}) %collective-permute-start.5) | collective-permute-done | bytes 1048608 | tf_op jit(solution)/shard_map/ppermute | solution.py:250
  31.7 0.1 fusion.7
  31.8 0.1 collective-permute-start.7
  31.9 0.5 collective-permute-start.6
  32.4 5.5 %shard_map.75.refs_3_ = f32[256,128]{1,0:T(8,128)S(1)} custom-call(s32[7,4]{1,0:T(8,128)S(1)} %multiply_add_fusion.table, f32[2,128,65536]{2,1,0:T(8,128)} %amp.15, f32[64,4096]{1,0:T(8,128)S(1)} %collective-permute-done.refs_0_, f32[64,2048]{1,0:T(8,128)S(1)} %collective-permute-done.8.refs_1_, f32[64,2048]{1,0:T(8,128)S(1)} %collective-permute-done.9.refs_2_, ...), custom_call_target="tpu_custom_call" | custom-call | flops 1073741824 | bytes 10485760 | tf_op jit(solution)/shard_map/pallas_call | solution.py:91
  37.9 2.4 %collective-permute-start.10 = (f32[64,4096]{1,0:T(8,128)}, f32[64,4096]{1,0:T(8,128)S(1)}, u32[]{:S(2)}, u32[]{:S(2)}) collective-permute-start(f32[64,4096]{1,0:T(8,128)} %get-tuple-element.23), channel_id=1, source_target_pairs={{0,16},{4,12},{8,24},{12,4},{16,0},{20,28},{24,8},{28,20},{1,17},{... | collective-permute-start | bytes 3145736 | tf_op jit(solution)/shard_map/ppermute | solution.py:250
  40.3 0.0 collective-permute-done.7.refs_2_
  40.3 0.0 collective-permute-done.6.refs_1_
  40.3 5.5 %shard_map.76.refs_3_ = f32[256,128]{1,0:T(8,128)S(1)} custom-call(s32[7,4]{1,0:T(8,128)S(1)} %multiply_add_fusion.table, f32[2,128,65536]{2,1,0:T(8,128)} %amp.15, f32[64,4096]{1,0:T(8,128)S(1)} %collective-permute-done.5.refs_0_, f32[64,2048]{1,0:T(8,128)S(1)} %collective-permute-done.6.refs_1_, f32[64,2048]{1,0:T(8,128)S(1)} %collective-permute-done.7.refs_2_, ...), custom_call_target="tpu_custom_call" | custom-call | flops 1073741824 | bytes 10485760 | tf_op jit(solution)/shard_map/pallas_call | solution.py:91
  45.8 0.0 collective-permute-done.2.refs_0_
  45.8 0.1 fusion.8
  45.9 0.1 collective-permute-start.4
  46.0 0.5 collective-permute-start.3
  46.5 0.8 collective-permute-start.12
  47.3 5.9 %collective-permute-done.10.refs_0_ = f32[64,4096]{1,0:T(8,128)S(1)} collective-permute-done((f32[64,4096]{1,0:T(8,128)}, f32[64,4096]{1,0:T(8,128)S(1)}, u32[]{:S(2)}, u32[]{:S(2)}) %collective-permute-start.10) | collective-permute-done | bytes 1048608 | tf_op jit(solution)/shard_map/ppermute | solution.py:250
  53.3 0.1 fusion.5
  53.4 0.1 collective-permute-start.14
  53.4 0.5 collective-permute-start.13
  53.9 0.0 collective-permute-done.4.refs_2_
  53.9 0.0 collective-permute-done.3.refs_1_
  53.9 5.5 %shard_map.77.token.refs_3_ = f32[256,128]{1,0:T(8,128)S(1)} custom-call(s32[7,4]{1,0:T(8,128)S(1)} %multiply_add_fusion.table, f32[2,128,65536]{2,1,0:T(8,128)} %amp.15, f32[64,4096]{1,0:T(8,128)S(1)} %collective-permute-done.2.refs_0_, f32[64,2048]{1,0:T(8,128)S(1)} %collective-permute-done.3.refs_1_, f32[64,2048]{1,0:T(8,128)S(1)} %collective-permute-done.4.refs_2_, ...), custom_call_target="tpu_custom_call" | custom-call | flops 1073741824 | bytes 10485760 | tf_op jit(solution)/shard_map/pallas_call | solution.py:91
  59.4 2.1 %collective-permute-start.11 = (f32[64,4096]{1,0:T(8,128)S(1)}, f32[64,4096]{1,0:T(8,128)S(1)}, u32[]{:S(2)}, u32[]{:S(2)}) collective-permute-start(f32[64,4096]{1,0:T(8,128)S(1)} %collective-permute-done.5.refs_0_), channel_id=1, source_target_pairs={{0,16},{4,12},{8,24},{12,4},{16,0},{20,28},{24,8},{28,20},{1,17},{... | collective-permute-start | bytes 3145736 | tf_op jit(solution)/shard_map/ppermute | solution.py:250
  61.5 5.5 %shard_map.79.refs_3_ = f32[256,128]{1,0:T(8,128)S(1)} custom-call(s32[7,4]{1,0:T(8,128)S(1)} %multiply_add_fusion.table, f32[2,128,65536]{2,1,0:T(8,128)} %amp.15, f32[64,4096]{1,0:T(8,128)S(1)} %collective-permute-done.10.refs_0_, f32[64,2048]{1,0:T(8,128)S(1)} %collective-permute-done.13.refs_1_, f32[64,2048]{1,0:T(8,128)S(1)} %collective-permute-done.14.refs_2_, ...), custom_call_target="tpu_custom_call" | custom-call | flops 1073741824 | bytes 10485760 | tf_op jit(solution)/shard_map/pallas_call | solution.py:91
  67.0 0.1 fusion.4
  67.1 0.1 collective-permute-start.16
  67.2 0.5 collective-permute-start.15
  67.7 4.1 %shard_map.78.fetched = f32[2,2,128,4096]{3,2,1,0:T(8,128)S(1)} custom-call(s32[7,4]{1,0:T(8,128)S(1)} %multiply_add_fusion.table, f32[2,128,65536]{2,1,0:T(8,128)} %amp.15, f32[256,128]{1,0:T(8,128)S(1)} %shard_map.77.token.refs_3_), custom_call_target="tpu_custom_call" | custom-call | tf_op jit(solution)/shard_map/pallas_call | solution.py:128
  71.8 5.6 %shard_map.80.refs_1_ = f32[256,128]{1,0:T(8,128)S(1)} custom-call(s32[7,4]{1,0:T(8,128)S(1)} %multiply_add_fusion.table, f32[2,128,65536]{2,1,0:T(8,128)} %amp.15, f32[64,4096]{1,0:T(8,128)S(1)} %collective-permute-done.12.refs_0_, f32[64,2048]{1,0:T(8,128)S(1)} %collective-permute-done.15.refs_1_, f32[64,2048]{1,0:T(8,128)S(1)} %collective-permute-done.16.refs_2_, ...), custom_call_target="tpu_custom_call" | custom-call | flops 1073741824 | bytes 10485760 | tf_op jit(solution)/shard_map/pallas_call | solution.py:91
  77.5 0.1 fusion.3
  77.6 0.2 collective-permute-start.18
  77.7 0.4 collective-permute-start.17
  78.2 1.3 %shard_map.81.refs_2_ = f32[256,128]{1,0:T(8,128)S(1)} custom-call(f32[2,2,128,4096]{3,2,1,0:T(8,128)S(1)} %shard_map.78.fetched, f32[64,4096]{1,0:T(8,128)S(1)} %collective-permute-done.11.refs_0_, f32[256,128]{1,0:T(8,128)S(1)} %shard_map.80.refs_1_), custom_call_target="tpu_custom_call" | custom-call | flops 536870912 | bytes 5242880 | tf_op jit(solution)/shard_map/pallas_call | solution.py:164
  79.5 0.1 collective-permute-done.18.refs_1_
  79.6 0.7 collective-permute-done.17.refs_0_
  80.3 1.4 %shard_map.82 = f32[64,256]{1,0:T(8,128)S(1)} custom-call(f32[2,2,128,4096]{3,2,1,0:T(8,128)S(1)} %shard_map.78.fetched, f32[64,2048]{1,0:T(8,128)S(1)} %collective-permute-done.17.refs_0_, f32[64,2048]{1,0:T(8,128)S(1)} %collective-permute-done.18.refs_1_, f32[256,128]{1,0:T(8,128)S(1)} %shard_map.81.refs_2_), custom_call_target="tpu_custom_call" | custom-call | flops 536870912 | bytes 5242880 | tf_op jit(solution)/shard_map/pallas_call | solution.py:164
  81.7 1.6 %collective-permute-start.19 = (f32[64,256]{1,0:T(8,128)S(1)}, f32[64,256]{1,0:T(8,128)S(1)}, u32[]{:S(2)}, u32[]{:S(2)}) collective-permute-start(f32[64,256]{1,0:T(8,128)S(1)} %shard_map.82), channel_id=1, source_target_pairs={{0,1},{1,0},{2,3},{3,2},{4,5},{5,4},{6,7},{7,6},{8,9},{9,8},{10,11... | collective-permute-start | bytes 196616 | tf_op jit(solution)/shard_map/ppermute | solution.py:250
  83.4 2.7 %collective-permute-done.19 = f32[64,256]{1,0:T(8,128)S(1)} collective-permute-done((f32[64,256]{1,0:T(8,128)S(1)}, f32[64,256]{1,0:T(8,128)S(1)}, u32[]{:S(2)}, u32[]{:S(2)}) %collective-permute-start.19) | collective-permute-done | bytes 65568 | tf_op jit(solution)/shard_map/ppermute | solution.py:250
  86.1 2.6 %collective-permute-start.20 = (f32[64,256]{1,0:T(8,128)S(1)}, f32[64,256]{1,0:T(8,128)S(1)}, u32[]{:S(2)}, u32[]{:S(2)}) collective-permute-start(f32[64,256]{1,0:T(8,128)S(1)} %add.23), channel_id=1, source_target_pairs={{0,2},{1,3},{2,0},{3,1},{4,6},{5,7},{6,4},{7,5},{8,10},{9,11},{10,... | collective-permute-start | bytes 196616 | tf_op jit(solution)/shard_map/ppermute | solution.py:250
  88.7 2.6 %collective-permute-done.20 = f32[64,256]{1,0:T(8,128)S(1)} collective-permute-done((f32[64,256]{1,0:T(8,128)S(1)}, f32[64,256]{1,0:T(8,128)S(1)}, u32[]{:S(2)}, u32[]{:S(2)}) %collective-permute-start.20) | collective-permute-done | bytes 65568 | tf_op jit(solution)/shard_map/ppermute | solution.py:250
  91.3 9.8 %all-gather = f32[512,256]{1,0:T(8,128)S(1)} all-gather(f32[64,256]{1,0:T(8,128)S(1)} %add.24), channel_id=2, replica_groups=mesh['bond'=8,'leg'=4] {'bond'}, dimensions={0}, use_global_device_ids=true | all-gather | bytes 589824 | tf_op jit(solution)/shard_map/all_gather | solution.py:340
  101.1 4.4 %shard_map.83 = f32[2,64,16]{2,1,0:T(8,128)} custom-call(f32[8,64,256]{2,1,0:T(8,128)S(1)} %bitcast.11, bf16[256,1024]{1,0:T(8,128)(2,1)S(1)} %get-tuple-element.48.first_hi, bf16[256,1024]{1,0:T(8,128)(2,1)S(1)} %get-tuple-element.47.first_lo, bf16[64,8192]{1,0:T(8,128)(2,1)S(1)} %copy-done.1), custom_call_target="tpu_custom_call" | custom-call | tf_op jit(solution)/shard_map/pallas_call | solution.py:218
  (26 shorter events, 0.1 us)
Async XLA Ops:
  0.0 6.3 %copy-start.4 = (s32[7,4]{1,0:T(8,128)S(1)}, s32[7,4]{1,0:T(8,128)}, u32[]{:S(2)}) copy-start(s32[7,4]{1,0:T(8,128)} %constant.34.clone) | copy-start | bytes 340
  0.0 6.3 %copy-start.5 = (s32[7,4]{1,0:T(8,128)S(1)}, s32[7,4]{1,0:T(8,128)}, u32[]{:S(2)}) copy-start(s32[7,4]{1,0:T(8,128)} %constant.33.clone) | copy-start | bytes 340
  0.0 6.3 %copy-start.6 = (s32[7,4]{1,0:T(8,128)S(1)}, s32[7,4]{1,0:T(8,128)}, u32[]{:S(2)}) copy-start(s32[7,4]{1,0:T(8,128)} %constant.32.clone) | copy-start | bytes 340
  0.0 6.3 %copy-start = (f32[64,8192]{1,0:T(8,128)S(1)}, f32[64,8192]{1,0:T(8,128)}, u32[]{:S(2)}) copy-start(f32[64,8192]{1,0:T(8,128)} %refs_0_.1) | copy-start | bytes 6291460
  0.0 20.3 %collective-permute-start.1 = (f32[64,8192]{1,0:T(8,128)}, f32[64,8192]{1,0:T(8,128)}, u32[]{:S(2)}, u32[]{:S(2)}) collective-permute-start(f32[64,8192]{1,0:T(8,128)} %refs_0_.1), channel_id=1, source_target_pairs={{0,4},{4,0},{8,12},{12,8},{16,20},{20,16},{24,28},{28,24},{1,5},{5... | collective-permute-start | bytes 6291464 | tf_op jit(solution)/shard_map/ppermute | solution.py:250
  3.8 15.9 %collective-permute-start = (f32[64,4096]{1,0:T(8,128)}, f32[64,4096]{1,0:T(8,128)S(1)}, u32[]{:S(2)}, u32[]{:S(2)}) collective-permute-start(f32[64,4096]{1,0:T(8,128)} %get-tuple-element.20), channel_id=1, source_target_pairs={{0,8},{4,20},{8,0},{12,28},{16,24},{20,4},{24,16},{28,12},{1,9},{5... | collective-permute-start | bytes 3145736 | tf_op jit(solution)/shard_map/ppermute | solution.py:250
  6.3 5.6 %copy-start.2 = (f32[16,4096]{1,0:T(8,128)S(1)}, f32[16,4096]{1,0:T(8,128)}, u32[]{:S(2)}) copy-start(f32[16,4096]{1,0:T(8,128)} %param.9) | copy-start | bytes 786436
  11.8 19.9 %collective-permute-start.5 = (f32[64,4096]{1,0:T(8,128)}, f32[64,4096]{1,0:T(8,128)S(1)}, u32[]{:S(2)}, u32[]{:S(2)}) collective-permute-start(f32[64,4096]{1,0:T(8,128)} %get-tuple-element.23), channel_id=1, source_target_pairs={{0,8},{4,20},{8,0},{12,28},{16,24},{20,4},{24,16},{28,12},{1,9},{5... | collective-permute-start | bytes 3145736 | tf_op jit(solution)/shard_map/ppermute | solution.py:250
  14.4 1.7 %copy-start.3 = (f32[8,4096]{1,0:T(8,128)S(1)}, f32[8,4096]{1,0:T(8,128)}, u32[]{:S(2)}) copy-start(f32[8,4096]{1,0:T(8,128)} %param.10) | copy-start | bytes 393220
  19.7 12.7 %collective-permute-start.9 = (f32[64,2048]{1,0:T(8,128)S(1)}, f32[64,2048]{1,0:T(8,128)S(1)}, u32[]{:S(2)}, u32[]{:S(2)}) collective-permute-start(f32[64,2048]{1,0:T(8,128)S(1)} %get-tuple-element.41), channel_id=1, source_target_pairs={{0,4},{4,0},{8,12},{12,8},{16,20},{20,16},{24,28},{28,24},{1,5},{5... | collective-permute-start | bytes 1572872 | tf_op jit(solution)/shard_map/ppermute | solution.py:250
  19.9 12.5 %collective-permute-start.8 = (f32[64,2048]{1,0:T(8,128)S(1)}, f32[64,2048]{1,0:T(8,128)S(1)}, u32[]{:S(2)}, u32[]{:S(2)}) collective-permute-start(f32[64,2048]{1,0:T(8,128)S(1)} %get-tuple-element.42), channel_id=1, source_target_pairs={{0,4},{4,0},{8,12},{12,8},{16,20},{20,16},{24,28},{28,24},{1,5},{5... | collective-permute-start | bytes 1572872 | tf_op jit(solution)/shard_map/ppermute | solution.py:250
  26.0 19.8 %collective-permute-start.2 = (f32[64,4096]{1,0:T(8,128)}, f32[64,4096]{1,0:T(8,128)S(1)}, u32[]{:S(2)}, u32[]{:S(2)}) collective-permute-start(f32[64,4096]{1,0:T(8,128)} %get-tuple-element.20), channel_id=1, source_target_pairs={{0,16},{4,12},{8,24},{12,4},{16,0},{20,28},{24,8},{28,20},{1,17},{... | collective-permute-start | bytes 3145736 | tf_op jit(solution)/shard_map/ppermute | solution.py:250
  31.8 8.4 %collective-permute-start.7 = (f32[64,2048]{1,0:T(8,128)S(1)}, f32[64,2048]{1,0:T(8,128)S(1)}, u32[]{:S(2)}, u32[]{:S(2)}) collective-permute-start(f32[64,2048]{1,0:T(8,128)S(1)} %get-tuple-element.43), channel_id=1, source_target_pairs={{0,4},{4,0},{8,12},{12,8},{16,20},{20,16},{24,28},{28,24},{1,5},{5... | collective-permute-start | bytes 1572872 | tf_op jit(solution)/shard_map/ppermute | solution.py:250
  31.9 8.4 %collective-permute-start.6 = (f32[64,2048]{1,0:T(8,128)S(1)}, f32[64,2048]{1,0:T(8,128)S(1)}, u32[]{:S(2)}, u32[]{:S(2)}) collective-permute-start(f32[64,2048]{1,0:T(8,128)S(1)} %get-tuple-element.44), channel_id=1, source_target_pairs={{0,4},{4,0},{8,12},{12,8},{16,20},{20,16},{24,28},{28,24},{1,5},{5... | collective-permute-start | bytes 1572872 | tf_op jit(solution)/shard_map/ppermute | solution.py:250
  37.9 15.4 %collective-permute-start.10 = (f32[64,4096]{1,0:T(8,128)}, f32[64,4096]{1,0:T(8,128)S(1)}, u32[]{:S(2)}, u32[]{:S(2)}) collective-permute-start(f32[64,4096]{1,0:T(8,128)} %get-tuple-element.23), channel_id=1, source_target_pairs={{0,16},{4,12},{8,24},{12,4},{16,0},{20,28},{24,8},{28,20},{1,17},{... | collective-permute-start | bytes 3145736 | tf_op jit(solution)/shard_map/ppermute | solution.py:250
  45.9 8.0 %collective-permute-start.4 = (f32[64,2048]{1,0:T(8,128)S(1)}, f32[64,2048]{1,0:T(8,128)S(1)}, u32[]{:S(2)}, u32[]{:S(2)}) collective-permute-start(f32[64,2048]{1,0:T(8,128)S(1)} %get-tuple-element.45), channel_id=1, source_target_pairs={{0,4},{4,0},{8,12},{12,8},{16,20},{20,16},{24,28},{28,24},{1,5},{5... | collective-permute-start | bytes 1572872 | tf_op jit(solution)/shard_map/ppermute | solution.py:250
  46.0 8.0 %collective-permute-start.3 = (f32[64,2048]{1,0:T(8,128)S(1)}, f32[64,2048]{1,0:T(8,128)S(1)}, u32[]{:S(2)}, u32[]{:S(2)}) collective-permute-start(f32[64,2048]{1,0:T(8,128)S(1)} %get-tuple-element.46), channel_id=1, source_target_pairs={{0,4},{4,0},{8,12},{12,8},{16,20},{20,16},{24,28},{28,24},{1,5},{5... | collective-permute-start | bytes 1572872 | tf_op jit(solution)/shard_map/ppermute | solution.py:250
  46.5 20.6 %collective-permute-start.12 = (f32[64,4096]{1,0:T(8,128)S(1)}, f32[64,4096]{1,0:T(8,128)S(1)}, u32[]{:S(2)}, u32[]{:S(2)}) collective-permute-start(f32[64,4096]{1,0:T(8,128)S(1)} %collective-permute-done.refs_0_), channel_id=1, source_target_pairs={{0,16},{4,12},{8,24},{12,4},{16,0},{20,28},{24,8},{28,20},{1,17},{... | collective-permute-start | bytes 3145736 | tf_op jit(solution)/shard_map/ppermute | solution.py:250
  53.4 8.2 %collective-permute-start.14 = (f32[64,2048]{1,0:T(8,128)S(1)}, f32[64,2048]{1,0:T(8,128)S(1)}, u32[]{:S(2)}, u32[]{:S(2)}) collective-permute-start(f32[64,2048]{1,0:T(8,128)S(1)} %get-tuple-element.37), channel_id=1, source_target_pairs={{0,4},{4,0},{8,12},{12,8},{16,20},{20,16},{24,28},{28,24},{1,5},{5... | collective-permute-start | bytes 1572872 | tf_op jit(solution)/shard_map/ppermute | solution.py:250
  53.4 8.1 %collective-permute-start.13 = (f32[64,2048]{1,0:T(8,128)S(1)}, f32[64,2048]{1,0:T(8,128)S(1)}, u32[]{:S(2)}, u32[]{:S(2)}) collective-permute-start(f32[64,2048]{1,0:T(8,128)S(1)} %get-tuple-element.38), channel_id=1, source_target_pairs={{0,4},{4,0},{8,12},{12,8},{16,20},{20,16},{24,28},{28,24},{1,5},{5... | collective-permute-start | bytes 1572872 | tf_op jit(solution)/shard_map/ppermute | solution.py:250
  59.4 18.0 %collective-permute-start.11 = (f32[64,4096]{1,0:T(8,128)S(1)}, f32[64,4096]{1,0:T(8,128)S(1)}, u32[]{:S(2)}, u32[]{:S(2)}) collective-permute-start(f32[64,4096]{1,0:T(8,128)S(1)} %collective-permute-done.5.refs_0_), channel_id=1, source_target_pairs={{0,16},{4,12},{8,24},{12,4},{16,0},{20,28},{24,8},{28,20},{1,17},{... | collective-permute-start | bytes 3145736 | tf_op jit(solution)/shard_map/ppermute | solution.py:250
  67.1 4.7 %collective-permute-start.16 = (f32[64,2048]{1,0:T(8,128)S(1)}, f32[64,2048]{1,0:T(8,128)S(1)}, u32[]{:S(2)}, u32[]{:S(2)}) collective-permute-start(f32[64,2048]{1,0:T(8,128)S(1)} %get-tuple-element.35), channel_id=1, source_target_pairs={{0,4},{4,0},{8,12},{12,8},{16,20},{20,16},{24,28},{28,24},{1,5},{5... | collective-permute-start | bytes 1572872 | tf_op jit(solution)/shard_map/ppermute | solution.py:250
  67.2 4.6 %collective-permute-start.15 = (f32[64,2048]{1,0:T(8,128)S(1)}, f32[64,2048]{1,0:T(8,128)S(1)}, u32[]{:S(2)}, u32[]{:S(2)}) collective-permute-start(f32[64,2048]{1,0:T(8,128)S(1)} %get-tuple-element.36), channel_id=1, source_target_pairs={{0,4},{4,0},{8,12},{12,8},{16,20},{20,16},{24,28},{28,24},{1,5},{5... | collective-permute-start | bytes 1572872 | tf_op jit(solution)/shard_map/ppermute | solution.py:250
  77.6 2.0 %collective-permute-start.18 = (f32[64,2048]{1,0:T(8,128)S(1)}, f32[64,2048]{1,0:T(8,128)S(1)}, u32[]{:S(2)}, u32[]{:S(2)}) collective-permute-start(f32[64,2048]{1,0:T(8,128)S(1)} %get-tuple-element.33), channel_id=1, source_target_pairs={{0,4},{4,0},{8,12},{12,8},{16,20},{20,16},{24,28},{28,24},{1,5},{5... | collective-permute-start | bytes 1572872 | tf_op jit(solution)/shard_map/ppermute | solution.py:250
  77.7 2.6 %collective-permute-start.17 = (f32[64,2048]{1,0:T(8,128)S(1)}, f32[64,2048]{1,0:T(8,128)S(1)}, u32[]{:S(2)}, u32[]{:S(2)}) collective-permute-start(f32[64,2048]{1,0:T(8,128)S(1)} %get-tuple-element.34), channel_id=1, source_target_pairs={{0,4},{4,0},{8,12},{12,8},{16,20},{20,16},{24,28},{28,24},{1,5},{5... | collective-permute-start | bytes 1572872 | tf_op jit(solution)/shard_map/ppermute | solution.py:250
  79.4 21.7 %copy-start.1 = (bf16[64,8192]{1,0:T(8,128)(2,1)S(1)}, bf16[64,8192]{1,0:T(8,128)(2,1)}, u32[]{:S(2)}) copy-start(bf16[64,8192]{1,0:T(8,128)(2,1)} %pad_maximum_fusion.1.third) | copy-start | bytes 3145732
  81.7 4.3 %collective-permute-start.19 = (f32[64,256]{1,0:T(8,128)S(1)}, f32[64,256]{1,0:T(8,128)S(1)}, u32[]{:S(2)}, u32[]{:S(2)}) collective-permute-start(f32[64,256]{1,0:T(8,128)S(1)} %shard_map.82), channel_id=1, source_target_pairs={{0,1},{1,0},{2,3},{3,2},{4,5},{5,4},{6,7},{7,6},{8,9},{9,8},{10,11... | collective-permute-start | bytes 196616 | tf_op jit(solution)/shard_map/ppermute | solution.py:250
  86.1 5.2 %collective-permute-start.20 = (f32[64,256]{1,0:T(8,128)S(1)}, f32[64,256]{1,0:T(8,128)S(1)}, u32[]{:S(2)}, u32[]{:S(2)}) collective-permute-start(f32[64,256]{1,0:T(8,128)S(1)} %add.23), channel_id=1, source_target_pairs={{0,2},{1,3},{2,0},{3,1},{4,6},{5,7},{6,4},{7,5},{8,10},{9,11},{10,... | collective-permute-start | bytes 196616 | tf_op jit(solution)/shard_map/ppermute | solution.py:250

commit v4 on v3

--- a/solution.py
+++ b/solution.py
@@ -10,7 +10,8 @@
 from jax.sharding import PartitionSpec as P
 
 LANES = 128
-FETCH_LAG = 1
+FETCH_LAG = 2
+LATE = 2
 LIMIT = 24
 STEP = 2048
 TWIN_CUTS = 2
@@ -112,29 +113,6 @@
     return result[0] if fetch is None else result
 
 
-def fetch_kernel(row, table, amp, token, fetched, sems):
-    unit = fetched.shape[-1]
-    copies = []
-    for index in range(fetched.shape[0]):
-        here = pl.ds(pl.multiple_of(table[row, index] * unit, LANES), unit)
-        copies.append(pltpu.make_async_copy(amp.at[:, :, here], fetched.at[index], sems.at[index]))
-        copies[-1].start()
-    for copy in copies:
-        copy.wait()
-
-
-def fetch_columns(table, row, amplitudes, unit, token):
-    parts, rows, _ = amplitudes.shape
-    return pl.pallas_call(
-        functools.partial(fetch_kernel, row),
-        in_specs=[pl.BlockSpec(memory_space=pltpu.SMEM)] + [pl.BlockSpec(memory_space=pl.ANY)] * 2,
-        out_specs=pl.BlockSpec(memory_space=pltpu.VMEM),
-        out_shape=pltpu.VMEM((2, parts, rows, unit), jnp.float32),
-        scratch_shapes=[pltpu.SemaphoreType.DMA((2,))],
-        compiler_params=pltpu.CompilerParams(vmem_limit_bytes=16 * 2**20),
-    )(table, amplitudes, token)
-
-
 def project_fetched_kernel(which, step, last, fetched, *refs):
     blocks, start, out = refs[:-2], refs[-2], refs[-1]
     bond_dim = blocks[0].shape[0]
@@ -285,7 +263,7 @@
     arrays = {block: vectors[:, block[2] * unit : (block[2] + 1) * unit] for block in held[:halves]}
     total = jnp.zeros((amplitudes.shape[0] * amplitudes.shape[1], 2 * bond_dim), jnp.float32)
     add = functools.partial(project, table)
-    arrived, fetched = [], []
+    arrived, fetched = [], {}
     totals = [after(total, *arrays.values())]
     products = [lambda total: add(0, 0, amplitudes, [vectors], unit, total)]
 
@@ -310,22 +288,24 @@
         mine = arrays[block]
         if number >= len(rounds) - 2:
             mine = after(mine, products_done(number + 2))
-        cuts = TWIN_CUTS if unit % (TWIN_CUTS * LANES) == 0 else 1
+        cuts = TWIN_CUTS if number >= 0 and unit % (TWIN_CUTS * LANES) == 0 else 1
         pair = [arrays[block]]
         for cut in range(cuts):
             some = mine[:, cut * unit // cuts : (cut + 1) * unit // cuts] if cuts > 1 else mine
             pair.append(swap(some, "bond", size, twin))
 
         def product(total, number=number, pair=pair):
-            if number == len(rounds) - 2:
-                fetched.append(fetch_columns(table, len(rounds), amplitudes, unit, totals[len(rounds) - 1]))
-                total = after(total, fetched[0])
-            return add(number + 1, 0, amplitudes, pair, unit, total)
+            if number in fetched:
+                total = project_fetched(fetched[number], 0, pair[:1], total)
+                return project_fetched(fetched[number], 1, pair[1:], total, last=number == len(rounds) - 1)
+            target = number + FETCH_LAG
+            if target < len(rounds) - LATE:
+                return add(number + 1, 0, amplitudes, pair, unit, total)
+            total, fetched[target] = add(number + 1, 0, amplitudes, pair, unit, total, fetch=target + 1)
+            return total
 
         products.append(product)
-    total = products_done(len(rounds) + 1)
-    total = project_fetched(fetched[0], 0, pair[:1], total)
-    return project_fetched(fetched[0], 1, pair[1:], total, last=True)
+    return products_done(len(rounds) + 2)
 
 
 def local(bond, leg, amplitudes, vectors, row_map, col_map):

time: 106 us -> 105 us (level)
  Pallas kernels: 49.9 us -> 44.6 us
  waiting for transfers between devices: 15.8 us -> 18.9 us
    pallas_call x1 -> x0, Pallas kernels: 4.08 us -> none  [fetch_columns(): pl.pallas_call(functools.partial(fetch_kernel, row), in_specs=[pl.BlockSp...]
    pallas_call x7 -> x6, Pallas kernels: 38.7 us -> 35 us  [project(): pl.pallas_call(functools.partial(project_kernel, places, unit, row, fetch...]
    ppermute x21, waiting for transfers between devices: 15.8 us -> 18.9 us  [swap(): return lax.ppermute(x, axis, [(i, partner(i)) for i in range(size)])]
    pallas_call x2 -> x4, Pallas kernels: 2.69 us -> 5.14 us  [project_fetched(): pl.pallas_call(functools.partial(project_fetched_kernel, which, step, las...]
  transfers between devices with their start and end apart: 21 -> 21, of which waited for: 6 -> 9; matrix products, arithmetic and copies ran while one was open for 11% -> 11% of each run, Pallas kernels for 42% -> 37%
where the time goes in v4:
time: 105 us; the launch traced here: 104 us
  Pallas kernels  44.6 us (42%)
  starting transfers between devices  19 us (18%)
  waiting for transfers between devices  18.9 us (18%)
  blocking collectives  10.1 us (10%)
  local copies, waits for them, and re-layouts  7.22 us (7%)
  other arithmetic  4.26 us (4%)
    pallas_call x6, Pallas kernels, project(): pl.pallas_call(functools.partial(project_kernel, places, unit, row, fetch...  35 us
    ppermute x21, starting transfers between devices, swap(): return lax.ppermute(x, axis, [(i, partner(i)) for i in range(size)])  19 us
    ppermute x21, waiting for transfers between devices, swap(): return lax.ppermute(x, axis, [(i, partner(i)) for i in range(size)])  18.9 us
    all_gather x1, blocking collectives, local(): slab = lax.all_gather(total, 'bond', axis=0)  10.1 us
    pallas_call x4, Pallas kernels, project_fetched(): pl.pallas_call(functools.partial(project_fetched_kernel, which, step, las...  5.14 us
    pallas_call x1, Pallas kernels, coarsen(): pl.pallas_call(functools.partial(coarsen_kernel, rows_q), in_specs=[pl.Bl...  4.41 us
    slice x1, local copies, waits for them, and re-layouts, gather_and_project(): vectors[:, block[2] * unit:(block[2] + 1) * unit]  3.21 us
  transfers between devices with their start and end apart: 21, of which 9 were waited for; matrix products, arithmetic and copies ran while one was open for 11% of the time, Pallas kernels for 37%

profile of v4, /device:TPU:0, one launch (start us, length us, event | category | flops | bytes accessed | tf_op | source)
XLA Modules:
  0.0 104.4 jit_solution(815393792293030664)
XLA Ops:
  0.0 0.5 collective-permute-start.3
  0.5 3.2 %fusion.2 = (f32[64,4096]{1,0:T(8,128)}, f32[64,4096]{1,0:T(8,128)}) fusion(f32[64,8192]{1,0:T(8,128)} %refs_0_.1), kind=kLoop, calls=%fused_computation.12 | loop fusion | bytes 4194304 | tf_op jit(solution)/shard_map/slice | solution.py:263
  3.7 2.5 %collective-permute-start = (f32[64,4096]{1,0:T(8,128)}, f32[64,4096]{1,0:T(8,128)S(1)}, u32[]{:S(2)}, u32[]{:S(2)}) collective-permute-start(f32[64,4096]{1,0:T(8,128)} %get-tuple-element.25), channel_id=1, source_target_pairs={{0,8},{4,20},{8,0},{12,28},{16,24},{20,4},{24,16},{28,12},{1,9},{5... | collective-permute-start | bytes 3145736 | tf_op jit(solution)/shard_map/ppermute | solution.py:228
  6.3 0.0 copy-start.2
  6.3 5.4 %shard_map.73.refs_1_ = f32[256,128]{1,0:T(8,128)S(1)} custom-call(s32[7,4]{1,0:T(8,128)S(1)} %multiply_add_fusion.table, f32[2,128,65536]{2,1,0:T(8,128)} %amp.11, f32[64,8192]{1,0:T(8,128)S(1)} %copy-done, f32[256,128]{1,0:T(8,128)S(1)} %broadcast_in_dim.8.refs_1_), custom_call_target="tpu_custom_call" | custom-call | flops 1073741824 | bytes 10485760 | tf_op jit(solution)/shard_map/pallas_call | solution.py:92
  11.7 0.1 collective-permute-start.10
  11.8 1.0 reshape.21
  12.8 1.4 %select_maximum_fusion = f32[32,64,128]{2,1,0:T(8,128)S(1)} fusion(f32[16,64,64]{2,1,0:T(8,128)} %reshape.21), kind=kLoop, calls=%fused_computation.6 | loop fusion | flops 1310720 | bytes 1310720 | tf_op jit(solution)/shard_map/concatenate | solution.py:222
  14.3 0.0 copy-start.3
  14.3 0.6 reduce-precision_convert_fusion
  14.9 1.1 %pad_maximum_fusion.1.third = bf16[64,8192]{1,0:T(8,128)(2,1)} fusion(bf16[32,8192]{1,0:T(8,128)(2,1)S(1)} %get-tuple-element.52, bf16[32,8192]{1,0:T(8,128)(2,1)S(1)} %get-tuple-element.51), kind=kLoop, calls=%fused_computation.10 | loop fusion | flops 2097152 | bytes 2097152 | tf_op jit(solution)/shard_map/concatenate | solution.py:224
  16.0 0.1 reshape.18
  16.1 0.2 copy.8
  16.3 0.5 fusion.9
  16.8 0.5 reshape.19
  17.3 1.2 %reshape.20 = f32[64,1024]{1,0:T(8,128)} reshape(f32[64,8,2,64]{3,2,1,0:T(2,128)S(1)} %get-tuple-element.56) | data formatting | bytes 524288 | tf_op jit(solution)/shard_map/reshape | solution.py:217
  18.4 1.1 %fusion = (bf16[256,1024]{1,0:T(8,128)(2,1)S(1)}, bf16[256,1024]{1,0:T(8,128)(2,1)S(1)}) fusion(f32[64,1024]{1,0:T(8,128)S(1)} %broadcast_in_dim.7, f32[64,1024]{1,0:T(8,128)} %reshape.20, f32[64,1024]{1,0:T(8,128)S(1)} %reshape.19), kind=kLoop, calls=%fused_computation.4 | loop fusion | flops 1835008 | bytes 1835008 | tf_op jit(solution)/shard_map/convert_element_type | solution.py:209
  19.6 0.1 fusion.8
  19.7 0.2 collective-permute-start.2
  19.8 0.4 collective-permute-start.1
  20.2 5.6 %shard_map.74.refs_3_ = f32[256,128]{1,0:T(8,128)S(1)} custom-call(s32[7,4]{1,0:T(8,128)S(1)} %multiply_add_fusion.table, f32[2,128,65536]{2,1,0:T(8,128)} %amp.11, f32[64,8192]{1,0:T(8,128)} %collective-permute-done.3.refs_0_, f32[256,128]{1,0:T(8,128)S(1)} %shard_map.73.refs_1_), custom_call_target="tpu_custom_call" | custom-call | flops 1073741824 | bytes 10485760 | tf_op jit(solution)/shard_map/pallas_call | solution.py:92
  25.8 2.1 %collective-permute-start.7 = (f32[64,4096]{1,0:T(8,128)}, f32[64,4096]{1,0:T(8,128)S(1)}, u32[]{:S(2)}, u32[]{:S(2)}) collective-permute-start(f32[64,4096]{1,0:T(8,128)} %get-tuple-element.25), channel_id=1, source_target_pairs={{0,16},{4,12},{8,24},{12,4},{16,0},{20,28},{24,8},{28,20},{1,17},{... | collective-permute-start | bytes 3145736 | tf_op jit(solution)/shard_map/ppermute | solution.py:228
  27.9 3.9 %collective-permute-done.10.refs_0_ = f32[64,4096]{1,0:T(8,128)S(1)} collective-permute-done((f32[64,4096]{1,0:T(8,128)}, f32[64,4096]{1,0:T(8,128)S(1)}, u32[]{:S(2)}, u32[]{:S(2)}) %collective-permute-start.10) | collective-permute-done | bytes 1048608 | tf_op jit(solution)/shard_map/ppermute | solution.py:228
  31.8 0.1 fusion.5
  31.9 0.1 collective-permute-start.12
  32.0 0.5 collective-permute-start.11
  32.5 5.4 %shard_map.75.refs_3_ = f32[256,128]{1,0:T(8,128)S(1)} custom-call(s32[7,4]{1,0:T(8,128)S(1)} %multiply_add_fusion.table, f32[2,128,65536]{2,1,0:T(8,128)} %amp.11, f32[64,4096]{1,0:T(8,128)S(1)} %collective-permute-done.refs_0_, f32[64,2048]{1,0:T(8,128)S(1)} %collective-permute-done.1.refs_1_, f32[64,2048]{1,0:T(8,128)S(1)} %collective-permute-done.2.refs_2_, ...), custom_call_target="tpu_custom_call" | custom-call | flops 1073741824 | bytes 10485760 | tf_op jit(solution)/shard_map/pallas_call | solution.py:92
  38.0 2.4 %collective-permute-start.4 = (f32[64,4096]{1,0:T(8,128)}, f32[64,4096]{1,0:T(8,128)S(1)}, u32[]{:S(2)}, u32[]{:S(2)}) collective-permute-start(f32[64,4096]{1,0:T(8,128)} %get-tuple-element.26), channel_id=1, source_target_pairs={{0,16},{4,12},{8,24},{12,4},{16,0},{20,28},{24,8},{28,20},{1,17},{... | collective-permute-start | bytes 3145736 | tf_op jit(solution)/shard_map/ppermute | solution.py:228
  40.4 0.0 collective-permute-done.11.refs_1_
  40.4 5.4 %shard_map.76.refs_3_ = f32[256,128]{1,0:T(8,128)S(1)} custom-call(s32[7,4]{1,0:T(8,128)S(1)} %multiply_add_fusion.table, f32[2,128,65536]{2,1,0:T(8,128)} %amp.11, f32[64,4096]{1,0:T(8,128)S(1)} %collective-permute-done.10.refs_0_, f32[64,2048]{1,0:T(8,128)S(1)} %collective-permute-done.11.refs_1_, f32[64,2048]{1,0:T(8,128)S(1)} %collective-permute-done.12.refs_2_, ...), custom_call_target="tpu_custom_call" | custom-call | flops 1073741824 | bytes 10485760 | tf_op jit(solution)/shard_map/pallas_call | solution.py:92
  45.8 0.1 fusion.6
  45.9 0.1 collective-permute-start.9
  46.0 0.5 collective-permute-start.8
  46.5 0.9 collective-permute-start.14
  47.3 6.0 %collective-permute-done.4.refs_0_ = f32[64,4096]{1,0:T(8,128)S(1)} collective-permute-done((f32[64,4096]{1,0:T(8,128)}, f32[64,4096]{1,0:T(8,128)S(1)}, u32[]{:S(2)}, u32[]{:S(2)}) %collective-permute-start.4) | collective-permute-done | bytes 1048608 | tf_op jit(solution)/shard_map/ppermute | solution.py:228
  53.3 0.1 fusion.7
  53.4 0.1 collective-permute-start.6
  53.5 0.5 collective-permute-start.5
  54.0 6.6 %shard_map.77 = (f32[256,128]{1,0:T(8,128)S(1)}, f32[2,2,128,4096]{3,2,1,0:T(8,128)S(1)}) custom-call(s32[7,4]{1,0:T(8,128)S(1)} %multiply_add_fusion.table, f32[2,128,65536]{2,1,0:T(8,128)} %amp.11, f32[64,4096]{1,0:T(8,128)S(1)} %collective-permute-done.7.refs_0_, f32[64,2048]{1,0:T(8,128)S(1)} %collective-permute-done.8.refs_1_, ...), custom_call_target="tpu_custom_call" | custom-call | flops 1073741824 | bytes 10485760 | tf_op jit(solution)/shard_map/pallas_call | solution.py:92
  60.6 2.1 %collective-permute-start.13 = (f32[64,4096]{1,0:T(8,128)S(1)}, f32[64,4096]{1,0:T(8,128)S(1)}, u32[]{:S(2)}, u32[]{:S(2)}) collective-permute-start(f32[64,4096]{1,0:T(8,128)S(1)} %collective-permute-done.10.refs_0_), channel_id=1, source_target_pairs={{0,16},{4,12},{8,24},{12,4},{16,0},{20,28},{24,8},{28,20},{1,17},{... | collective-permute-start | bytes 3145736 | tf_op jit(solution)/shard_map/ppermute | solution.py:228
  62.7 0.0 collective-permute-done.6.refs_2_
  62.7 0.0 collective-permute-done.5.refs_1_
  62.7 6.6 %shard_map.78 = (f32[256,128]{1,0:T(8,128)S(1)}, f32[2,2,128,4096]{3,2,1,0:T(8,128)S(1)}) custom-call(s32[7,4]{1,0:T(8,128)S(1)} %multiply_add_fusion.table, f32[2,128,65536]{2,1,0:T(8,128)} %amp.11, f32[64,4096]{1,0:T(8,128)S(1)} %collective-permute-done.4.refs_0_, f32[64,2048]{1,0:T(8,128)S(1)} %collective-permute-done.5.refs_1_, ...), custom_call_target="tpu_custom_call" | custom-call | flops 1073741824 | bytes 10485760 | tf_op jit(solution)/shard_map/pallas_call | solution.py:92
  69.3 0.1 fusion.4
  69.4 0.1 collective-permute-start.16
  69.5 0.5 collective-permute-start.15
  70.0 1.3 %shard_map.79.refs_2_ = f32[256,128]{1,0:T(8,128)S(1)} custom-call(f32[2,2,128,4096]{3,2,1,0:T(8,128)S(1)} %get-tuple-element.31.fetched, f32[64,4096]{1,0:T(8,128)S(1)} %collective-permute-done.14.refs_0_, f32[256,128]{1,0:T(8,128)S(1)} %get-tuple-element.34.refs_1_), custom_call_target="tpu_custom_call" | custom-call | flops 536870912 | bytes 5242880 | tf_op jit(solution)/shard_map/pallas_call | solution.py:142
  71.3 0.1 collective-permute-done.16.refs_1_
  71.4 0.7 collective-permute-done.15.refs_0_
  72.1 1.3 %shard_map.80.refs_1_ = f32[256,128]{1,0:T(8,128)S(1)} custom-call(f32[2,2,128,4096]{3,2,1,0:T(8,128)S(1)} %get-tuple-element.31.fetched, f32[64,2048]{1,0:T(8,128)S(1)} %collective-permute-done.15.refs_0_, f32[64,2048]{1,0:T(8,128)S(1)} %collective-permute-done.16.refs_1_, f32[256,128]{1,0:T(8,128)S(1)} %shard_map.79.refs_2_), custom_call_target="tpu_custom_call" | custom-call | flops 536870912 | bytes 5242880 | tf_op jit(solution)/shard_map/pallas_call | solution.py:142
  73.4 2.4 %collective-permute-done.13.refs_0_ = f32[64,4096]{1,0:T(8,128)S(1)} collective-permute-done((f32[64,4096]{1,0:T(8,128)S(1)}, f32[64,4096]{1,0:T(8,128)S(1)}, u32[]{:S(2)}, u32[]{:S(2)}) %collective-permute-start.13) | collective-permute-done | bytes 1048608 | tf_op jit(solution)/shard_map/ppermute | solution.py:228
  75.8 0.1 fusion.3
  75.9 0.1 collective-permute-start.18
  76.0 0.5 collective-permute-start.17
  76.5 1.3 %shard_map.81.refs_2_ = f32[256,128]{1,0:T(8,128)S(1)} custom-call(f32[2,2,128,4096]{3,2,1,0:T(8,128)S(1)} %get-tuple-element.28.fetched, f32[64,4096]{1,0:T(8,128)S(1)} %collective-permute-done.13.refs_0_, f32[256,128]{1,0:T(8,128)S(1)} %shard_map.80.refs_1_), custom_call_target="tpu_custom_call" | custom-call | flops 536870912 | bytes 5242880 | tf_op jit(solution)/shard_map/pallas_call | solution.py:142
  77.8 0.1 collective-permute-done.18.refs_1_
  77.9 0.7 collective-permute-done.17.refs_0_
  78.6 1.4 %shard_map.82 = f32[64,256]{1,0:T(8,128)S(1)} custom-call(f32[2,2,128,4096]{3,2,1,0:T(8,128)S(1)} %get-tuple-element.28.fetched, f32[64,2048]{1,0:T(8,128)S(1)} %collective-permute-done.17.refs_0_, f32[64,2048]{1,0:T(8,128)S(1)} %collective-permute-done.18.refs_1_, f32[256,128]{1,0:T(8,128)S(1)} %shard_map.81.refs_2_), custom_call_target="tpu_custom_call" | custom-call | flops 536870912 | bytes 5242880 | tf_op jit(solution)/shard_map/pallas_call | solution.py:142
  80.0 2.1 %collective-permute-start.19 = (f32[64,256]{1,0:T(8,128)S(1)}, f32[64,256]{1,0:T(8,128)S(1)}, u32[]{:S(2)}, u32[]{:S(2)}) collective-permute-start(f32[64,256]{1,0:T(8,128)S(1)} %shard_map.82), channel_id=1, source_target_pairs={{0,1},{1,0},{2,3},{3,2},{4,5},{5,4},{6,7},{7,6},{8,9},{9,8},{10,11... | collective-permute-start | bytes 196616 | tf_op jit(solution)/shard_map/ppermute | solution.py:228
  82.2 2.4 %collective-permute-done.19 = f32[64,256]{1,0:T(8,128)S(1)} collective-permute-done((f32[64,256]{1,0:T(8,128)S(1)}, f32[64,256]{1,0:T(8,128)S(1)}, u32[]{:S(2)}, u32[]{:S(2)}) %collective-permute-start.19) | collective-permute-done | bytes 65568 | tf_op jit(solution)/shard_map/ppermute | solution.py:228
  84.6 2.9 %collective-permute-start.20 = (f32[64,256]{1,0:T(8,128)S(1)}, f32[64,256]{1,0:T(8,128)S(1)}, u32[]{:S(2)}, u32[]{:S(2)}) collective-permute-start(f32[64,256]{1,0:T(8,128)S(1)} %add.23), channel_id=1, source_target_pairs={{0,2},{1,3},{2,0},{3,1},{4,6},{5,7},{6,4},{7,5},{8,10},{9,11},{10,... | collective-permute-start | bytes 196616 | tf_op jit(solution)/shard_map/ppermute | solution.py:228
  87.5 2.3 %collective-permute-done.20 = f32[64,256]{1,0:T(8,128)S(1)} collective-permute-done((f32[64,256]{1,0:T(8,128)S(1)}, f32[64,256]{1,0:T(8,128)S(1)}, u32[]{:S(2)}, u32[]{:S(2)}) %collective-permute-start.20) | collective-permute-done | bytes 65568 | tf_op jit(solution)/shard_map/ppermute | solution.py:228
  89.9 10.1 %all-gather = f32[512,256]{1,0:T(8,128)S(1)} all-gather(f32[64,256]{1,0:T(8,128)S(1)} %add.24), channel_id=2, replica_groups=mesh['bond'=8,'leg'=4] {'bond'}, dimensions={0}, use_global_device_ids=true | all-gather | bytes 589824 | tf_op jit(solution)/shard_map/all_gather | solution.py:320
  100.0 4.4 %shard_map.83 = f32[2,64,16]{2,1,0:T(8,128)} custom-call(f32[8,64,256]{2,1,0:T(8,128)S(1)} %bitcast.11, bf16[256,1024]{1,0:T(8,128)(2,1)S(1)} %get-tuple-element.54.first_hi, bf16[256,1024]{1,0:T(8,128)(2,1)S(1)} %get-tuple-element.53.first_lo, bf16[64,8192]{1,0:T(8,128)(2,1)S(1)} %copy-done.1), custom_call_target="tpu_custom_call" | custom-call | tf_op jit(solution)/shard_map/pallas_call | solution.py:196
  (26 shorter events, 0.1 us)
Async XLA Ops:
  0.0 6.3 %copy-start.4 = (s32[7,4]{1,0:T(8,128)S(1)}, s32[7,4]{1,0:T(8,128)}, u32[]{:S(2)}) copy-start(s32[7,4]{1,0:T(8,128)} %constant.34.clone) | copy-start | bytes 340
  0.0 6.3 %copy-start.5 = (s32[7,4]{1,0:T(8,128)S(1)}, s32[7,4]{1,0:T(8,128)}, u32[]{:S(2)}) copy-start(s32[7,4]{1,0:T(8,128)} %constant.33.clone) | copy-start | bytes 340
  0.0 6.3 %copy-start.6 = (s32[7,4]{1,0:T(8,128)S(1)}, s32[7,4]{1,0:T(8,128)}, u32[]{:S(2)}) copy-start(s32[7,4]{1,0:T(8,128)} %constant.32.clone) | copy-start | bytes 340
  0.0 6.3 %copy-start = (f32[64,8192]{1,0:T(8,128)S(1)}, f32[64,8192]{1,0:T(8,128)}, u32[]{:S(2)}) copy-start(f32[64,8192]{1,0:T(8,128)} %refs_0_.1) | copy-start | bytes 6291460
  0.0 20.2 %collective-permute-start.3 = (f32[64,8192]{1,0:T(8,128)}, f32[64,8192]{1,0:T(8,128)}, u32[]{:S(2)}, u32[]{:S(2)}) collective-permute-start(f32[64,8192]{1,0:T(8,128)} %refs_0_.1), channel_id=1, source_target_pairs={{0,4},{4,0},{8,12},{12,8},{16,20},{20,16},{24,28},{28,24},{1,5},{5... | collective-permute-start | bytes 6291464 | tf_op jit(solution)/shard_map/ppermute | solution.py:228
  3.7 15.8 %collective-permute-start = (f32[64,4096]{1,0:T(8,128)}, f32[64,4096]{1,0:T(8,128)S(1)}, u32[]{:S(2)}, u32[]{:S(2)}) collective-permute-start(f32[64,4096]{1,0:T(8,128)} %get-tuple-element.25), channel_id=1, source_target_pairs={{0,8},{4,20},{8,0},{12,28},{16,24},{20,4},{24,16},{28,12},{1,9},{5... | collective-permute-start | bytes 3145736 | tf_op jit(solution)/shard_map/ppermute | solution.py:228
  6.3 5.5 %copy-start.2 = (f32[16,4096]{1,0:T(8,128)S(1)}, f32[16,4096]{1,0:T(8,128)}, u32[]{:S(2)}) copy-start(f32[16,4096]{1,0:T(8,128)} %param.9) | copy-start | bytes 786436
  11.7 20.1 %collective-permute-start.10 = (f32[64,4096]{1,0:T(8,128)}, f32[64,4096]{1,0:T(8,128)S(1)}, u32[]{:S(2)}, u32[]{:S(2)}) collective-permute-start(f32[64,4096]{1,0:T(8,128)} %get-tuple-element.26), channel_id=1, source_target_pairs={{0,8},{4,20},{8,0},{12,28},{16,24},{20,4},{24,16},{28,12},{1,9},{5... | collective-permute-start | bytes 3145736 | tf_op jit(solution)/shard_map/ppermute | solution.py:228
  14.3 1.7 %copy-start.3 = (f32[8,4096]{1,0:T(8,128)S(1)}, f32[8,4096]{1,0:T(8,128)}, u32[]{:S(2)}) copy-start(f32[8,4096]{1,0:T(8,128)} %param.10) | copy-start | bytes 393220
  19.7 12.9 %collective-permute-start.2 = (f32[64,2048]{1,0:T(8,128)S(1)}, f32[64,2048]{1,0:T(8,128)S(1)}, u32[]{:S(2)}, u32[]{:S(2)}) collective-permute-start(f32[64,2048]{1,0:T(8,128)S(1)} %get-tuple-element.49), channel_id=1, source_target_pairs={{0,4},{4,0},{8,12},{12,8},{16,20},{20,16},{24,28},{28,24},{1,5},{5... | collective-permute-start | bytes 1572872 | tf_op jit(solution)/shard_map/ppermute | solution.py:228
  19.8 12.7 %collective-permute-start.1 = (f32[64,2048]{1,0:T(8,128)S(1)}, f32[64,2048]{1,0:T(8,128)S(1)}, u32[]{:S(2)}, u32[]{:S(2)}) collective-permute-start(f32[64,2048]{1,0:T(8,128)S(1)} %get-tuple-element.50), channel_id=1, source_target_pairs={{0,4},{4,0},{8,12},{12,8},{16,20},{20,16},{24,28},{28,24},{1,5},{5... | collective-permute-start | bytes 1572872 | tf_op jit(solution)/shard_map/ppermute | solution.py:228
  25.8 20.0 %collective-permute-start.7 = (f32[64,4096]{1,0:T(8,128)}, f32[64,4096]{1,0:T(8,128)S(1)}, u32[]{:S(2)}, u32[]{:S(2)}) collective-permute-start(f32[64,4096]{1,0:T(8,128)} %get-tuple-element.25), channel_id=1, source_target_pairs={{0,16},{4,12},{8,24},{12,4},{16,0},{20,28},{24,8},{28,20},{1,17},{... | collective-permute-start | bytes 3145736 | tf_op jit(solution)/shard_map/ppermute | solution.py:228
  31.9 8.4 %collective-permute-start.12 = (f32[64,2048]{1,0:T(8,128)S(1)}, f32[64,2048]{1,0:T(8,128)S(1)}, u32[]{:S(2)}, u32[]{:S(2)}) collective-permute-start(f32[64,2048]{1,0:T(8,128)S(1)} %get-tuple-element.43), channel_id=1, source_target_pairs={{0,4},{4,0},{8,12},{12,8},{16,20},{20,16},{24,28},{28,24},{1,5},{5... | collective-permute-start | bytes 1572872 | tf_op jit(solution)/shard_map/ppermute | solution.py:228
  32.0 8.3 %collective-permute-start.11 = (f32[64,2048]{1,0:T(8,128)S(1)}, f32[64,2048]{1,0:T(8,128)S(1)}, u32[]{:S(2)}, u32[]{:S(2)}) collective-permute-start(f32[64,2048]{1,0:T(8,128)S(1)} %get-tuple-element.44), channel_id=1, source_target_pairs={{0,4},{4,0},{8,12},{12,8},{16,20},{20,16},{24,28},{28,24},{1,5},{5... | collective-permute-start | bytes 1572872 | tf_op jit(solution)/shard_map/ppermute | solution.py:228
  38.0 15.4 %collective-permute-start.4 = (f32[64,4096]{1,0:T(8,128)}, f32[64,4096]{1,0:T(8,128)S(1)}, u32[]{:S(2)}, u32[]{:S(2)}) collective-permute-start(f32[64,4096]{1,0:T(8,128)} %get-tuple-element.26), channel_id=1, source_target_pairs={{0,16},{4,12},{8,24},{12,4},{16,0},{20,28},{24,8},{28,20},{1,17},{... | collective-permute-start | bytes 3145736 | tf_op jit(solution)/shard_map/ppermute | solution.py:228
  45.9 8.1 %collective-permute-start.9 = (f32[64,2048]{1,0:T(8,128)S(1)}, f32[64,2048]{1,0:T(8,128)S(1)}, u32[]{:S(2)}, u32[]{:S(2)}) collective-permute-start(f32[64,2048]{1,0:T(8,128)S(1)} %get-tuple-element.45), channel_id=1, source_target_pairs={{0,4},{4,0},{8,12},{12,8},{16,20},{20,16},{24,28},{28,24},{1,5},{5... | collective-permute-start | bytes 1572872 | tf_op jit(solution)/shard_map/ppermute | solution.py:228
  46.0 8.0 %collective-permute-start.8 = (f32[64,2048]{1,0:T(8,128)S(1)}, f32[64,2048]{1,0:T(8,128)S(1)}, u32[]{:S(2)}, u32[]{:S(2)}) collective-permute-start(f32[64,2048]{1,0:T(8,128)S(1)} %get-tuple-element.46), channel_id=1, source_target_pairs={{0,4},{4,0},{8,12},{12,8},{16,20},{20,16},{24,28},{28,24},{1,5},{5... | collective-permute-start | bytes 1572872 | tf_op jit(solution)/shard_map/ppermute | solution.py:228
  46.5 22.8 %collective-permute-start.14 = (f32[64,4096]{1,0:T(8,128)S(1)}, f32[64,4096]{1,0:T(8,128)S(1)}, u32[]{:S(2)}, u32[]{:S(2)}) collective-permute-start(f32[64,4096]{1,0:T(8,128)S(1)} %collective-permute-done.refs_0_), channel_id=1, source_target_pairs={{0,16},{4,12},{8,24},{12,4},{16,0},{20,28},{24,8},{28,20},{1,17},{... | collective-permute-start | bytes 3145736 | tf_op jit(solution)/shard_map/ppermute | solution.py:228
  53.4 9.3 %collective-permute-start.6 = (f32[64,2048]{1,0:T(8,128)S(1)}, f32[64,2048]{1,0:T(8,128)S(1)}, u32[]{:S(2)}, u32[]{:S(2)}) collective-permute-start(f32[64,2048]{1,0:T(8,128)S(1)} %get-tuple-element.47), channel_id=1, source_target_pairs={{0,4},{4,0},{8,12},{12,8},{16,20},{20,16},{24,28},{28,24},{1,5},{5... | collective-permute-start | bytes 1572872 | tf_op jit(solution)/shard_map/ppermute | solution.py:228
  53.5 9.2 %collective-permute-start.5 = (f32[64,2048]{1,0:T(8,128)S(1)}, f32[64,2048]{1,0:T(8,128)S(1)}, u32[]{:S(2)}, u32[]{:S(2)}) collective-permute-start(f32[64,2048]{1,0:T(8,128)S(1)} %get-tuple-element.48), channel_id=1, source_target_pairs={{0,4},{4,0},{8,12},{12,8},{16,20},{20,16},{24,28},{28,24},{1,5},{5... | collective-permute-start | bytes 1572872 | tf_op jit(solution)/shard_map/ppermute | solution.py:228
  60.6 15.2 %collective-permute-start.13 = (f32[64,4096]{1,0:T(8,128)S(1)}, f32[64,4096]{1,0:T(8,128)S(1)}, u32[]{:S(2)}, u32[]{:S(2)}) collective-permute-start(f32[64,4096]{1,0:T(8,128)S(1)} %collective-permute-done.10.refs_0_), channel_id=1, source_target_pairs={{0,16},{4,12},{8,24},{12,4},{16,0},{20,28},{24,8},{28,20},{1,17},{... | collective-permute-start | bytes 3145736 | tf_op jit(solution)/shard_map/ppermute | solution.py:228
  69.4 2.0 %collective-permute-start.16 = (f32[64,2048]{1,0:T(8,128)S(1)}, f32[64,2048]{1,0:T(8,128)S(1)}, u32[]{:S(2)}, u32[]{:S(2)}) collective-permute-start(f32[64,2048]{1,0:T(8,128)S(1)} %get-tuple-element.41), channel_id=1, source_target_pairs={{0,4},{4,0},{8,12},{12,8},{16,20},{20,16},{24,28},{28,24},{1,5},{5... | collective-permute-start | bytes 1572872 | tf_op jit(solution)/shard_map/ppermute | solution.py:228
  69.5 2.6 %collective-permute-start.15 = (f32[64,2048]{1,0:T(8,128)S(1)}, f32[64,2048]{1,0:T(8,128)S(1)}, u32[]{:S(2)}, u32[]{:S(2)}) collective-permute-start(f32[64,2048]{1,0:T(8,128)S(1)} %get-tuple-element.42), channel_id=1, source_target_pairs={{0,4},{4,0},{8,12},{12,8},{16,20},{20,16},{24,28},{28,24},{1,5},{5... | collective-permute-start | bytes 1572872 | tf_op jit(solution)/shard_map/ppermute | solution.py:228
  75.9 2.0 %collective-permute-start.18 = (f32[64,2048]{1,0:T(8,128)S(1)}, f32[64,2048]{1,0:T(8,128)S(1)}, u32[]{:S(2)}, u32[]{:S(2)}) collective-permute-start(f32[64,2048]{1,0:T(8,128)S(1)} %get-tuple-element.39), channel_id=1, source_target_pairs={{0,4},{4,0},{8,12},{12,8},{16,20},{20,16},{24,28},{28,24},{1,5},{5... | collective-permute-start | bytes 1572872 | tf_op jit(solution)/shard_map/ppermute | solution.py:228
  76.0 2.6 %collective-permute-start.17 = (f32[64,2048]{1,0:T(8,128)S(1)}, f32[64,2048]{1,0:T(8,128)S(1)}, u32[]{:S(2)}, u32[]{:S(2)}) collective-permute-start(f32[64,2048]{1,0:T(8,128)S(1)} %get-tuple-element.40), channel_id=1, source_target_pairs={{0,4},{4,0},{8,12},{12,8},{16,20},{20,16},{24,28},{28,24},{1,5},{5... | collective-permute-start | bytes 1572872 | tf_op jit(solution)/shard_map/ppermute | solution.py:228
  77.7 22.2 %copy-start.1 = (bf16[64,8192]{1,0:T(8,128)(2,1)S(1)}, bf16[64,8192]{1,0:T(8,128)(2,1)}, u32[]{:S(2)}) copy-start(bf16[64,8192]{1,0:T(8,128)(2,1)} %pad_maximum_fusion.1.third) | copy-start | bytes 3145732
  80.0 4.5 %collective-permute-start.19 = (f32[64,256]{1,0:T(8,128)S(1)}, f32[64,256]{1,0:T(8,128)S(1)}, u32[]{:S(2)}, u32[]{:S(2)}) collective-permute-start(f32[64,256]{1,0:T(8,128)S(1)} %shard_map.82), channel_id=1, source_target_pairs={{0,1},{1,0},{2,3},{3,2},{4,5},{5,4},{6,7},{7,6},{8,9},{9,8},{10,11... | collective-permute-start | bytes 196616 | tf_op jit(solution)/shard_map/ppermute | solution.py:228
  84.6 5.3 %collective-permute-start.20 = (f32[64,256]{1,0:T(8,128)S(1)}, f32[64,256]{1,0:T(8,128)S(1)}, u32[]{:S(2)}, u32[]{:S(2)}) collective-permute-start(f32[64,256]{1,0:T(8,128)S(1)} %add.23), channel_id=1, source_target_pairs={{0,2},{1,3},{2,0},{3,1},{4,6},{5,7},{6,4},{7,5},{8,10},{9,11},{10,... | collective-permute-start | bytes 196616 | tf_op jit(solution)/shard_map/ppermute | solution.py:228

commit v5 on v4

--- a/solution.py
+++ b/solution.py
@@ -260,7 +260,10 @@
     origin = me ^ jnp.where(me % 2 == 0, where[:, :, 0], where[:, :, 1])
     table = origin * halves + where[:, :, 2]
 
-    arrays = {block: vectors[:, block[2] * unit : (block[2] + 1) * unit] for block in held[:halves]}
+    arrays, rest = {}, vectors
+    for block in held[:halves]:
+        arrays[block] = rest[:, block[2] * unit : (block[2] + 1) * unit]
+        rest = after(vectors, *arrays.values())
     total = jnp.zeros((amplitudes.shape[0] * amplitudes.shape[1], 2 * bond_dim), jnp.float32)
     add = functools.partial(project, table)
     arrived, fetched = [], {}

time: 105 us -> 104 us (level)
  waiting for transfers between devices: 18.9 us -> 17.5 us
    ppermute x21, waiting for transfers between devices: 18.9 us -> 17.5 us  [swap(): return lax.ppermute(x, axis, [(i, partner(i)) for i in range(size)])]
    slice x1 -> x2, local copies, waits for them, and re-layouts: 3.21 us -> 3.48 us  [gather_and_project(): arrays[block] = rest[:, block[2] * unit:(block[2] + 1) * unit]]
  transfers between devices with their start and end apart: 21 -> 21, of which waited for: 9 -> 9; matrix products, arithmetic and copies ran while one was open for 11% -> 11% of each run, Pallas kernels for 37% -> 38%
where the time goes in v5:
time: 104 us
  Pallas kernels  44.9 us (43%)
  starting transfers between devices  19 us (18%)
  waiting for transfers between devices  17.5 us (17%)
  blocking collectives  10.1 us (10%)
  local copies, waits for them, and re-layouts  7.5 us (7%)
  other arithmetic  4.28 us (4%)
    pallas_call x6, Pallas kernels, project(): pl.pallas_call(functools.partial(project_kernel, places, unit, row, fetch...  35.2 us
    ppermute x21, starting transfers between devices, swap(): return lax.ppermute(x, axis, [(i, partner(i)) for i in range(size)])  19 us
    ppermute x21, waiting for transfers between devices, swap(): return lax.ppermute(x, axis, [(i, partner(i)) for i in range(size)])  17.5 us
    all_gather x1, blocking collectives, local(): slab = lax.all_gather(total, 'bond', axis=0)  10.1 us
    pallas_call x4, Pallas kernels, project_fetched(): pl.pallas_call(functools.partial(project_fetched_kernel, which, step, las...  5.25 us
    pallas_call x1, Pallas kernels, coarsen(): pl.pallas_call(functools.partial(coarsen_kernel, rows_q), in_specs=[pl.Bl...  4.4 us
    slice x2, local copies, waits for them, and re-layouts, gather_and_project(): arrays[block] = rest[:, block[2] * unit:(block[2] + 1) * unit]  3.48 us
  transfers between devices with their start and end apart: 21, of which 9 were waited for; matrix products, arithmetic and copies ran while one was open for 11% of the time, Pallas kernels for 38%

profile of v5, /device:TPU:0, one launch (start us, length us, event | category | flops | bytes accessed | tf_op | source)
XLA Modules:
  0.0 103.6 jit_solution(17124072966856967582)
XLA Ops:
  0.0 0.5 collective-permute-start.3
  0.5 2.4 %slice.42 = f32[64,4096]{1,0:T(8,128)} slice(f32[64,8192]{1,0:T(8,128)} %refs_0_.1), slice={[0:64], [0:4096]} | slice | bytes 2097152 | tf_op jit(solution)/shard_map/slice | solution.py:265
  3.0 2.5 %collective-permute-start = (f32[64,4096]{1,0:T(8,128)}, f32[64,4096]{1,0:T(8,128)S(1)}, u32[]{:S(2)}, u32[]{:S(2)}) collective-permute-start(f32[64,4096]{1,0:T(8,128)} %slice.42), channel_id=1, source_target_pairs={{0,8},{4,20},{8,0},{12,28},{16,24},{20,4},{24,16},{28,12},{1,9},{5... | collective-permute-start | bytes 3145736 | tf_op jit(solution)/shard_map/ppermute | solution.py:228
  5.5 1.1 %slice.43 = f32[64,4096]{1,0:T(8,128)} slice(f32[64,8192]{1,0:T(8,128)S(1)} %copy-done), slice={[0:64], [4096:8192]} | slice | bytes 2097152 | tf_op jit(solution)/shard_map/slice | solution.py:265
  6.6 0.0 copy-start.2
  6.6 5.5 %shard_map.73.refs_1_ = f32[256,128]{1,0:T(8,128)S(1)} custom-call(s32[7,4]{1,0:T(8,128)S(1)} %multiply_add_fusion.table, f32[2,128,65536]{2,1,0:T(8,128)} %amp.11, f32[64,8192]{1,0:T(8,128)S(1)} %copy-done, f32[256,128]{1,0:T(8,128)S(1)} %broadcast_in_dim.8.refs_1_), custom_call_target="tpu_custom_call" | custom-call | flops 1073741824 | bytes 10485760 | tf_op jit(solution)/shard_map/pallas_call | solution.py:92
  12.1 0.1 collective-permute-start.10
  12.1 1.0 reshape.21
  13.2 1.4 %select_maximum_fusion = f32[32,64,128]{2,1,0:T(8,128)S(1)} fusion(f32[16,64,64]{2,1,0:T(8,128)} %reshape.21), kind=kLoop, calls=%fused_computation.6 | loop fusion | flops 1310720 | bytes 1310720 | tf_op jit(solution)/shard_map/concatenate | solution.py:222
  14.6 0.0 copy-start.3
  14.6 0.6 reduce-precision_convert_fusion
  15.2 1.1 %pad_maximum_fusion.1.third = bf16[64,8192]{1,0:T(8,128)(2,1)} fusion(bf16[32,8192]{1,0:T(8,128)(2,1)S(1)} %get-tuple-element.52, bf16[32,8192]{1,0:T(8,128)(2,1)S(1)} %get-tuple-element.51), kind=kLoop, calls=%fused_computation.10 | loop fusion | flops 2097152 | bytes 2097152 | tf_op jit(solution)/shard_map/concatenate | solution.py:224
  16.3 0.1 reshape.18
  16.4 0.2 copy.8
  16.6 0.5 fusion.8
  17.1 0.5 reshape.19
  17.6 1.2 %reshape.20 = f32[64,1024]{1,0:T(8,128)} reshape(f32[64,8,2,64]{3,2,1,0:T(2,128)S(1)} %get-tuple-element.56) | data formatting | bytes 524288 | tf_op jit(solution)/shard_map/reshape | solution.py:217
  18.8 1.1 %fusion = (bf16[256,1024]{1,0:T(8,128)(2,1)S(1)}, bf16[256,1024]{1,0:T(8,128)(2,1)S(1)}) fusion(f32[64,1024]{1,0:T(8,128)S(1)} %broadcast_in_dim.7, f32[64,1024]{1,0:T(8,128)} %reshape.20, f32[64,1024]{1,0:T(8,128)S(1)} %reshape.19), kind=kLoop, calls=%fused_computation.4 | loop fusion | flops 1835008 | bytes 1835008 | tf_op jit(solution)/shard_map/convert_element_type | solution.py:209
  19.9 0.1 fusion.7
  20.0 0.2 collective-permute-start.2
  20.2 0.4 collective-permute-start.1
  20.6 0.0 collective-permute-done.3.refs_0_
  20.6 5.6 %shard_map.74.refs_3_ = f32[256,128]{1,0:T(8,128)S(1)} custom-call(s32[7,4]{1,0:T(8,128)S(1)} %multiply_add_fusion.table, f32[2,128,65536]{2,1,0:T(8,128)} %amp.11, f32[64,8192]{1,0:T(8,128)} %collective-permute-done.3.refs_0_, f32[256,128]{1,0:T(8,128)S(1)} %shard_map.73.refs_1_), custom_call_target="tpu_custom_call" | custom-call | flops 1073741824 | bytes 10485760 | tf_op jit(solution)/shard_map/pallas_call | solution.py:92
  26.2 2.1 %collective-permute-start.7 = (f32[64,4096]{1,0:T(8,128)}, f32[64,4096]{1,0:T(8,128)S(1)}, u32[]{:S(2)}, u32[]{:S(2)}) collective-permute-start(f32[64,4096]{1,0:T(8,128)} %slice.42), channel_id=1, source_target_pairs={{0,16},{4,12},{8,24},{12,4},{16,0},{20,28},{24,8},{28,20},{1,17},{... | collective-permute-start | bytes 3145736 | tf_op jit(solution)/shard_map/ppermute | solution.py:228
  28.3 1.6 %collective-permute-done.10.refs_0_ = f32[64,4096]{1,0:T(8,128)S(1)} collective-permute-done((f32[64,4096]{1,0:T(8,128)}, f32[64,4096]{1,0:T(8,128)S(1)}, u32[]{:S(2)}, u32[]{:S(2)}) %collective-permute-start.10) | collective-permute-done | bytes 1048608 | tf_op jit(solution)/shard_map/ppermute | solution.py:228
  29.9 0.1 fusion.4
  30.0 0.1 collective-permute-start.12
  30.0 0.5 collective-permute-start.11
  30.5 0.0 collective-permute-done.2.refs_2_
  30.6 5.5 %shard_map.75.refs_3_ = f32[256,128]{1,0:T(8,128)S(1)} custom-call(s32[7,4]{1,0:T(8,128)S(1)} %multiply_add_fusion.table, f32[2,128,65536]{2,1,0:T(8,128)} %amp.11, f32[64,4096]{1,0:T(8,128)S(1)} %collective-permute-done.refs_0_, f32[64,2048]{1,0:T(8,128)S(1)} %collective-permute-done.1.refs_1_, f32[64,2048]{1,0:T(8,128)S(1)} %collective-permute-done.2.refs_2_, ...), custom_call_target="tpu_custom_call" | custom-call | flops 1073741824 | bytes 10485760 | tf_op jit(solution)/shard_map/pallas_call | solution.py:92
  36.0 2.4 %collective-permute-start.4 = (f32[64,4096]{1,0:T(8,128)}, f32[64,4096]{1,0:T(8,128)S(1)}, u32[]{:S(2)}, u32[]{:S(2)}) collective-permute-start(f32[64,4096]{1,0:T(8,128)} %slice.43), channel_id=1, source_target_pairs={{0,16},{4,12},{8,24},{12,4},{16,0},{20,28},{24,8},{28,20},{1,17},{... | collective-permute-start | bytes 3145736 | tf_op jit(solution)/shard_map/ppermute | solution.py:228
  38.5 5.5 %shard_map.76.refs_3_ = f32[256,128]{1,0:T(8,128)S(1)} custom-call(s32[7,4]{1,0:T(8,128)S(1)} %multiply_add_fusion.table, f32[2,128,65536]{2,1,0:T(8,128)} %amp.11, f32[64,4096]{1,0:T(8,128)S(1)} %collective-permute-done.10.refs_0_, f32[64,2048]{1,0:T(8,128)S(1)} %collective-permute-done.11.refs_1_, f32[64,2048]{1,0:T(8,128)S(1)} %collective-permute-done.12.refs_2_, ...), custom_call_target="tpu_custom_call" | custom-call | flops 1073741824 | bytes 10485760 | tf_op jit(solution)/shard_map/pallas_call | solution.py:92
  43.9 0.1 fusion.5
  44.0 0.1 collective-permute-start.9
  44.1 0.5 collective-permute-start.8
  44.6 0.8 collective-permute-start.14
  45.5 7.1 %collective-permute-done.4.refs_0_ = f32[64,4096]{1,0:T(8,128)S(1)} collective-permute-done((f32[64,4096]{1,0:T(8,128)}, f32[64,4096]{1,0:T(8,128)S(1)}, u32[]{:S(2)}, u32[]{:S(2)}) %collective-permute-start.4) | collective-permute-done | bytes 1048608 | tf_op jit(solution)/shard_map/ppermute | solution.py:228
  52.5 0.1 fusion.6
  52.6 0.1 collective-permute-start.6
  52.7 0.5 collective-permute-start.5
  53.2 6.6 %shard_map.77 = (f32[256,128]{1,0:T(8,128)S(1)}, f32[2,2,128,4096]{3,2,1,0:T(8,128)S(1)}) custom-call(s32[7,4]{1,0:T(8,128)S(1)} %multiply_add_fusion.table, f32[2,128,65536]{2,1,0:T(8,128)} %amp.11, f32[64,4096]{1,0:T(8,128)S(1)} %collective-permute-done.7.refs_0_, f32[64,2048]{1,0:T(8,128)S(1)} %collective-permute-done.8.refs_1_, ...), custom_call_target="tpu_custom_call" | custom-call | flops 1073741824 | bytes 10485760 | tf_op jit(solution)/shard_map/pallas_call | solution.py:92
  59.8 2.1 %collective-permute-start.13 = (f32[64,4096]{1,0:T(8,128)S(1)}, f32[64,4096]{1,0:T(8,128)S(1)}, u32[]{:S(2)}, u32[]{:S(2)}) collective-permute-start(f32[64,4096]{1,0:T(8,128)S(1)} %collective-permute-done.10.refs_0_), channel_id=1, source_target_pairs={{0,16},{4,12},{8,24},{12,4},{16,0},{20,28},{24,8},{28,20},{1,17},{... | collective-permute-start | bytes 3145736 | tf_op jit(solution)/shard_map/ppermute | solution.py:228
  61.9 6.6 %shard_map.78 = (f32[256,128]{1,0:T(8,128)S(1)}, f32[2,2,128,4096]{3,2,1,0:T(8,128)S(1)}) custom-call(s32[7,4]{1,0:T(8,128)S(1)} %multiply_add_fusion.table, f32[2,128,65536]{2,1,0:T(8,128)} %amp.11, f32[64,4096]{1,0:T(8,128)S(1)} %collective-permute-done.4.refs_0_, f32[64,2048]{1,0:T(8,128)S(1)} %collective-permute-done.5.refs_1_, ...), custom_call_target="tpu_custom_call" | custom-call | flops 1073741824 | bytes 10485760 | tf_op jit(solution)/shard_map/pallas_call | solution.py:92
  68.5 0.1 fusion.3
  68.6 0.1 collective-permute-start.16
  68.7 0.5 collective-permute-start.15
  69.2 1.3 %shard_map.79.refs_2_ = f32[256,128]{1,0:T(8,128)S(1)} custom-call(f32[2,2,128,4096]{3,2,1,0:T(8,128)S(1)} %get-tuple-element.33.fetched, f32[64,4096]{1,0:T(8,128)S(1)} %collective-permute-done.14.refs_0_, f32[256,128]{1,0:T(8,128)S(1)} %get-tuple-element.36.refs_1_), custom_call_target="tpu_custom_call" | custom-call | flops 536870912 | bytes 5242880 | tf_op jit(solution)/shard_map/pallas_call | solution.py:142
  70.5 0.1 collective-permute-done.16.refs_1_
  70.6 0.7 collective-permute-done.15.refs_0_
  71.3 1.3 %shard_map.80.refs_1_ = f32[256,128]{1,0:T(8,128)S(1)} custom-call(f32[2,2,128,4096]{3,2,1,0:T(8,128)S(1)} %get-tuple-element.33.fetched, f32[64,2048]{1,0:T(8,128)S(1)} %collective-permute-done.15.refs_0_, f32[64,2048]{1,0:T(8,128)S(1)} %collective-permute-done.16.refs_1_, f32[256,128]{1,0:T(8,128)S(1)} %shard_map.79.refs_2_), custom_call_target="tpu_custom_call" | custom-call | flops 536870912 | bytes 5242880 | tf_op jit(solution)/shard_map/pallas_call | solution.py:142
  72.6 2.4 %collective-permute-done.13.refs_0_ = f32[64,4096]{1,0:T(8,128)S(1)} collective-permute-done((f32[64,4096]{1,0:T(8,128)S(1)}, f32[64,4096]{1,0:T(8,128)S(1)}, u32[]{:S(2)}, u32[]{:S(2)}) %collective-permute-start.13) | collective-permute-done | bytes 1048608 | tf_op jit(solution)/shard_map/ppermute | solution.py:228
  75.0 0.1 fusion.2
  75.1 0.1 collective-permute-start.18
  75.2 0.5 collective-permute-start.17
  75.7 1.3 %shard_map.81.refs_2_ = f32[256,128]{1,0:T(8,128)S(1)} custom-call(f32[2,2,128,4096]{3,2,1,0:T(8,128)S(1)} %get-tuple-element.30.fetched, f32[64,4096]{1,0:T(8,128)S(1)} %collective-permute-done.13.refs_0_, f32[256,128]{1,0:T(8,128)S(1)} %shard_map.80.refs_1_), custom_call_target="tpu_custom_call" | custom-call | flops 536870912 | bytes 5242880 | tf_op jit(solution)/shard_map/pallas_call | solution.py:142
  77.0 0.1 collective-permute-done.18.refs_1_
  77.1 0.7 collective-permute-done.17.refs_0_
  77.8 1.4 %shard_map.82 = f32[64,256]{1,0:T(8,128)S(1)} custom-call(f32[2,2,128,4096]{3,2,1,0:T(8,128)S(1)} %get-tuple-element.30.fetched, f32[64,2048]{1,0:T(8,128)S(1)} %collective-permute-done.17.refs_0_, f32[64,2048]{1,0:T(8,128)S(1)} %collective-permute-done.18.refs_1_, f32[256,128]{1,0:T(8,128)S(1)} %shard_map.81.refs_2_), custom_call_target="tpu_custom_call" | custom-call | flops 536870912 | bytes 5242880 | tf_op jit(solution)/shard_map/pallas_call | solution.py:142
  79.2 2.1 %collective-permute-start.19 = (f32[64,256]{1,0:T(8,128)S(1)}, f32[64,256]{1,0:T(8,128)S(1)}, u32[]{:S(2)}, u32[]{:S(2)}) collective-permute-start(f32[64,256]{1,0:T(8,128)S(1)} %shard_map.82), channel_id=1, source_target_pairs={{0,1},{1,0},{2,3},{3,2},{4,5},{5,4},{6,7},{7,6},{8,9},{9,8},{10,11... | collective-permute-start | bytes 196616 | tf_op jit(solution)/shard_map/ppermute | solution.py:228
  81.3 2.4 %collective-permute-done.19 = f32[64,256]{1,0:T(8,128)S(1)} collective-permute-done((f32[64,256]{1,0:T(8,128)S(1)}, f32[64,256]{1,0:T(8,128)S(1)}, u32[]{:S(2)}, u32[]{:S(2)}) %collective-permute-start.19) | collective-permute-done | bytes 65568 | tf_op jit(solution)/shard_map/ppermute | solution.py:228
  83.8 2.9 %collective-permute-start.20 = (f32[64,256]{1,0:T(8,128)S(1)}, f32[64,256]{1,0:T(8,128)S(1)}, u32[]{:S(2)}, u32[]{:S(2)}) collective-permute-start(f32[64,256]{1,0:T(8,128)S(1)} %add.23), channel_id=1, source_target_pairs={{0,2},{1,3},{2,0},{3,1},{4,6},{5,7},{6,4},{7,5},{8,10},{9,11},{10,... | collective-permute-start | bytes 196616 | tf_op jit(solution)/shard_map/ppermute | solution.py:228
  86.7 2.4 %collective-permute-done.20 = f32[64,256]{1,0:T(8,128)S(1)} collective-permute-done((f32[64,256]{1,0:T(8,128)S(1)}, f32[64,256]{1,0:T(8,128)S(1)}, u32[]{:S(2)}, u32[]{:S(2)}) %collective-permute-start.20) | collective-permute-done | bytes 65568 | tf_op jit(solution)/shard_map/ppermute | solution.py:228
  89.1 10.1 %all-gather = f32[512,256]{1,0:T(8,128)S(1)} all-gather(f32[64,256]{1,0:T(8,128)S(1)} %add.24), channel_id=2, replica_groups=mesh['bond'=8,'leg'=4] {'bond'}, dimensions={0}, use_global_device_ids=true | all-gather | bytes 589824 | tf_op jit(solution)/shard_map/all_gather | solution.py:323
  99.2 4.4 %shard_map.83 = f32[2,64,16]{2,1,0:T(8,128)} custom-call(f32[8,64,256]{2,1,0:T(8,128)S(1)} %bitcast.11, bf16[256,1024]{1,0:T(8,128)(2,1)S(1)} %get-tuple-element.54.first_hi, bf16[256,1024]{1,0:T(8,128)(2,1)S(1)} %get-tuple-element.53.first_lo, bf16[64,8192]{1,0:T(8,128)(2,1)S(1)} %copy-done.1), custom_call_target="tpu_custom_call" | custom-call | tf_op jit(solution)/shard_map/pallas_call | solution.py:196
  (27 shorter events, 0.1 us)
Async XLA Ops:
  0.0 6.5 %copy-start.4 = (s32[7,4]{1,0:T(8,128)S(1)}, s32[7,4]{1,0:T(8,128)}, u32[]{:S(2)}) copy-start(s32[7,4]{1,0:T(8,128)} %constant.34.clone) | copy-start | bytes 340
  0.0 6.5 %copy-start.5 = (s32[7,4]{1,0:T(8,128)S(1)}, s32[7,4]{1,0:T(8,128)}, u32[]{:S(2)}) copy-start(s32[7,4]{1,0:T(8,128)} %constant.33.clone) | copy-start | bytes 340
  0.0 6.5 %copy-start.6 = (s32[7,4]{1,0:T(8,128)S(1)}, s32[7,4]{1,0:T(8,128)}, u32[]{:S(2)}) copy-start(s32[7,4]{1,0:T(8,128)} %constant.32.clone) | copy-start | bytes 340
  0.0 5.5 %copy-start = (f32[64,8192]{1,0:T(8,128)S(1)}, f32[64,8192]{1,0:T(8,128)}, u32[]{:S(2)}) copy-start(f32[64,8192]{1,0:T(8,128)} %refs_0_.1) | copy-start | bytes 6291460
  0.0 20.6 %collective-permute-start.3 = (f32[64,8192]{1,0:T(8,128)}, f32[64,8192]{1,0:T(8,128)}, u32[]{:S(2)}, u32[]{:S(2)}) collective-permute-start(f32[64,8192]{1,0:T(8,128)} %refs_0_.1), channel_id=1, source_target_pairs={{0,4},{4,0},{8,12},{12,8},{16,20},{20,16},{24,28},{28,24},{1,5},{5... | collective-permute-start | bytes 6291464 | tf_op jit(solution)/shard_map/ppermute | solution.py:228
  3.0 16.9 %collective-permute-start = (f32[64,4096]{1,0:T(8,128)}, f32[64,4096]{1,0:T(8,128)S(1)}, u32[]{:S(2)}, u32[]{:S(2)}) collective-permute-start(f32[64,4096]{1,0:T(8,128)} %slice.42), channel_id=1, source_target_pairs={{0,8},{4,20},{8,0},{12,28},{16,24},{20,4},{24,16},{28,12},{1,9},{5... | collective-permute-start | bytes 3145736 | tf_op jit(solution)/shard_map/ppermute | solution.py:228
  6.6 5.6 %copy-start.2 = (f32[16,4096]{1,0:T(8,128)S(1)}, f32[16,4096]{1,0:T(8,128)}, u32[]{:S(2)}) copy-start(f32[16,4096]{1,0:T(8,128)} %param.9) | copy-start | bytes 786436
  12.1 17.8 %collective-permute-start.10 = (f32[64,4096]{1,0:T(8,128)}, f32[64,4096]{1,0:T(8,128)S(1)}, u32[]{:S(2)}, u32[]{:S(2)}) collective-permute-start(f32[64,4096]{1,0:T(8,128)} %slice.43), channel_id=1, source_target_pairs={{0,8},{4,20},{8,0},{12,28},{16,24},{20,4},{24,16},{28,12},{1,9},{5... | collective-permute-start | bytes 3145736 | tf_op jit(solution)/shard_map/ppermute | solution.py:228
  14.6 1.7 %copy-start.3 = (f32[8,4096]{1,0:T(8,128)S(1)}, f32[8,4096]{1,0:T(8,128)}, u32[]{:S(2)}) copy-start(f32[8,4096]{1,0:T(8,128)} %param.10) | copy-start | bytes 393220
  20.0 10.6 %collective-permute-start.2 = (f32[64,2048]{1,0:T(8,128)S(1)}, f32[64,2048]{1,0:T(8,128)S(1)}, u32[]{:S(2)}, u32[]{:S(2)}) collective-permute-start(f32[64,2048]{1,0:T(8,128)S(1)} %get-tuple-element.49), channel_id=1, source_target_pairs={{0,4},{4,0},{8,12},{12,8},{16,20},{20,16},{24,28},{28,24},{1,5},{5... | collective-permute-start | bytes 1572872 | tf_op jit(solution)/shard_map/ppermute | solution.py:228
  20.2 10.4 %collective-permute-start.1 = (f32[64,2048]{1,0:T(8,128)S(1)}, f32[64,2048]{1,0:T(8,128)S(1)}, u32[]{:S(2)}, u32[]{:S(2)}) collective-permute-start(f32[64,2048]{1,0:T(8,128)S(1)} %get-tuple-element.50), channel_id=1, source_target_pairs={{0,4},{4,0},{8,12},{12,8},{16,20},{20,16},{24,28},{28,24},{1,5},{5... | collective-permute-start | bytes 1572872 | tf_op jit(solution)/shard_map/ppermute | solution.py:228
  26.2 17.7 %collective-permute-start.7 = (f32[64,4096]{1,0:T(8,128)}, f32[64,4096]{1,0:T(8,128)S(1)}, u32[]{:S(2)}, u32[]{:S(2)}) collective-permute-start(f32[64,4096]{1,0:T(8,128)} %slice.42), channel_id=1, source_target_pairs={{0,16},{4,12},{8,24},{12,4},{16,0},{20,28},{24,8},{28,20},{1,17},{... | collective-permute-start | bytes 3145736 | tf_op jit(solution)/shard_map/ppermute | solution.py:228
  30.0 8.5 %collective-permute-start.12 = (f32[64,2048]{1,0:T(8,128)S(1)}, f32[64,2048]{1,0:T(8,128)S(1)}, u32[]{:S(2)}, u32[]{:S(2)}) collective-permute-start(f32[64,2048]{1,0:T(8,128)S(1)} %get-tuple-element.43), channel_id=1, source_target_pairs={{0,4},{4,0},{8,12},{12,8},{16,20},{20,16},{24,28},{28,24},{1,5},{5... | collective-permute-start | bytes 1572872 | tf_op jit(solution)/shard_map/ppermute | solution.py:228
  30.0 8.4 %collective-permute-start.11 = (f32[64,2048]{1,0:T(8,128)S(1)}, f32[64,2048]{1,0:T(8,128)S(1)}, u32[]{:S(2)}, u32[]{:S(2)}) collective-permute-start(f32[64,2048]{1,0:T(8,128)S(1)} %get-tuple-element.44), channel_id=1, source_target_pairs={{0,4},{4,0},{8,12},{12,8},{16,20},{20,16},{24,28},{28,24},{1,5},{5... | collective-permute-start | bytes 1572872 | tf_op jit(solution)/shard_map/ppermute | solution.py:228
  36.0 16.5 %collective-permute-start.4 = (f32[64,4096]{1,0:T(8,128)}, f32[64,4096]{1,0:T(8,128)S(1)}, u32[]{:S(2)}, u32[]{:S(2)}) collective-permute-start(f32[64,4096]{1,0:T(8,128)} %slice.43), channel_id=1, source_target_pairs={{0,16},{4,12},{8,24},{12,4},{16,0},{20,28},{24,8},{28,20},{1,17},{... | collective-permute-start | bytes 3145736 | tf_op jit(solution)/shard_map/ppermute | solution.py:228
  44.0 9.2 %collective-permute-start.9 = (f32[64,2048]{1,0:T(8,128)S(1)}, f32[64,2048]{1,0:T(8,128)S(1)}, u32[]{:S(2)}, u32[]{:S(2)}) collective-permute-start(f32[64,2048]{1,0:T(8,128)S(1)} %get-tuple-element.45), channel_id=1, source_target_pairs={{0,4},{4,0},{8,12},{12,8},{16,20},{20,16},{24,28},{28,24},{1,5},{5... | collective-permute-start | bytes 1572872 | tf_op jit(solution)/shard_map/ppermute | solution.py:228
  44.1 9.1 %collective-permute-start.8 = (f32[64,2048]{1,0:T(8,128)S(1)}, f32[64,2048]{1,0:T(8,128)S(1)}, u32[]{:S(2)}, u32[]{:S(2)}) collective-permute-start(f32[64,2048]{1,0:T(8,128)S(1)} %get-tuple-element.46), channel_id=1, source_target_pairs={{0,4},{4,0},{8,12},{12,8},{16,20},{20,16},{24,28},{28,24},{1,5},{5... | collective-permute-start | bytes 1572872 | tf_op jit(solution)/shard_map/ppermute | solution.py:228
  44.6 23.9 %collective-permute-start.14 = (f32[64,4096]{1,0:T(8,128)S(1)}, f32[64,4096]{1,0:T(8,128)S(1)}, u32[]{:S(2)}, u32[]{:S(2)}) collective-permute-start(f32[64,4096]{1,0:T(8,128)S(1)} %collective-permute-done.refs_0_), channel_id=1, source_target_pairs={{0,16},{4,12},{8,24},{12,4},{16,0},{20,28},{24,8},{28,20},{1,17},{... | collective-permute-start | bytes 3145736 | tf_op jit(solution)/shard_map/ppermute | solution.py:228
  52.6 9.3 %collective-permute-start.6 = (f32[64,2048]{1,0:T(8,128)S(1)}, f32[64,2048]{1,0:T(8,128)S(1)}, u32[]{:S(2)}, u32[]{:S(2)}) collective-permute-start(f32[64,2048]{1,0:T(8,128)S(1)} %get-tuple-element.47), channel_id=1, source_target_pairs={{0,4},{4,0},{8,12},{12,8},{16,20},{20,16},{24,28},{28,24},{1,5},{5... | collective-permute-start | bytes 1572872 | tf_op jit(solution)/shard_map/ppermute | solution.py:228
  52.7 9.2 %collective-permute-start.5 = (f32[64,2048]{1,0:T(8,128)S(1)}, f32[64,2048]{1,0:T(8,128)S(1)}, u32[]{:S(2)}, u32[]{:S(2)}) collective-permute-start(f32[64,2048]{1,0:T(8,128)S(1)} %get-tuple-element.48), channel_id=1, source_target_pairs={{0,4},{4,0},{8,12},{12,8},{16,20},{20,16},{24,28},{28,24},{1,5},{5... | collective-permute-start | bytes 1572872 | tf_op jit(solution)/shard_map/ppermute | solution.py:228
  59.8 15.2 %collective-permute-start.13 = (f32[64,4096]{1,0:T(8,128)S(1)}, f32[64,4096]{1,0:T(8,128)S(1)}, u32[]{:S(2)}, u32[]{:S(2)}) collective-permute-start(f32[64,4096]{1,0:T(8,128)S(1)} %collective-permute-done.10.refs_0_), channel_id=1, source_target_pairs={{0,16},{4,12},{8,24},{12,4},{16,0},{20,28},{24,8},{28,20},{1,17},{... | collective-permute-start | bytes 3145736 | tf_op jit(solution)/shard_map/ppermute | solution.py:228
  68.6 2.0 %collective-permute-start.16 = (f32[64,2048]{1,0:T(8,128)S(1)}, f32[64,2048]{1,0:T(8,128)S(1)}, u32[]{:S(2)}, u32[]{:S(2)}) collective-permute-start(f32[64,2048]{1,0:T(8,128)S(1)} %get-tuple-element.41), channel_id=1, source_target_pairs={{0,4},{4,0},{8,12},{12,8},{16,20},{20,16},{24,28},{28,24},{1,5},{5... | collective-permute-start | bytes 1572872 | tf_op jit(solution)/shard_map/ppermute | solution.py:228
  68.7 2.6 %collective-permute-start.15 = (f32[64,2048]{1,0:T(8,128)S(1)}, f32[64,2048]{1,0:T(8,128)S(1)}, u32[]{:S(2)}, u32[]{:S(2)}) collective-permute-start(f32[64,2048]{1,0:T(8,128)S(1)} %get-tuple-element.42), channel_id=1, source_target_pairs={{0,4},{4,0},{8,12},{12,8},{16,20},{20,16},{24,28},{28,24},{1,5},{5... | collective-permute-start | bytes 1572872 | tf_op jit(solution)/shard_map/ppermute | solution.py:228
  75.1 2.0 %collective-permute-start.18 = (f32[64,2048]{1,0:T(8,128)S(1)}, f32[64,2048]{1,0:T(8,128)S(1)}, u32[]{:S(2)}, u32[]{:S(2)}) collective-permute-start(f32[64,2048]{1,0:T(8,128)S(1)} %get-tuple-element.39), channel_id=1, source_target_pairs={{0,4},{4,0},{8,12},{12,8},{16,20},{20,16},{24,28},{28,24},{1,5},{5... | collective-permute-start | bytes 1572872 | tf_op jit(solution)/shard_map/ppermute | solution.py:228
  75.2 2.6 %collective-permute-start.17 = (f32[64,2048]{1,0:T(8,128)S(1)}, f32[64,2048]{1,0:T(8,128)S(1)}, u32[]{:S(2)}, u32[]{:S(2)}) collective-permute-start(f32[64,2048]{1,0:T(8,128)S(1)} %get-tuple-element.40), channel_id=1, source_target_pairs={{0,4},{4,0},{8,12},{12,8},{16,20},{20,16},{24,28},{28,24},{1,5},{5... | collective-permute-start | bytes 1572872 | tf_op jit(solution)/shard_map/ppermute | solution.py:228
  77.0 22.2 %copy-start.1 = (bf16[64,8192]{1,0:T(8,128)(2,1)S(1)}, bf16[64,8192]{1,0:T(8,128)(2,1)}, u32[]{:S(2)}) copy-start(bf16[64,8192]{1,0:T(8,128)(2,1)} %pad_maximum_fusion.1.third) | copy-start | bytes 3145732
  79.2 4.5 %collective-permute-start.19 = (f32[64,256]{1,0:T(8,128)S(1)}, f32[64,256]{1,0:T(8,128)S(1)}, u32[]{:S(2)}, u32[]{:S(2)}) collective-permute-start(f32[64,256]{1,0:T(8,128)S(1)} %shard_map.82), channel_id=1, source_target_pairs={{0,1},{1,0},{2,3},{3,2},{4,5},{5,4},{6,7},{7,6},{8,9},{9,8},{10,11... | collective-permute-start | bytes 196616 | tf_op jit(solution)/shard_map/ppermute | solution.py:228
  83.8 5.3 %collective-permute-start.20 = (f32[64,256]{1,0:T(8,128)S(1)}, f32[64,256]{1,0:T(8,128)S(1)}, u32[]{:S(2)}, u32[]{:S(2)}) collective-permute-start(f32[64,256]{1,0:T(8,128)S(1)} %add.23), channel_id=1, source_target_pairs={{0,2},{1,3},{2,0},{3,1},{4,6},{5,7},{6,4},{7,5},{8,10},{9,11},{10,... | collective-permute-start | bytes 196616 | tf_op jit(solution)/shard_map/ppermute | solution.py:228
